TPU v7x, 32 devices: a whole 2x2x4 slice. The times are simulated.
32 devices in a mesh: pipe: 4 (over y, x), dp: 8 (over z, core).
Axes of the slice: x: 2, y: 2, z: 4, core: 2. Of those that a mesh axis runs over, the one named last changes fastest.
Arguments:
- activations: bfloat16 [2, 4, 1024, 6144], P(None, 'pipe', 'dp'), may hold values from -6 to 6
- queries: bfloat16 [2, 4, 1024, 128], P(None, 'pipe', 'dp'), may hold values from -16 to 16
- keys: bfloat16 [2, 4, 1024, 128], P(None, 'pipe', 'dp'), may hold values from -16 to 16
- grad_out: bfloat16 [2, 4, 1024, 128], P(None, 'pipe', 'dp'), may hold values from -0.4375 to 0.4375
- segment_ids: int32 [2, 4, 8, 128], P(None, 'pipe', 'dp'), may hold values from 0 to 3, never falling along the last dimension, each value on 1 to 64 neighbouring positions
Outputs:
- grad_value: bfloat16 [4, 6144, 128], P('pipe', 'dp')
Inputs may be any that keep to these rules, and one draw needn't show every extreme that they name: `segment_ids`: ids restart at 0 in every micro-batch; each document spans 1 to 64 tokens, one exactly that many.
All inputs are finite; a program needn't handle non-finite values.
Results may differ from a plain program's by a relative error of at most 0.0063.
Values sent between devices are 32-bit elements; how exact they have to be, the bound alone decides.
No kernel may reach another device: no remote copies, remote signals or barrier semaphores. Data moves between devices by JAX's collectives and lax.ppermute only.
A program may use at most 64 MiB of HBM per device.

v0:
```python
import jax
import jax.numpy as jnp
from jax import lax
from jax.sharding import PartitionSpec as P


def partner(block, axis, distance):
    count = lax.axis_size(axis)
    route = []
    for low in range(count):
        high = low | 1 << distance
        if high != low and high < count:
            route += [(low, high), (high, low)]
    return lax.ppermute(block, axis, route)


def section_partial(acts, query_rows, key_rows, grad_rows, segs):
    length = query_rows.shape[0]
    scores = jnp.dot(query_rows, key_rows.T, preferred_element_type=jnp.float32) / jnp.sqrt(
        jnp.float32(query_rows.shape[1])
    )
    position = jnp.arange(length, dtype=jnp.int32)
    keep = (position[None, :] <= position[:, None]) & (segs[None, :] == segs[:, None])
    masked = jnp.where(keep, scores, jnp.float32(-1e30))
    top = jnp.max(masked, axis=1, keepdims=True)
    weights = jnp.where(keep, jnp.exp(masked - top), jnp.float32(0.0))
    probs = (weights / jnp.sum(weights, axis=1, keepdims=True)).astype(jnp.bfloat16)
    grad_v = jnp.einsum("qk,qd->kd", probs, grad_rows, preferred_element_type=jnp.float32).astype(
        jnp.bfloat16
    )
    return jnp.einsum("td,te->de", acts, grad_v, preferred_element_type=jnp.float32).astype(
        jnp.bfloat16
    )


def body(activations, queries, keys, grad_out, segment_ids):
    partials = []
    for half in range(2):
        partials.append(
            section_partial(
                activations[half, 0],
                queries[half, 0],
                keys[half, 0],
                grad_out[half, 0],
                segment_ids[half, 0, 0],
            )
        )
    lower_part, upper_part = partials
    levels = lax.axis_size("pipe").bit_length() - 1
    stacked = jnp.stack([lower_part.astype(jnp.float32), upper_part.astype(jnp.float32)])
    reduced = lax.psum_scatter(stacked, "dp", scatter_dimension=1, tiled=True)
    lower_sum = reduced[0]
    upper_sum = reduced[1]
    moved = upper_sum
    for level in range(levels):
        moved = partner(moved, "pipe", level)
    total = lower_sum + moved
    return total.astype(jnp.bfloat16)[None]


def solution(mesh):
    return jax.shard_map(
        body,
        mesh=mesh,
        in_specs=(
            P(None, "pipe", "dp", None),
            P(None, "pipe", "dp", None),
            P(None, "pipe", "dp", None),
            P(None, "pipe", "dp", None),
            P(None, "pipe", "dp", None),
        ),
        out_specs=P("pipe", "dp", None),
        check_vma=False,
    )
```

profile of v0, /device:TPU:12, one launch (start us, length us, event | category | flops | bytes accessed | tf_op | source)
XLA Modules:
  0.0 117.9 jit_solution(8392823469370529336)
XLA Ops:
  6.5 0.0 copy-start
  6.5 0.0 reduce-scatter.2.cloned.1.call-start
  6.5 0.7 slice_bitcast_fusion.3
  7.2 1.0 fusion.56
  8.2 1.0 fusion.55
  9.2 0.1 fusion.13
  9.3 2.2 %fusion = bf16[1,6144,128]{1,2,0:T(8,128)(2,1)S(1)} fusion(bf16[2,1,128,6144]{3,2,1,0:T(8,128)(2,1)} %param.5, f32[128,128]{0,1:T(8,128)S(1)} %get-tuple-element.10, bf16[2,1,128,128]{3,2,1,0:T(8,128)(2,1)} %param.8, f32[128]{0:T(128)S(1)} %get-tuple-element.11, f32[128]{0:T(128)S(1)} %get-tuple-element.9, s32[128]{0:T(128)S(1)} %get-tuple-element.5), kind=kOutput, calls=%fused_computation.2 | convolution fusion | flops 206438400 | bytes 3246080 | tf_op jit(solution)/shard_map/td,te->de/dot_general | solution.py:31
  11.5 0.0 copy-done
  11.5 2.2 %fusion.1 = bf16[1,6144,128]{1,2,0:T(8,128)(2,1)S(1)} fusion(bf16[2,1,128,6144]{3,2,1,0:T(8,128)(2,1)} %param.5, f32[128,128]{0,1:T(8,128)S(1)} %get-tuple-element.8, bf16[2,1,128,128]{3,2,1,0:T(8,128)(2,1)S(1)} %copy-done, f32[128]{0:T(128)S(1)} %get-tuple-element.12, f32[128]{0:T(128)S(1)} %get-tuple-element.7, s32[128]{0:T(128)S(1)} %get-tuple-element.6), kind=kOutput, calls=%fused_computation.3 | convolution fusion | flops 206438400 | bytes 3246080 | tf_op jit(solution)/shard_map/td,te->de/dot_general | solution.py:31
  13.7 3.1 %maximum_convert_fusion = f32[2,6144,128]{1,2,0:T(8,128)} fusion(bf16[1,6144,128]{1,2,0:T(8,128)(2,1)S(1)} %fusion.1, bf16[1,6144,128]{1,2,0:T(8,128)(2,1)S(1)} %fusion), kind=kLoop, calls=%fused_computation.4 | loop fusion | flops 3145728 | bytes 9437184 | tf_op jit(solution)/shard_map/stack | solution.py:50
  16.8 0.0 reduce-scatter.2.cloned.1.call-update
  16.8 68.3 %reduce-scatter.2.cloned.1.call-done = f32[2,768,128]{1,2,0:T(8,128)} async-done(((f32[2,6144,128]{1,2,0:T(8,128)}), f32[2,768,128]{1,2,0:T(8,128)}) %reduce-scatter.2.cloned.1.call-update) | async-done | bytes 786448 | tf_op jit(solution)/shard_map/reduce_scatter | solution.py:51
  85.1 1.0 slice_bitcast_fusion
  86.1 1.5 %collective-permute-start = (f32[768,128]{0,1:T(8,128)S(1)}, f32[768,128]{0,1:T(8,128)S(1)}, u32[]{:S(2)}, u32[]{:S(2)}) collective-permute-start(f32[768,128]{0,1:T(8,128)S(1)} %slice_bitcast_fusion), channel_id=1, source_target_pairs={{0,8},{8,0},{16,24},{24,16},{1,9},{9,1},{17,25},{25,17},{2,10},{10... | collective-permute-start | bytes 1179656 | tf_op jit(solution)/shard_map/ppermute | solution.py:14
  87.7 10.4 %collective-permute-done = f32[768,128]{0,1:T(8,128)S(1)} collective-permute-done((f32[768,128]{0,1:T(8,128)S(1)}, f32[768,128]{0,1:T(8,128)S(1)}, u32[]{:S(2)}, u32[]{:S(2)}) %collective-permute-start) | collective-permute-done | bytes 393248 | tf_op jit(solution)/shard_map/ppermute | solution.py:14
  98.1 0.4 collective-permute-start.1
  98.4 10.8 %collective-permute-done.1 = f32[768,128]{0,1:T(8,128)S(1)} collective-permute-done((f32[768,128]{0,1:T(8,128)S(1)}, f32[768,128]{0,1:T(8,128)S(1)}, u32[]{:S(2)}, u32[]{:S(2)}) %collective-permute-start.1) | collective-permute-done | bytes 393248 | tf_op jit(solution)/shard_map/ppermute | solution.py:14
  109.2 1.1 fusion.10
  110.3 0.8 copy.6
Async XLA Ops:
  6.5 5.0 %copy-start = (bf16[2,1,128,128]{3,2,1,0:T(8,128)(2,1)S(1)}, bf16[2,1,128,128]{3,2,1,0:T(8,128)(2,1)}, u32[]{:S(2)}) copy-start(bf16[2,1,128,128]{3,2,1,0:T(8,128)(2,1)} %param.8) | copy-start | bytes 196612
  6.5 78.6 %reduce-scatter.2.cloned.1.call-start = ((), (), s32[]{:S(2)}) async-start(), calls=%async_computation.1 | async-start | bytes 7077888 | tf_op jit(solution)/shard_map/reduce_scatter | solution.py:51
  86.1 11.9 %collective-permute-start = (f32[768,128]{0,1:T(8,128)S(1)}, f32[768,128]{0,1:T(8,128)S(1)}, u32[]{:S(2)}, u32[]{:S(2)}) collective-permute-start(f32[768,128]{0,1:T(8,128)S(1)} %slice_bitcast_fusion), channel_id=1, source_target_pairs={{0,8},{8,0},{16,24},{24,16},{1,9},{9,1},{17,25},{25,17},{2,10},{10... | collective-permute-start | bytes 1179656 | tf_op jit(solution)/shard_map/ppermute | solution.py:14
  98.1 11.1 %collective-permute-start.1 = (f32[768,128]{0,1:T(8,128)S(1)}, f32[768,128]{0,1:T(8,128)S(1)}, u32[]{:S(2)}, u32[]{:S(2)}) collective-permute-start(f32[768,128]{0,1:T(8,128)S(1)} %collective-permute-done), channel_id=1, source_target_pairs={{0,16},{16,0},{8,24},{24,8},{1,17},{17,1},{9,25},{25,9},{2,18},{18... | collective-permute-start | bytes 1179656 | tf_op jit(solution)/shard_map/ppermute | solution.py:14
Sparse Core Ops, SparseCore 0:
  16.9 68.1 reduce-scatter.1
where the time goes:
time: 118 us
  waiting for transfers between devices  89.5 us (76%)
  between operations  13.4 us (11%)
  matrix products  6.32 us (5%)
  other arithmetic  4.25 us (4%)
  local copies, waits for them, and re-layouts  2.54 us (2%)
  starting transfers between devices  1.89 us (2%)
    reduce_scatter x1, waiting for transfers between devices, body(): reduced = lax.psum_scatter(stacked, 'dp', scatter_dimension=1, tiled=True)  68.3 us
    ppermute x2, waiting for transfers between devices, partner(): return lax.ppermute(block, axis, route)  21.2 us
    dot_general x2, matrix products, section_partial(): jnp.einsum('td,te->de', acts, grad_v, preferred_element_type=jnp.float32)  4.42 us
    another operation x1, other arithmetic, body(): jnp.stack([lower_part.astype(jnp.float32), upper_part.astype(jnp.float32)])  3.07 us
  transfers between devices with their start and end apart: 3, of which 3 were waited for; matrix products, arithmetic and copies ran while one was open for 0% of the time, Pallas kernels for 0%

commit v1 on v0

v1 whole, which is shorter than its diff:
```python
import jax
import jax.numpy as jnp
from jax import lax
from jax.sharding import PartitionSpec as P


def section_grad_v(query_rows, key_rows, grad_rows, segs):
    length = query_rows.shape[0]
    scores = jnp.dot(query_rows, key_rows.T, preferred_element_type=jnp.float32) / jnp.sqrt(
        jnp.float32(query_rows.shape[1])
    )
    position = jnp.arange(length, dtype=jnp.int32)
    keep = (position[None, :] <= position[:, None]) & (segs[None, :] == segs[:, None])
    masked = jnp.where(keep, scores, jnp.float32(-1e30))
    top = jnp.max(masked, axis=1, keepdims=True)
    weights = jnp.where(keep, jnp.exp(masked - top), jnp.float32(0.0))
    probs = (weights / jnp.sum(weights, axis=1, keepdims=True)).astype(jnp.bfloat16)
    return jnp.einsum("qk,qd->kd", probs, grad_rows, preferred_element_type=jnp.float32).astype(
        jnp.bfloat16
    )


def body(activations, queries, keys, grad_out, segment_ids):
    ways = lax.axis_size("dp")
    slots = lax.axis_size("pipe")
    chips = ways // 2
    me = lax.axis_index("dp")
    width = activations.shape[3] // ways
    grads = [
        section_grad_v(queries[h, 0], keys[h, 0], grad_out[h, 0], segment_ids[h, 0, 0])
        for h in range(2)
    ]

    def part(half, owner):
        acts = lax.dynamic_slice_in_dim(activations[half, 0], owner * width, width, axis=1)
        return jnp.einsum("te,td->ed", grads[half], acts, preferred_element_type=jnp.float32)

    def swap(block, distance):
        return lax.ppermute(block, "dp", [(i, i ^ distance) for i in range(ways)])

    def mirror(block):
        return lax.ppermute(block, "pipe", [(i, slots - 1 - i) for i in range(slots)])

    total = [None] * chips
    for r in reversed(range(chips)):
        owner = me ^ (2 * r)
        got = swap(jnp.stack([part(1, owner ^ 1), part(0, owner ^ 1)]), 1)
        moved = mirror(part(1, owner) + got[0])
        total[r] = part(0, owner) + got[1] + moved
    for r in reversed(range(1, chips)):
        low = r & -r
        total[r ^ low] = total[r ^ low] + swap(total[r], 2 * low)
    return total[0].T.astype(jnp.bfloat16)[None]


def solution(mesh):
    spec = P(None, "pipe", "dp", None)
    return jax.shard_map(
        body,
        mesh=mesh,
        in_specs=(spec,) * 5,
        out_specs=P("pipe", "dp", None),
        check_vma=False,
    )
```

time: 118 us -> 69.1 us (0.59)
  the two profiles are of different devices: /device:TPU:12 before, /device:TPU:0 now
where the time goes in v1:
time: 69.1 us; the launch traced here: 68.5 us
  waiting for transfers between devices  26.8 us (39%)
  starting transfers between devices  18 us (26%)
  matrix products  11.6 us (17%)
  other arithmetic  8.22 us (12%)
  local copies, waits for them, and re-layouts  3.62 us (5%)
    ppermute x4, waiting for transfers between devices, mirror(): lax.ppermute(block, 'pipe', [(i, slots - 1 - i) for i in range(slots)])  14.3 us
    ppermute x7, waiting for transfers between devices, swap(): return lax.ppermute(block, 'dp', [(i, i ^ distance) for i in range(ways)])  12.6 us
    ppermute x4, starting transfers between devices, mirror(): lax.ppermute(block, 'pipe', [(i, slots - 1 - i) for i in range(slots)])  9.49 us
    dot_general x16, matrix products, part(): jnp.einsum('te,td->ed', grads[half], acts, preferred_element_type=jnp.flo...  9.32 us
    ppermute x7, starting transfers between devices, swap(): return lax.ppermute(block, 'dp', [(i, i ^ distance) for i in range(ways)])  8.51 us
    another operation x4, other arithmetic, body(): got = swap(jnp.stack([part(1, owner ^ 1), part(0, owner ^ 1)]), 1)  3.79 us
    add x2, other arithmetic, body(): total[r] = part(0, owner) + got[1] + moved  2.15 us
    slice x1, local copies, waits for them, and re-layouts, part(): activations[half, 0]  2.12 us
  transfers between devices with their start and end apart: 11, of which 5 were waited for; matrix products, arithmetic and copies ran while one was open for 22% of the time, Pallas kernels for 0%

profile of v1, /device:TPU:0, one launch (start us, length us, event | category | flops | bytes accessed | tf_op | source)
XLA Modules:
  0.0 68.5 jit_solution(1068598748967264841)
XLA Ops:
  0.0 0.7 slice_bitcast_fusion.8
  0.7 1.0 %fusion.112 = (f32[128]{0:T(128)S(1)}, f32[128,128]{0,1:T(8,128)S(1)}) fusion(bf16[2,1,128,128]{3,2,1,0:T(8,128)(2,1)} %param.7, bf16[2,1,128,128]{3,2,1,0:T(8,128)(2,1)} %param.6, s32[128]{0:T(128)S(1)} %get-tuple-element.8), kind=kOutput, calls=%fused_computation.135 | convolution fusion | flops 4292480 | bytes 132608 | tf_op jit(solution)/shard_map/dot_general | solution.py:9
  1.6 1.0 %fusion.113 = (f32[128]{0:T(128)S(1)}, f32[128,128]{0,1:T(8,128)S(1)}) fusion(bf16[2,1,128,128]{3,2,1,0:T(8,128)(2,1)} %param.7, bf16[2,1,128,128]{3,2,1,0:T(8,128)(2,1)} %param.6, s32[128]{0:T(128)S(1)} %get-tuple-element.7), kind=kOutput, calls=%fused_computation.136 | convolution fusion | flops 4292480 | bytes 132608 | tf_op jit(solution)/shard_map/dot_general | solution.py:9
  2.6 2.1 %fusion.111 = (bf16[1,1,128,6144]{3,2,1,0:T(8,128)(2,1)S(1)}, bf16[1,1,128,6144]{3,2,1,0:T(8,128)(2,1)S(1)}) fusion(bf16[2,1,128,6144]{3,2,1,0:T(8,128)(2,1)} %param.5), kind=kLoop, calls=%fused_computation.134 | loop fusion | bytes 6291456 | tf_op jit(solution)/shard_map/slice | solution.py:35
  5.8 0.9 %pad_maximum_fusion.3 = f32[2,128,768]{2,1,0:T(8,128)} fusion(f32[1,128,768]{2,1,0:T(8,128)S(1)} %convolution_bitcast_fusion, f32[1,128,768]{2,1,0:T(8,128)S(1)} %convolution_bitcast_fusion.1), kind=kLoop, calls=%fused_computation.17 | loop fusion | flops 196608 | bytes 1572864 | tf_op jit(solution)/shard_map/stack | solution.py:47
  6.7 0.5 collective-permute-start.8
  7.6 1.0 %pad_maximum_fusion.2 = f32[2,128,768]{2,1,0:T(8,128)} fusion(f32[1,128,768]{2,1,0:T(8,128)S(1)} %convolution_bitcast_fusion.2, f32[1,128,768]{2,1,0:T(8,128)S(1)} %convolution_bitcast_fusion.3), kind=kLoop, calls=%fused_computation.16 | loop fusion | flops 196608 | bytes 1572864 | tf_op jit(solution)/shard_map/stack | solution.py:47
  9.1 0.9 %pad_maximum_fusion.1 = f32[2,128,768]{2,1,0:T(8,128)} fusion(f32[1,128,768]{2,1,0:T(8,128)S(1)} %convolution_bitcast_fusion.4, f32[1,128,768]{2,1,0:T(8,128)S(1)} %convolution_bitcast_fusion.5), kind=kLoop, calls=%fused_computation.15 | loop fusion | flops 196608 | bytes 1572864 | tf_op jit(solution)/shard_map/stack | solution.py:47
  10.1 0.4 collective-permute-start.2
  11.0 0.9 %pad_maximum_fusion = f32[2,128,768]{2,1,0:T(8,128)} fusion(f32[1,128,768]{2,1,0:T(8,128)S(1)} %convolution_bitcast_fusion.6, f32[1,128,768]{2,1,0:T(8,128)S(1)} %convolution_bitcast_fusion.7), kind=kLoop, calls=%fused_computation.14 | loop fusion | flops 196608 | bytes 1572864 | tf_op jit(solution)/shard_map/stack | solution.py:47
  12.0 1.0 %fusion.25 = f32[128,768]{1,0:T(8,128)} fusion(bf16[128,128]{1,0:T(8,128)(2,1)S(1)} %convolution_convert_fusion.1, bf16[1,1,128,6144]{3,2,1,0:T(8,128)(2,1)S(1)} %get-tuple-element.6, s32[]{:T(128)S(6)} %select_n.55), kind=kOutput, calls=%fused_computation.47 | convolution fusion | flops 25165824 | bytes 622596 | tf_op jit(solution)/shard_map/te,td->ed/dot_general | solution.py:36
  13.0 1.0 %fusion.33 = f32[128,768]{1,0:T(8,128)} fusion(bf16[128,128]{1,0:T(8,128)(2,1)S(1)} %convolution_convert_fusion.1, bf16[1,1,128,6144]{3,2,1,0:T(8,128)(2,1)S(1)} %get-tuple-element.6, s32[]{:T(128)S(6)} %select_n.53), kind=kOutput, calls=%fused_computation.53 | convolution fusion | flops 25165824 | bytes 622596 | tf_op jit(solution)/shard_map/te,td->ed/dot_general | solution.py:36
  14.3 1.3 %fusion.5 = f32[128,768]{1,0:T(8,128)S(1)} fusion(f32[2,128,768]{2,1,0:T(8,128)} %collective-permute-done.4, bf16[128,128]{1,0:T(8,128)(2,1)S(1)} %convolution_convert_fusion, bf16[1,1,128,6144]{3,2,1,0:T(8,128)(2,1)S(1)} %get-tuple-element.5, s32[]{:T(128)S(6)} %select_n.53), kind=kOutput, calls=%fused_computation.24 | convolution fusion | flops 25264128 | bytes 1015812 | tf_op jit(solution)/shard_map/te,td->ed/dot_general | solution.py:36
  15.5 4.0 %collective-permute-start.5 = (f32[128,768]{1,0:T(8,128)S(1)}, f32[128,768]{1,0:T(8,128)S(1)}, u32[]{:S(2)}, u32[]{:S(2)}) collective-permute-start(f32[128,768]{1,0:T(8,128)S(1)} %fusion.5), channel_id=1, source_target_pairs={{0,24},{8,16},{16,8},{24,0},{1,25},{9,17},{17,9},{25,1},{2,26},{10... | collective-permute-start | bytes 1179656 | tf_op jit(solution)/shard_map/ppermute | solution.py:42
  19.5 1.2 %fusion.2 = f32[128,768]{1,0:T(8,128)S(1)} fusion(f32[2,128,768]{2,1,0:T(8,128)} %collective-permute-done.8, bf16[128,128]{1,0:T(8,128)(2,1)S(1)} %convolution_convert_fusion, bf16[1,1,128,6144]{3,2,1,0:T(8,128)(2,1)S(1)} %get-tuple-element.5, s32[]{:T(128)S(6)} %select_n.55), kind=kOutput, calls=%fused_computation.19 | convolution fusion | flops 25264128 | bytes 1015812 | tf_op jit(solution)/shard_map/te,td->ed/dot_general | solution.py:36
  20.9 1.3 %fusion.8 = f32[128,768]{1,0:T(8,128)S(1)} fusion(f32[2,128,768]{2,1,0:T(8,128)} %collective-permute-done.2, bf16[128,128]{1,0:T(8,128)(2,1)S(1)} %convolution_convert_fusion, bf16[1,1,128,6144]{3,2,1,0:T(8,128)(2,1)S(1)} %get-tuple-element.5, s32[]{:T(128)S(6)} %select_n.51), kind=kOutput, calls=%fused_computation.29 | convolution fusion | flops 25264128 | bytes 1015812 | tf_op jit(solution)/shard_map/te,td->ed/dot_general | solution.py:36
  22.1 2.9 %collective-permute-start.3 = (f32[128,768]{1,0:T(8,128)S(1)}, f32[128,768]{1,0:T(8,128)S(1)}, u32[]{:S(2)}, u32[]{:S(2)}) collective-permute-start(f32[128,768]{1,0:T(8,128)S(1)} %fusion.8), channel_id=1, source_target_pairs={{0,24},{8,16},{16,8},{24,0},{1,25},{9,17},{17,9},{25,1},{2,26},{10... | collective-permute-start | bytes 1179656 | tf_op jit(solution)/shard_map/ppermute | solution.py:42
  25.1 4.4 %collective-permute-done.5 = f32[128,768]{1,0:T(8,128)S(1)} collective-permute-done((f32[128,768]{1,0:T(8,128)S(1)}, f32[128,768]{1,0:T(8,128)S(1)}, u32[]{:S(2)}, u32[]{:S(2)}) %collective-permute-start.5) | collective-permute-done | bytes 393248 | tf_op jit(solution)/shard_map/ppermute | solution.py:42
  29.4 1.1 %fusion.7 = f32[128,768]{1,0:T(8,128)S(1)} fusion(f32[128,768]{1,0:T(8,128)S(1)} %collective-permute-done.5, f32[128,768]{1,0:T(8,128)S(1)} %copy-done.1, f32[2,128,768]{2,1,0:T(8,128)} %collective-permute-done.4), kind=kLoop, calls=%fused_computation.27 | loop fusion | flops 196608 | bytes 1572864 | tf_op jit(solution)/shard_map/add | solution.py:49
  30.5 2.2 %collective-permute-start.6 = (f32[128,768]{1,0:T(8,128)S(1)}, f32[128,768]{1,0:T(8,128)S(1)}, u32[]{:S(2)}, u32[]{:S(2)}) collective-permute-start(f32[128,768]{1,0:T(8,128)S(1)} %fusion.7), channel_id=1, source_target_pairs={{0,2},{1,3},{2,0},{3,1},{4,6},{5,7},{6,4},{7,5},{8,10},{9,11},{10,... | collective-permute-start | bytes 1179656 | tf_op jit(solution)/shard_map/ppermute | solution.py:39
  32.7 1.2 %fusion.12 = f32[128,768]{1,0:T(8,128)S(1)} fusion(f32[2,128,768]{2,1,0:T(8,128)} %collective-permute-done, bf16[128,128]{1,0:T(8,128)(2,1)S(1)} %convolution_convert_fusion, bf16[1,1,128,6144]{3,2,1,0:T(8,128)(2,1)S(1)} %get-tuple-element.5, s32[]{:T(128)S(6)} %select_n.47), kind=kOutput, calls=%fused_computation.35 | convolution fusion | flops 25264128 | bytes 1015812 | tf_op jit(solution)/shard_map/te,td->ed/dot_general | solution.py:36
  33.9 2.5 %collective-permute-start.1 = (f32[128,768]{1,0:T(8,128)S(1)}, f32[128,768]{1,0:T(8,128)S(1)}, u32[]{:S(2)}, u32[]{:S(2)}) collective-permute-start(f32[128,768]{1,0:T(8,128)S(1)} %fusion.12), channel_id=1, source_target_pairs={{0,24},{8,16},{16,8},{24,0},{1,25},{9,17},{17,9},{25,1},{2,26},{10... | collective-permute-start | bytes 1179656 | tf_op jit(solution)/shard_map/ppermute | solution.py:42
  36.4 1.4 %collective-permute-done.9 = f32[128,768]{1,0:T(8,128)S(1)} collective-permute-done((f32[128,768]{1,0:T(8,128)S(1)}, f32[128,768]{1,0:T(8,128)S(1)}, u32[]{:S(2)}, u32[]{:S(2)}) %collective-permute-start.9) | collective-permute-done | bytes 393248 | tf_op jit(solution)/shard_map/ppermute | solution.py:42
  37.9 1.1 %fusion.4 = f32[128,768]{1,0:T(8,128)S(1)} fusion(f32[128,768]{1,0:T(8,128)S(1)} %collective-permute-done.9, f32[128,768]{1,0:T(8,128)S(1)} %copy-done, f32[2,128,768]{2,1,0:T(8,128)} %collective-permute-done.8), kind=kLoop, calls=%fused_computation.22 | loop fusion | flops 196608 | bytes 1572864 | tf_op jit(solution)/shard_map/add | solution.py:49
  38.9 2.2 %collective-permute-start.10 = (f32[128,768]{1,0:T(8,128)S(1)}, f32[128,768]{1,0:T(8,128)S(1)}, u32[]{:S(2)}, u32[]{:S(2)}) collective-permute-start(f32[128,768]{1,0:T(8,128)S(1)} %fusion.4), channel_id=1, source_target_pairs={{0,2},{1,3},{2,0},{3,1},{4,6},{5,7},{6,4},{7,5},{8,10},{9,11},{10,... | collective-permute-start | bytes 1179656 | tf_op jit(solution)/shard_map/ppermute | solution.py:39
  41.1 5.2 %collective-permute-done.3 = f32[128,768]{1,0:T(8,128)S(1)} collective-permute-done((f32[128,768]{1,0:T(8,128)S(1)}, f32[128,768]{1,0:T(8,128)S(1)}, u32[]{:S(2)}, u32[]{:S(2)}) %collective-permute-start.3) | collective-permute-done | bytes 393248 | tf_op jit(solution)/shard_map/ppermute | solution.py:42
  46.3 1.1 %fusion.11 = f32[128,768]{1,0:T(8,128)S(1)} fusion(f32[128,768]{1,0:T(8,128)S(1)} %collective-permute-done.6, f32[128,768]{1,0:T(8,128)S(1)} %collective-permute-done.3, f32[128,768]{1,0:T(8,128)S(1)} %fusion.41, f32[2,128,768]{2,1,0:T(8,128)} %collective-permute-done.2), kind=kLoop, calls=%fused_computation.33 | loop fusion | flops 294912 | bytes 1966080 | tf_op jit(solution)/shard_map/add | solution.py:52
  47.4 3.2 %collective-permute-start.7 = (f32[128,768]{1,0:T(8,128)S(1)}, f32[128,768]{1,0:T(8,128)S(1)}, u32[]{:S(2)}, u32[]{:S(2)}) collective-permute-start(f32[128,768]{1,0:T(8,128)S(1)} %fusion.11), channel_id=1, source_target_pairs={{0,4},{1,5},{2,6},{3,7},{4,0},{5,1},{6,2},{7,3},{8,12},{9,13},{10,... | collective-permute-start | bytes 1179656 | tf_op jit(solution)/shard_map/ppermute | solution.py:39
  50.8 3.3 %collective-permute-done.1 = f32[128,768]{1,0:T(8,128)S(1)} collective-permute-done((f32[128,768]{1,0:T(8,128)S(1)}, f32[128,768]{1,0:T(8,128)S(1)}, u32[]{:S(2)}, u32[]{:S(2)}) %collective-permute-start.1) | collective-permute-done | bytes 393248 | tf_op jit(solution)/shard_map/ppermute | solution.py:42
  54.1 12.5 %collective-permute-done.7 = f32[128,768]{1,0:T(8,128)S(1)} collective-permute-done((f32[128,768]{1,0:T(8,128)S(1)}, f32[128,768]{1,0:T(8,128)S(1)}, u32[]{:S(2)}, u32[]{:S(2)}) %collective-permute-start.7) | collective-permute-done | bytes 393248 | tf_op jit(solution)/shard_map/ppermute | solution.py:39
  66.6 1.1 %fusion.18 = bf16[1,768,128]{1,2,0:T(8,128)(2,1)S(1)} fusion(f32[128,768]{1,0:T(8,128)S(1)} %collective-permute-done.10, f32[128,768]{1,0:T(8,128)S(1)} %collective-permute-done.7, f32[128,768]{1,0:T(8,128)S(1)} %collective-permute-done.1, f32[128,768]{1,0:T(8,128)S(1)} %fusion.49, f32[2,128,768]{2,1,0:T(8,128)} %collective-permute-done), kind=kLoop, calls=%fused_computation.42 | loop fusion | flops 491520 | bytes 2162688 | tf_op jit(solution)/shard_map/broadcast_in_dim | solution.py:53
  67.7 0.8 %copy.6 = bf16[1,768,128]{2,1,0:T(8,128)(2,1)} copy(bf16[1,768,128]{1,2,0:T(8,128)(2,1)S(1)} %fusion.18) | data formatting | bytes 393216 | tf_op jit(solution)/shard_map/broadcast_in_dim | solution.py:53
  (28 shorter events, 3.1 us)
Async XLA Ops:
  2.6 2.3 %copy-start.2 = (bf16[2,1,128,128]{3,2,1,0:T(8,128)(2,1)S(1)}, bf16[2,1,128,128]{3,2,1,0:T(8,128)(2,1)}, u32[]{:S(2)}) copy-start(bf16[2,1,128,128]{3,2,1,0:T(8,128)(2,1)} %param.8) | copy-start | bytes 196612
  6.7 12.8 %collective-permute-start.8 = (f32[2,128,768]{2,1,0:T(8,128)}, f32[2,128,768]{2,1,0:T(8,128)}, u32[]{:S(2)}, u32[]{:S(2)}) collective-permute-start(f32[2,128,768]{2,1,0:T(8,128)} %pad_maximum_fusion.3), channel_id=1, source_target_pairs={{0,1},{1,0},{2,3},{3,2},{4,5},{5,4},{6,7},{7,6},{8,9},{9,8},{10,11... | collective-permute-start | bytes 2359304 | tf_op jit(solution)/shard_map/ppermute | solution.py:39
  8.6 5.7 %collective-permute-start.4 = (f32[2,128,768]{2,1,0:T(8,128)}, f32[2,128,768]{2,1,0:T(8,128)}, u32[]{:S(2)}, u32[]{:S(2)}) collective-permute-start(f32[2,128,768]{2,1,0:T(8,128)} %pad_maximum_fusion.2), channel_id=1, source_target_pairs={{0,1},{1,0},{2,3},{3,2},{4,5},{5,4},{6,7},{7,6},{8,9},{9,8},{10,11... | collective-permute-start | bytes 2359304 | tf_op jit(solution)/shard_map/ppermute | solution.py:39
  10.1 10.8 %collective-permute-start.2 = (f32[2,128,768]{2,1,0:T(8,128)}, f32[2,128,768]{2,1,0:T(8,128)}, u32[]{:S(2)}, u32[]{:S(2)}) collective-permute-start(f32[2,128,768]{2,1,0:T(8,128)} %pad_maximum_fusion.1), channel_id=1, source_target_pairs={{0,1},{1,0},{2,3},{3,2},{4,5},{5,4},{6,7},{7,6},{8,9},{9,8},{10,11... | collective-permute-start | bytes 2359304 | tf_op jit(solution)/shard_map/ppermute | solution.py:39
  12.0 20.7 %collective-permute-start = (f32[2,128,768]{2,1,0:T(8,128)}, f32[2,128,768]{2,1,0:T(8,128)}, u32[]{:S(2)}, u32[]{:S(2)}) collective-permute-start(f32[2,128,768]{2,1,0:T(8,128)} %pad_maximum_fusion), channel_id=1, source_target_pairs={{0,1},{1,0},{2,3},{3,2},{4,5},{5,4},{6,7},{7,6},{8,9},{9,8},{10,11... | collective-permute-start | bytes 2359304 | tf_op jit(solution)/shard_map/ppermute | solution.py:39
  14.2 15.2 %copy-start.1 = (f32[128,768]{1,0:T(8,128)S(1)}, f32[128,768]{1,0:T(8,128)}, u32[]{:S(2)}) copy-start(f32[128,768]{1,0:T(8,128)} %fusion.33) | copy-start | bytes 1179652
  15.5 13.9 %collective-permute-start.5 = (f32[128,768]{1,0:T(8,128)S(1)}, f32[128,768]{1,0:T(8,128)S(1)}, u32[]{:S(2)}, u32[]{:S(2)}) collective-permute-start(f32[128,768]{1,0:T(8,128)S(1)} %fusion.5), channel_id=1, source_target_pairs={{0,24},{8,16},{16,8},{24,0},{1,25},{9,17},{17,9},{25,1},{2,26},{10... | collective-permute-start | bytes 1179656 | tf_op jit(solution)/shard_map/ppermute | solution.py:42
  20.8 17.1 %copy-start = (f32[128,768]{1,0:T(8,128)S(1)}, f32[128,768]{1,0:T(8,128)}, u32[]{:S(2)}) copy-start(f32[128,768]{1,0:T(8,128)} %fusion.25) | copy-start | bytes 1179652
  20.8 17.1 %collective-permute-start.9 = (f32[128,768]{1,0:T(8,128)S(1)}, f32[128,768]{1,0:T(8,128)S(1)}, u32[]{:S(2)}, u32[]{:S(2)}) collective-permute-start(f32[128,768]{1,0:T(8,128)S(1)} %fusion.2), channel_id=1, source_target_pairs={{0,24},{8,16},{16,8},{24,0},{1,25},{9,17},{17,9},{25,1},{2,26},{10... | collective-permute-start | bytes 1179656 | tf_op jit(solution)/shard_map/ppermute | solution.py:42
  22.1 24.1 %collective-permute-start.3 = (f32[128,768]{1,0:T(8,128)S(1)}, f32[128,768]{1,0:T(8,128)S(1)}, u32[]{:S(2)}, u32[]{:S(2)}) collective-permute-start(f32[128,768]{1,0:T(8,128)S(1)} %fusion.8), channel_id=1, source_target_pairs={{0,24},{8,16},{16,8},{24,0},{1,25},{9,17},{17,9},{25,1},{2,26},{10... | collective-permute-start | bytes 1179656 | tf_op jit(solution)/shard_map/ppermute | solution.py:42
  30.5 15.8 %collective-permute-start.6 = (f32[128,768]{1,0:T(8,128)S(1)}, f32[128,768]{1,0:T(8,128)S(1)}, u32[]{:S(2)}, u32[]{:S(2)}) collective-permute-start(f32[128,768]{1,0:T(8,128)S(1)} %fusion.7), channel_id=1, source_target_pairs={{0,2},{1,3},{2,0},{3,1},{4,6},{5,7},{6,4},{7,5},{8,10},{9,11},{10,... | collective-permute-start | bytes 1179656 | tf_op jit(solution)/shard_map/ppermute | solution.py:39
  33.9 20.2 %collective-permute-start.1 = (f32[128,768]{1,0:T(8,128)S(1)}, f32[128,768]{1,0:T(8,128)S(1)}, u32[]{:S(2)}, u32[]{:S(2)}) collective-permute-start(f32[128,768]{1,0:T(8,128)S(1)} %fusion.12), channel_id=1, source_target_pairs={{0,24},{8,16},{16,8},{24,0},{1,25},{9,17},{17,9},{25,1},{2,26},{10... | collective-permute-start | bytes 1179656 | tf_op jit(solution)/shard_map/ppermute | solution.py:42
  38.9 15.1 %collective-permute-start.10 = (f32[128,768]{1,0:T(8,128)S(1)}, f32[128,768]{1,0:T(8,128)S(1)}, u32[]{:S(2)}, u32[]{:S(2)}) collective-permute-start(f32[128,768]{1,0:T(8,128)S(1)} %fusion.4), channel_id=1, source_target_pairs={{0,2},{1,3},{2,0},{3,1},{4,6},{5,7},{6,4},{7,5},{8,10},{9,11},{10,... | collective-permute-start | bytes 1179656 | tf_op jit(solution)/shard_map/ppermute | solution.py:39
  47.4 19.2 %collective-permute-start.7 = (f32[128,768]{1,0:T(8,128)S(1)}, f32[128,768]{1,0:T(8,128)S(1)}, u32[]{:S(2)}, u32[]{:S(2)}) collective-permute-start(f32[128,768]{1,0:T(8,128)S(1)} %fusion.11), channel_id=1, source_target_pairs={{0,4},{1,5},{2,6},{3,7},{4,0},{5,1},{6,2},{7,3},{8,12},{9,13},{10,... | collective-permute-start | bytes 1179656 | tf_op jit(solution)/shard_map/ppermute | solution.py:39

commit v2 on v1

v2 whole, which is shorter than its diff:
```python
import functools

import jax
import jax.numpy as jnp
from jax import lax
from jax.experimental import pallas as pl
from jax.experimental.pallas import tpu as pltpu
from jax.sharding import PartitionSpec as P

VMEM = pl.BlockSpec(memory_space=pltpu.VMEM)
SMALL = pltpu.CompilerParams(vmem_limit_bytes=8 << 20)


def grad_v_columns(query_rows, key_rows, grad_rows, segs):
    length, head = query_rows.shape
    scores = lax.dot_general(
        query_rows, key_rows, (((1,), (1,)), ((), ())), preferred_element_type=jnp.float32
    ) / jnp.sqrt(jnp.float32(head))
    shape = (length, length)
    across = jnp.broadcast_to(segs, shape)
    keep = (across == across.T) & (
        lax.broadcasted_iota(jnp.int32, shape, 1) <= lax.broadcasted_iota(jnp.int32, shape, 0)
    )
    masked = jnp.where(keep, scores, jnp.float32(-1e30))
    top = jnp.max(masked, axis=1, keepdims=True)
    weights = jnp.where(keep, jnp.exp(masked - top), jnp.float32(0.0))
    probs = (weights / jnp.sum(weights, axis=1, keepdims=True)).astype(jnp.bfloat16)
    return lax.dot_general(
        grad_rows, probs, (((0,), (0,)), ((), ())), preferred_element_type=jnp.float32
    ).astype(jnp.bfloat16)


def block_columns(flip, width):
    owner = lax.axis_index("dp") ^ flip
    return pl.ds(pl.multiple_of(owner * width, 128), width)


def front_kernel(flip, width, acts, queries, keys, grad_out, segs, grads, first, *scratch):
    columns, ready = scratch[0], scratch[-1]
    sources = [queries, keys, grad_out, segs, acts.at[1, 0, :, block_columns(flip, width)]]
    holders = [*scratch[1:-1], columns]
    copies = [
        pltpu.make_async_copy(source, holder, ready.at[i])
        for i, (source, holder) in enumerate(zip(sources, holders))
    ]
    for copy in copies:
        copy.start()
    for copy in copies[:-1]:
        copy.wait()
    query_rows, key_rows, grad_rows, seg_rows = scratch[1:-1]
    for half in (1, 0):
        grads[half] = grad_v_columns(
            query_rows[half, 0], key_rows[half, 0], grad_rows[half, 0], seg_rows[half, 0]
        )
    copies[-1].wait()
    first[0] = jnp.dot(grads[1], columns[...], preferred_element_type=jnp.float32)


def front(activations, queries, keys, grad_out, segment_ids, flip, width):
    head, length = queries.shape[3], queries.shape[2]
    if width % 128:
        grads = jnp.stack(
            [
                grad_v_columns(
                    queries[h, 0], keys[h, 0], grad_out[h, 0], segment_ids[h, 0]
                )
                for h in range(2)
            ]
        )
        return grads, *plain_blocks(activations, grads, width, [[[(DOT, 1, flip)]]])
    small = (queries, keys, grad_out, segment_ids)
    return pl.pallas_call(
        functools.partial(front_kernel, flip, width),
        out_shape=(
            jax.ShapeDtypeStruct((2, head, length), jnp.bfloat16),
            jax.ShapeDtypeStruct((1, head, width), jnp.float32),
        ),
        in_specs=[pl.BlockSpec(memory_space=pltpu.HBM)] * 5,
        out_specs=(VMEM, VMEM),
        scratch_shapes=[
            pltpu.VMEM((length, width), activations.dtype),
            *(pltpu.VMEM(value.shape, value.dtype) for value in small),
            pltpu.SemaphoreType.DMA((5,)),
        ],
        compiler_params=SMALL,
        name="front",
    )(activations, *small)


def plain_blocks(acts, grads, width, plan):
    def slab(terms):
        value = None
        for term in terms:
            if term[0] is DOT:
                owner = lax.axis_index("dp") ^ term[2]
                columns = lax.dynamic_slice_in_dim(acts[term[1], 0], owner * width, width, axis=1)
                term = jnp.dot(grads[term[1]], columns, preferred_element_type=jnp.float32)
            else:
                term = term[0][term[1]]
            value = term if value is None else value + term
        return value

    return tuple(jnp.stack([slab(terms) for terms in slabs]) for slabs in plan)


def blocks_kernel(plan, count, width, *refs):
    outs = refs[count:]
    acts, grads = refs[0], refs[1]
    for out, slabs in zip(outs, plan):
        for place, (dots, adds) in enumerate(slabs):
            value = None
            for half, flip in dots:
                term = jnp.dot(
                    grads[half],
                    acts[half, 0, :, block_columns(flip, width)],
                    preferred_element_type=jnp.float32,
                )
                value = term if value is None else value + term
            for operand, slab in adds:
                term = refs[operand][slab]
                value = term if value is None else value + term
            out[place] = value


def blocks(name, acts, grads, width, plan):
    if width % 128:
        return plain_blocks(acts, grads, width, plan)
    operands = [acts, grads]
    numbers = {}
    static = []
    for slabs in plan:
        made = []
        for terms in slabs:
            dots = tuple(term[1:] for term in terms if term[0] is DOT)
            adds = []
            for term in terms:
                if term[0] is not DOT:
                    if id(term[0]) not in numbers:
                        numbers[id(term[0])] = len(operands)
                        operands.append(term[0])
                    adds.append((numbers[id(term[0])], term[1]))
            made.append((dots, tuple(adds)))
        static.append(tuple(made))
    head = grads.shape[1]
    return pl.pallas_call(
        functools.partial(blocks_kernel, tuple(static), len(operands), width),
        out_shape=tuple(
            jax.ShapeDtypeStruct((len(slabs), head, width), jnp.float32) for slabs in static
        ),
        in_specs=[VMEM] * len(operands),
        out_specs=tuple(VMEM for _ in static),
        compiler_params=SMALL,
        name=name,
    )(*operands)


DOT = object()


def finish_kernel(count, *refs):
    out = refs[count]
    for low in range(0, out.shape[1], 128):
        value = refs[0][0, :, low : low + 128]
        for ref in refs[1:count]:
            value = value + ref[0, :, low : low + 128]
        out[0, low : low + 128, :] = value.T.astype(out.dtype)


def finish(terms):
    head, width = terms[0].shape[1:]
    if width % 128:
        return functools.reduce(jnp.add, terms).swapaxes(1, 2).astype(jnp.bfloat16)
    return pl.pallas_call(
        functools.partial(finish_kernel, len(terms)),
        out_shape=jax.ShapeDtypeStruct((1, width, head), jnp.bfloat16),
        in_specs=[VMEM] * len(terms),
        out_specs=VMEM,
        compiler_params=SMALL,
        name="finish",
    )(*terms)


def body(activations, queries, keys, grad_out, segment_ids):
    ways = lax.axis_size("dp")
    slots = lax.axis_size("pipe")
    chips = ways // 2
    width = activations.shape[3] // ways

    def swap(block, distance):
        return lax.ppermute(block, "dp", [(i, i ^ distance) for i in range(ways)])

    def mirror(block):
        return lax.ppermute(block, "pipe", [(i, slots - 1 - i) for i in range(slots)])

    last = chips - 1
    grads, first = front(
        activations, queries, keys, grad_out, segment_ids, 2 * last + 1, width
    )
    make = functools.partial(blocks, acts=activations, grads=grads, width=width)
    order = list(reversed(range(chips)))
    got_upper = {last: swap(first, 1)}
    got_lower = {}
    for r in order:
        plan = [[[(DOT, 0, 2 * r + 1)]]]
        if r != last:
            plan.append([[(DOT, 1, 2 * r + 1)]])
        sent = make("theirs", plan=plan)
        got_lower[r] = swap(sent[0], 1)
        if r != last:
            got_upper[r] = swap(sent[1], 1)
    moved = {}
    for r in order:
        (upper,) = make("upper", plan=[[[(DOT, 1, 2 * r), (got_upper[r], 0)]]])
        moved[r] = mirror(upper)
    terms = {r: [(DOT, 0, 2 * r), (got_lower[r], 0), (moved[r], 0)] for r in order}
    (base,) = make("base", plan=[[terms[0][:2]]])
    terms[0] = [(base, 0), terms[0][2]]
    for r in order[:-1]:
        (total,) = make("lower", plan=[[terms[r]]])
        low = r & -r
        terms[r ^ low].append((swap(total, 2 * low), 0))
    return finish([term[0] for term in terms[0]])


def solution(mesh):
    spec = P(None, "pipe", "dp", None)
    return jax.shard_map(
        body,
        mesh=mesh,
        in_specs=(spec,) * 5,
        out_specs=P("pipe", "dp", None),
        check_vma=False,
    )
```

time: 69.1 us -> 60 us (0.87)
  matrix products: 11.6 us -> 0 us
  other arithmetic: 8.22 us -> 0 us
  Pallas kernels: 0 us -> 4.66 us
  waiting for transfers between devices: 26.8 us -> 31.3 us
  local copies, waits for them, and re-layouts: 3.62 us -> 5.08 us
    dot_general x20 -> x0, matrix products: 11.6 us -> none  [the longest x16 9.32 us: part(): jnp.einsum('te,td->ed', grads[half], acts, preferred_element_type=jnp.flo...]
    ppermute x4, waiting for transfers between devices: 14.3 us -> 19.6 us  [mirror(): lax.ppermute(block, 'pipe', [(i, slots - 1 - i) for i in range(slots)])]
    unnamed x6 -> x10, local copies, waits for them, and re-layouts: 0.01 us -> 5.08 us
    pallas_call x0 -> x14, Pallas kernels: none -> 4.66 us  [the longest x12 2.5 us: blocks(): pl.pallas_call(functools.partial(blocks_kernel, tuple(static), len(operan...]
    another operation x4 -> x0, other arithmetic: 3.79 us -> none  [body(): got = swap(jnp.stack([part(1, owner ^ 1), part(0, owner ^ 1)]), 1)]
    add x3 -> x0, other arithmetic: 3.23 us -> none  [the longest x2 2.15 us: body(): total[r] = part(0, owner) + got[1] + moved]
    slice x1 -> x0, local copies, waits for them, and re-layouts: 2.12 us -> none  [part(): activations[half, 0]]
    broadcast_in_dim x1 -> x0, other arithmetic: 1.09 us -> none  [body(): return total[0].T.astype(jnp.bfloat16)[None]]
  transfers between devices with their start and end apart: 11 -> 15, of which waited for: 5 -> 5; matrix products, arithmetic and copies ran while one was open for 22% -> 0% of each run, Pallas kernels for 0% -> 4%
where the time goes in v2:
time: 60 us; the launch traced here: 59.7 us
  waiting for transfers between devices  31.3 us (52%)
  starting transfers between devices  18.5 us (31%)
  local copies, waits for them, and re-layouts  5.08 us (8%)
  Pallas kernels  4.66 us (8%)
    ppermute x4, waiting for transfers between devices, mirror(): lax.ppermute(block, 'pipe', [(i, slots - 1 - i) for i in range(slots)])  19.6 us
    ppermute x11, waiting for transfers between devices, swap(): return lax.ppermute(block, 'dp', [(i, i ^ distance) for i in range(ways)])  11.7 us
    ppermute x4, starting transfers between devices, mirror(): lax.ppermute(block, 'pipe', [(i, slots - 1 - i) for i in range(slots)])  9.96 us
    ppermute x11, starting transfers between devices, swap(): return lax.ppermute(block, 'dp', [(i, i ^ distance) for i in range(ways)])  8.52 us
    unnamed x10, local copies, waits for them, and re-layouts  5.08 us
    pallas_call x12, Pallas kernels, blocks(): pl.pallas_call(functools.partial(blocks_kernel, tuple(static), len(operan...  2.5 us
    pallas_call x1, Pallas kernels, front(): pl.pallas_call(functools.partial(front_kernel, flip, width), out_shape=(j...  1.34 us
  transfers between devices with their start and end apart: 15, of which 5 were waited for; matrix products, arithmetic and copies ran while one was open for 0% of the time, Pallas kernels for 4%

profile of v2, /device:TPU:0, one launch (start us, length us, event | category | flops | bytes accessed | tf_op | source)
XLA Modules:
  0.0 59.7 jit_solution(10034211786872975831)
XLA Ops:
  0.0 1.9 %copy-done = bf16[2,1,128,6144]{3,2,1,0:T(8,128)(2,1)S(1)} copy-done((bf16[2,1,128,6144]{3,2,1,0:T(8,128)(2,1)S(1)}, bf16[2,1,128,6144]{3,2,1,0:T(8,128)(2,1)}, u32[]{:S(2)}) %copy-start) | copy-done | bytes 3145752
  1.9 0.8 %copy-done.1 = bf16[2,1,128,128]{3,2,1,0:T(8,128)(2,1)S(1)} copy-done((bf16[2,1,128,128]{3,2,1,0:T(8,128)(2,1)S(1)}, bf16[2,1,128,128]{3,2,1,0:T(8,128)(2,1)}, u32[]{:S(2)}) %copy-start.1) | copy-done | bytes 65560
  2.7 0.8 %copy-done.2 = bf16[2,1,128,128]{3,2,1,0:T(8,128)(2,1)S(1)} copy-done((bf16[2,1,128,128]{3,2,1,0:T(8,128)(2,1)S(1)}, bf16[2,1,128,128]{3,2,1,0:T(8,128)(2,1)}, u32[]{:S(2)}) %copy-start.2) | copy-done | bytes 65560
  3.6 0.8 %copy-done.3 = bf16[2,1,128,128]{3,2,1,0:T(8,128)(2,1)S(1)} copy-done((bf16[2,1,128,128]{3,2,1,0:T(8,128)(2,1)S(1)}, bf16[2,1,128,128]{3,2,1,0:T(8,128)(2,1)}, u32[]{:S(2)}) %copy-start.3) | copy-done | bytes 65560
  4.4 0.7 %copy-done.4 = s32[2,1,1,128]{3,2,1,0:T(1,128)S(1)} copy-done((s32[2,1,1,128]{3,2,1,0:T(1,128)S(1)}, s32[2,1,1,128]{3,2,1,0:T(1,128)}, u32[]{:S(2)}) %copy-start.4) | copy-done | bytes 1048
  5.1 1.3 %front.1 = (bf16[2,128,128]{2,1,0:T(8,128)(2,1)S(1)}, f32[1,128,768]{2,1,0:T(8,128)S(1)}) custom-call(bf16[2,1,128,6144]{3,2,1,0:T(8,128)(2,1)S(1)} %copy-done, bf16[2,1,128,128]{3,2,1,0:T(8,128)(2,1)S(1)} %copy-done.1, bf16[2,1,128,128]{3,2,1,0:T(8,128)(2,1)S(1)} %copy-done.2, bf16[2,1,128,128]{3,2,1,0:T(8,128)(2,1)S(1)} %copy-done.3, ...), custom_call_target="tpu_custom_call" | custom-call | tf_op jit(solution)/shard_map/front/pallas_call | solution.py:72
  6.4 0.5 collective-permute-start.7
  7.0 0.2 theirs.7
  7.3 0.2 theirs.5
  7.6 0.5 collective-permute-start.4
  8.4 0.2 upper.6
  8.6 4.0 %collective-permute-start.8 = (f32[1,128,768]{2,1,0:T(8,128)S(1)}, f32[1,128,768]{2,1,0:T(8,128)S(1)}, u32[]{:S(2)}, u32[]{:S(2)}) collective-permute-start(f32[1,128,768]{2,1,0:T(8,128)S(1)} %upper.6), channel_id=1, source_target_pairs={{0,24},{8,16},{16,8},{24,0},{1,25},{9,17},{17,9},{25,1},{2,26},{10... | collective-permute-start | bytes 1179656 | tf_op jit(solution)/shard_map/ppermute | solution.py:193
  12.6 0.2 theirs.4
  12.9 0.5 collective-permute-start.11
  13.4 0.2 upper.7
  13.7 0.2 upper.5
  14.1 8.4 %collective-permute-done.8.refs_3_ = f32[1,128,768]{2,1,0:T(8,128)S(1)} collective-permute-done((f32[1,128,768]{2,1,0:T(8,128)S(1)}, f32[1,128,768]{2,1,0:T(8,128)S(1)}, u32[]{:S(2)}, u32[]{:S(2)}) %collective-permute-start.8) | collective-permute-done | bytes 393248 | tf_op jit(solution)/shard_map/ppermute | solution.py:193
  22.5 3.0 %collective-permute-start.5 = (f32[1,128,768]{2,1,0:T(8,128)S(1)}, f32[1,128,768]{2,1,0:T(8,128)S(1)}, u32[]{:S(2)}, u32[]{:S(2)}) collective-permute-start(f32[1,128,768]{2,1,0:T(8,128)S(1)} %upper.5), channel_id=1, source_target_pairs={{0,24},{8,16},{16,8},{24,0},{1,25},{9,17},{17,9},{25,1},{2,26},{10... | collective-permute-start | bytes 1179656 | tf_op jit(solution)/shard_map/ppermute | solution.py:193
  25.5 0.2 lower.3
  25.7 1.6 %collective-permute-start.9 = (f32[1,128,768]{2,1,0:T(8,128)S(1)}, f32[1,128,768]{2,1,0:T(8,128)S(1)}, u32[]{:S(2)}, u32[]{:S(2)}) collective-permute-start(f32[1,128,768]{2,1,0:T(8,128)S(1)} %lower.3), channel_id=1, source_target_pairs={{0,2},{1,3},{2,0},{3,1},{4,6},{5,7},{6,4},{7,5},{8,10},{9,11},{10,... | collective-permute-start | bytes 1179656 | tf_op jit(solution)/shard_map/ppermute | solution.py:190
  27.3 0.2 upper.4
  27.6 3.3 %collective-permute-done.13.refs_3_ = f32[1,128,768]{2,1,0:T(8,128)S(1)} collective-permute-done((f32[1,128,768]{2,1,0:T(8,128)S(1)}, f32[1,128,768]{2,1,0:T(8,128)S(1)}, u32[]{:S(2)}, u32[]{:S(2)}) %collective-permute-start.13) | collective-permute-done | bytes 393248 | tf_op jit(solution)/shard_map/ppermute | solution.py:193
  30.9 3.0 %collective-permute-start.2 = (f32[1,128,768]{2,1,0:T(8,128)S(1)}, f32[1,128,768]{2,1,0:T(8,128)S(1)}, u32[]{:S(2)}, u32[]{:S(2)}) collective-permute-start(f32[1,128,768]{2,1,0:T(8,128)S(1)} %upper.4), channel_id=1, source_target_pairs={{0,24},{8,16},{16,8},{24,0},{1,25},{9,17},{17,9},{25,1},{2,26},{10... | collective-permute-start | bytes 1179656 | tf_op jit(solution)/shard_map/ppermute | solution.py:193
  33.9 0.2 lower.5
  34.1 1.6 %collective-permute-start.14 = (f32[1,128,768]{2,1,0:T(8,128)S(1)}, f32[1,128,768]{2,1,0:T(8,128)S(1)}, u32[]{:S(2)}, u32[]{:S(2)}) collective-permute-start(f32[1,128,768]{2,1,0:T(8,128)S(1)} %lower.5), channel_id=1, source_target_pairs={{0,2},{1,3},{2,0},{3,1},{4,6},{5,7},{6,4},{7,5},{8,10},{9,11},{10,... | collective-permute-start | bytes 1179656 | tf_op jit(solution)/shard_map/ppermute | solution.py:190
  35.7 3.6 %collective-permute-done.5.refs_3_ = f32[1,128,768]{2,1,0:T(8,128)S(1)} collective-permute-done((f32[1,128,768]{2,1,0:T(8,128)S(1)}, f32[1,128,768]{2,1,0:T(8,128)S(1)}, u32[]{:S(2)}, u32[]{:S(2)}) %collective-permute-start.5) | collective-permute-done | bytes 393248 | tf_op jit(solution)/shard_map/ppermute | solution.py:193
  39.4 0.2 lower.4
  39.6 3.2 %collective-permute-start.10 = (f32[1,128,768]{2,1,0:T(8,128)S(1)}, f32[1,128,768]{2,1,0:T(8,128)S(1)}, u32[]{:S(2)}, u32[]{:S(2)}) collective-permute-start(f32[1,128,768]{2,1,0:T(8,128)S(1)} %lower.4), channel_id=1, source_target_pairs={{0,4},{1,5},{2,6},{3,7},{4,0},{5,1},{6,2},{7,3},{8,12},{9,13},{10,... | collective-permute-start | bytes 1179656 | tf_op jit(solution)/shard_map/ppermute | solution.py:190
  42.7 0.2 base.1.refs_0_
  42.9 4.2 %collective-permute-done.2.refs_1_ = f32[1,128,768]{2,1,0:T(8,128)S(1)} collective-permute-done((f32[1,128,768]{2,1,0:T(8,128)S(1)}, f32[1,128,768]{2,1,0:T(8,128)S(1)}, u32[]{:S(2)}, u32[]{:S(2)}) %collective-permute-start.2) | collective-permute-done | bytes 393248 | tf_op jit(solution)/shard_map/ppermute | solution.py:193
  47.2 11.7 %collective-permute-done.10.refs_2_ = f32[1,128,768]{2,1,0:T(8,128)S(1)} collective-permute-done((f32[1,128,768]{2,1,0:T(8,128)S(1)}, f32[1,128,768]{2,1,0:T(8,128)S(1)}, u32[]{:S(2)}, u32[]{:S(2)}) %collective-permute-start.10) | collective-permute-done | bytes 393248 | tf_op jit(solution)/shard_map/ppermute | solution.py:190
  58.9 0.8 %finish.1 = bf16[1,768,128]{2,1,0:T(8,128)(2,1)} custom-call(f32[1,128,768]{2,1,0:T(8,128)S(1)} %base.1.refs_0_, f32[1,128,768]{2,1,0:T(8,128)S(1)} %collective-permute-done.2.refs_1_, f32[1,128,768]{2,1,0:T(8,128)S(1)} %collective-permute-done.10.refs_2_, f32[1,128,768]{2,1,0:T(8,128)S(1)} %collective-permute-done.14.refs_3_), custom_call_target="tpu_custom_call" | custom-call | tf_op jit(solution)/shard_map/finish/pallas_call | solution.py:173
  (22 shorter events, 0.8 us)
Async XLA Ops:
  0.0 1.9 %copy-start = (bf16[2,1,128,6144]{3,2,1,0:T(8,128)(2,1)S(1)}, bf16[2,1,128,6144]{3,2,1,0:T(8,128)(2,1)}, u32[]{:S(2)}) copy-start(bf16[2,1,128,6144]{3,2,1,0:T(8,128)(2,1)} %refs_0_.23) | copy-start | bytes 9437188
  1.9 0.8 %copy-start.1 = (bf16[2,1,128,128]{3,2,1,0:T(8,128)(2,1)S(1)}, bf16[2,1,128,128]{3,2,1,0:T(8,128)(2,1)}, u32[]{:S(2)}) copy-start(bf16[2,1,128,128]{3,2,1,0:T(8,128)(2,1)} %queries.1) | copy-start | bytes 196612
  2.7 0.8 %copy-start.2 = (bf16[2,1,128,128]{3,2,1,0:T(8,128)(2,1)S(1)}, bf16[2,1,128,128]{3,2,1,0:T(8,128)(2,1)}, u32[]{:S(2)}) copy-start(bf16[2,1,128,128]{3,2,1,0:T(8,128)(2,1)} %keys.1) | copy-start | bytes 196612
  3.6 0.8 %copy-start.3 = (bf16[2,1,128,128]{3,2,1,0:T(8,128)(2,1)S(1)}, bf16[2,1,128,128]{3,2,1,0:T(8,128)(2,1)}, u32[]{:S(2)}) copy-start(bf16[2,1,128,128]{3,2,1,0:T(8,128)(2,1)} %grad_out.1) | copy-start | bytes 196612
  4.4 0.7 %copy-start.4 = (s32[2,1,1,128]{3,2,1,0:T(1,128)S(1)}, s32[2,1,1,128]{3,2,1,0:T(1,128)}, u32[]{:S(2)}) copy-start(s32[2,1,1,128]{3,2,1,0:T(1,128)} %segs.1) | copy-start | bytes 3076
  6.4 2.0 %collective-permute-start.7 = (f32[1,128,768]{2,1,0:T(8,128)S(1)}, f32[1,128,768]{2,1,0:T(8,128)S(1)}, u32[]{:S(2)}, u32[]{:S(2)}) collective-permute-start(f32[1,128,768]{2,1,0:T(8,128)S(1)} %get-tuple-element.18), channel_id=1, source_target_pairs={{0,1},{1,0},{2,3},{3,2},{4,5},{5,4},{6,7},{7,6},{8,9},{9,8},{10,11... | collective-permute-start | bytes 1179656 | tf_op jit(solution)/shard_map/ppermute | solution.py:190
  7.2 5.7 %collective-permute-start.12 = (f32[1,128,768]{2,1,0:T(8,128)S(1)}, f32[1,128,768]{2,1,0:T(8,128)S(1)}, u32[]{:S(2)}, u32[]{:S(2)}) collective-permute-start(f32[1,128,768]{2,1,0:T(8,128)S(1)} %get-tuple-element.20), channel_id=1, source_target_pairs={{0,1},{1,0},{2,3},{3,2},{4,5},{5,4},{6,7},{7,6},{8,9},{9,8},{10,11... | collective-permute-start | bytes 1179656 | tf_op jit(solution)/shard_map/ppermute | solution.py:190
  7.6 6.0 %collective-permute-start.4 = (f32[1,128,768]{2,1,0:T(8,128)S(1)}, f32[1,128,768]{2,1,0:T(8,128)S(1)}, u32[]{:S(2)}, u32[]{:S(2)}) collective-permute-start(f32[1,128,768]{2,1,0:T(8,128)S(1)} %get-tuple-element.17), channel_id=1, source_target_pairs={{0,1},{1,0},{2,3},{3,2},{4,5},{5,4},{6,7},{7,6},{8,9},{9,8},{10,11... | collective-permute-start | bytes 1179656 | tf_op jit(solution)/shard_map/ppermute | solution.py:190
  8.3 5.6 %collective-permute-start.6 = (f32[1,128,768]{2,1,0:T(8,128)S(1)}, f32[1,128,768]{2,1,0:T(8,128)S(1)}, u32[]{:S(2)}, u32[]{:S(2)}) collective-permute-start(f32[1,128,768]{2,1,0:T(8,128)S(1)} %theirs.6), channel_id=1, source_target_pairs={{0,1},{1,0},{2,3},{3,2},{4,5},{5,4},{6,7},{7,6},{8,9},{9,8},{10,11... | collective-permute-start | bytes 1179656 | tf_op jit(solution)/shard_map/ppermute | solution.py:190
  8.6 13.9 %collective-permute-start.8 = (f32[1,128,768]{2,1,0:T(8,128)S(1)}, f32[1,128,768]{2,1,0:T(8,128)S(1)}, u32[]{:S(2)}, u32[]{:S(2)}) collective-permute-start(f32[1,128,768]{2,1,0:T(8,128)S(1)} %upper.6), channel_id=1, source_target_pairs={{0,24},{8,16},{16,8},{24,0},{1,25},{9,17},{17,9},{25,1},{2,26},{10... | collective-permute-start | bytes 1179656 | tf_op jit(solution)/shard_map/ppermute | solution.py:193
  12.8 12.8 %collective-permute-start.1 = (f32[1,128,768]{2,1,0:T(8,128)S(1)}, f32[1,128,768]{2,1,0:T(8,128)S(1)}, u32[]{:S(2)}, u32[]{:S(2)}) collective-permute-start(f32[1,128,768]{2,1,0:T(8,128)S(1)} %get-tuple-element.15), channel_id=1, source_target_pairs={{0,1},{1,0},{2,3},{3,2},{4,5},{5,4},{6,7},{7,6},{8,9},{9,8},{10,11... | collective-permute-start | bytes 1179656 | tf_op jit(solution)/shard_map/ppermute | solution.py:190
  12.9 14.6 %collective-permute-start.11 = (f32[1,128,768]{2,1,0:T(8,128)S(1)}, f32[1,128,768]{2,1,0:T(8,128)S(1)}, u32[]{:S(2)}, u32[]{:S(2)}) collective-permute-start(f32[1,128,768]{2,1,0:T(8,128)S(1)} %get-tuple-element.19), channel_id=1, source_target_pairs={{0,1},{1,0},{2,3},{3,2},{4,5},{5,4},{6,7},{7,6},{8,9},{9,8},{10,11... | collective-permute-start | bytes 1179656 | tf_op jit(solution)/shard_map/ppermute | solution.py:190
  13.6 17.3 %collective-permute-start.13 = (f32[1,128,768]{2,1,0:T(8,128)S(1)}, f32[1,128,768]{2,1,0:T(8,128)S(1)}, u32[]{:S(2)}, u32[]{:S(2)}) collective-permute-start(f32[1,128,768]{2,1,0:T(8,128)S(1)} %upper.7), channel_id=1, source_target_pairs={{0,24},{8,16},{16,8},{24,0},{1,25},{9,17},{17,9},{25,1},{2,26},{10... | collective-permute-start | bytes 1179656 | tf_op jit(solution)/shard_map/ppermute | solution.py:193
  13.9 20.2 %collective-permute-start.3 = (f32[1,128,768]{2,1,0:T(8,128)S(1)}, f32[1,128,768]{2,1,0:T(8,128)S(1)}, u32[]{:S(2)}, u32[]{:S(2)}) collective-permute-start(f32[1,128,768]{2,1,0:T(8,128)S(1)} %get-tuple-element.16), channel_id=1, source_target_pairs={{0,1},{1,0},{2,3},{3,2},{4,5},{5,4},{6,7},{7,6},{8,9},{9,8},{10,11... | collective-permute-start | bytes 1179656 | tf_op jit(solution)/shard_map/ppermute | solution.py:190
  22.5 16.9 %collective-permute-start.5 = (f32[1,128,768]{2,1,0:T(8,128)S(1)}, f32[1,128,768]{2,1,0:T(8,128)S(1)}, u32[]{:S(2)}, u32[]{:S(2)}) collective-permute-start(f32[1,128,768]{2,1,0:T(8,128)S(1)} %upper.5), channel_id=1, source_target_pairs={{0,24},{8,16},{16,8},{24,0},{1,25},{9,17},{17,9},{25,1},{2,26},{10... | collective-permute-start | bytes 1179656 | tf_op jit(solution)/shard_map/ppermute | solution.py:193
  25.7 13.7 %collective-permute-start.9 = (f32[1,128,768]{2,1,0:T(8,128)S(1)}, f32[1,128,768]{2,1,0:T(8,128)S(1)}, u32[]{:S(2)}, u32[]{:S(2)}) collective-permute-start(f32[1,128,768]{2,1,0:T(8,128)S(1)} %lower.3), channel_id=1, source_target_pairs={{0,2},{1,3},{2,0},{3,1},{4,6},{5,7},{6,4},{7,5},{8,10},{9,11},{10,... | collective-permute-start | bytes 1179656 | tf_op jit(solution)/shard_map/ppermute | solution.py:190
  27.5 15.2 %collective-permute-start = (f32[1,128,768]{2,1,0:T(8,128)S(1)}, f32[1,128,768]{2,1,0:T(8,128)S(1)}, u32[]{:S(2)}, u32[]{:S(2)}) collective-permute-start(f32[1,128,768]{2,1,0:T(8,128)S(1)} %get-tuple-element.14), channel_id=1, source_target_pairs={{0,1},{1,0},{2,3},{3,2},{4,5},{5,4},{6,7},{7,6},{8,9},{9,8},{10,11... | collective-permute-start | bytes 1179656 | tf_op jit(solution)/shard_map/ppermute | solution.py:190
  30.9 16.2 %collective-permute-start.2 = (f32[1,128,768]{2,1,0:T(8,128)S(1)}, f32[1,128,768]{2,1,0:T(8,128)S(1)}, u32[]{:S(2)}, u32[]{:S(2)}) collective-permute-start(f32[1,128,768]{2,1,0:T(8,128)S(1)} %upper.4), channel_id=1, source_target_pairs={{0,24},{8,16},{16,8},{24,0},{1,25},{9,17},{17,9},{25,1},{2,26},{10... | collective-permute-start | bytes 1179656 | tf_op jit(solution)/shard_map/ppermute | solution.py:193
  34.1 13.1 %collective-permute-start.14 = (f32[1,128,768]{2,1,0:T(8,128)S(1)}, f32[1,128,768]{2,1,0:T(8,128)S(1)}, u32[]{:S(2)}, u32[]{:S(2)}) collective-permute-start(f32[1,128,768]{2,1,0:T(8,128)S(1)} %lower.5), channel_id=1, source_target_pairs={{0,2},{1,3},{2,0},{3,1},{4,6},{5,7},{6,4},{7,5},{8,10},{9,11},{10,... | collective-permute-start | bytes 1179656 | tf_op jit(solution)/shard_map/ppermute | solution.py:190
  39.6 19.3 %collective-permute-start.10 = (f32[1,128,768]{2,1,0:T(8,128)S(1)}, f32[1,128,768]{2,1,0:T(8,128)S(1)}, u32[]{:S(2)}, u32[]{:S(2)}) collective-permute-start(f32[1,128,768]{2,1,0:T(8,128)S(1)} %lower.4), channel_id=1, source_target_pairs={{0,4},{1,5},{2,6},{3,7},{4,0},{5,1},{6,2},{7,3},{8,12},{9,13},{10,... | collective-permute-start | bytes 1179656 | tf_op jit(solution)/shard_map/ppermute | solution.py:190

commit v3 on v2

--- a/solution.py
+++ b/solution.py
@@ -84,7 +84,7 @@
         ],
         compiler_params=SMALL,
         name="front",
-    )(activations, *small)
+    )(*(pltpu.with_memory_space_constraint(x, pltpu.HBM) for x in (activations, *small)))
 
 
 def plain_blocks(acts, grads, width, plan):

time: 60 us -> 55.6 us (0.927)
  local copies, waits for them, and re-layouts: 5.08 us -> 0.01 us
  Pallas kernels: 4.66 us -> 5.46 us
    unnamed x10 -> x2, local copies, waits for them, and re-layouts: 5.08 us -> 0.01 us
    pallas_call x1, Pallas kernels: 1.34 us -> 2.14 us  [front(): pl.pallas_call(functools.partial(front_kernel, flip, width), out_shape=(j...]
  transfers between devices with their start and end apart: 15 -> 15, of which waited for: 5 -> 5; matrix products, arithmetic and copies ran while one was open for 0% -> 0% of each run, Pallas kernels for 4% -> 5%
where the time goes in v3:
time: 55.6 us; the launch traced here: 55.4 us
  waiting for transfers between devices  31.3 us (56%)
  starting transfers between devices  18.4 us (33%)
  Pallas kernels  5.46 us (10%)
    ppermute x4, waiting for transfers between devices, mirror(): lax.ppermute(block, 'pipe', [(i, slots - 1 - i) for i in range(slots)])  19.6 us
    ppermute x11, waiting for transfers between devices, swap(): return lax.ppermute(block, 'dp', [(i, i ^ distance) for i in range(ways)])  11.7 us
    ppermute x4, starting transfers between devices, mirror(): lax.ppermute(block, 'pipe', [(i, slots - 1 - i) for i in range(slots)])  9.96 us
    ppermute x11, starting transfers between devices, swap(): return lax.ppermute(block, 'dp', [(i, i ^ distance) for i in range(ways)])  8.49 us
    pallas_call x12, Pallas kernels, blocks(): pl.pallas_call(functools.partial(blocks_kernel, tuple(static), len(operan...  2.5 us
    pallas_call x1, Pallas kernels, front(): pl.pallas_call(functools.partial(front_kernel, flip, width), out_shape=(j...  2.14 us
  transfers between devices with their start and end apart: 15, of which 5 were waited for; matrix products, arithmetic and copies ran while one was open for 0% of the time, Pallas kernels for 5%

profile of v3, /device:TPU:0, one launch (start us, length us, event | category | flops | bytes accessed | tf_op | source)
XLA Modules:
  0.0 55.4 jit_solution(6402292688233132794)
XLA Ops:
  0.0 2.1 %front.1 = (bf16[2,128,128]{2,1,0:T(8,128)(2,1)S(1)}, f32[1,128,768]{2,1,0:T(8,128)S(1)}) custom-call(bf16[2,1,128,6144]{3,2,1,0:T(8,128)(2,1)} %refs_0_.23, bf16[2,1,128,128]{3,2,1,0:T(8,128)(2,1)} %queries.1, bf16[2,1,128,128]{3,2,1,0:T(8,128)(2,1)} %keys.1, bf16[2,1,128,128]{3,2,1,0:T(8,128)(2,1)} %grad_out.1, s32[2,1,1,128]{3,2,1,0:T(1,128)} %segs.1), custom_call_target="tpu_custom_call" | custom-call | tf_op jit(solution)/shard_map/front/pallas_call | solution.py:72
  2.1 0.5 collective-permute-start.7
  2.7 0.2 theirs.7
  2.9 0.1 collective-permute-start.12
  3.1 0.2 theirs.5
  3.3 0.5 collective-permute-start.4
  3.8 0.2 theirs.6
  4.0 0.1 collective-permute-start.6
  4.1 0.2 upper.6
  4.3 4.0 %collective-permute-start.8 = (f32[1,128,768]{2,1,0:T(8,128)S(1)}, f32[1,128,768]{2,1,0:T(8,128)S(1)}, u32[]{:S(2)}, u32[]{:S(2)}) collective-permute-start(f32[1,128,768]{2,1,0:T(8,128)S(1)} %upper.6), channel_id=1, source_target_pairs={{0,24},{8,16},{16,8},{24,0},{1,25},{9,17},{17,9},{25,1},{2,26},{10... | collective-permute-start | bytes 1179656 | tf_op jit(solution)/shard_map/ppermute | solution.py:193
  8.3 0.2 theirs.4
  8.6 0.5 collective-permute-start.11
  9.1 0.2 upper.7
  9.3 0.1 collective-permute-start.13
  9.4 0.2 upper.5
  9.7 0.2 collective-permute-start.3
  9.8 8.4 %collective-permute-done.8.refs_3_ = f32[1,128,768]{2,1,0:T(8,128)S(1)} collective-permute-done((f32[1,128,768]{2,1,0:T(8,128)S(1)}, f32[1,128,768]{2,1,0:T(8,128)S(1)}, u32[]{:S(2)}, u32[]{:S(2)}) %collective-permute-start.8) | collective-permute-done | bytes 393248 | tf_op jit(solution)/shard_map/ppermute | solution.py:193
  18.2 3.0 %collective-permute-start.5 = (f32[1,128,768]{2,1,0:T(8,128)S(1)}, f32[1,128,768]{2,1,0:T(8,128)S(1)}, u32[]{:S(2)}, u32[]{:S(2)}) collective-permute-start(f32[1,128,768]{2,1,0:T(8,128)S(1)} %upper.5), channel_id=1, source_target_pairs={{0,24},{8,16},{16,8},{24,0},{1,25},{9,17},{17,9},{25,1},{2,26},{10... | collective-permute-start | bytes 1179656 | tf_op jit(solution)/shard_map/ppermute | solution.py:193
  21.2 0.2 lower.3
  21.4 1.6 %collective-permute-start.9 = (f32[1,128,768]{2,1,0:T(8,128)S(1)}, f32[1,128,768]{2,1,0:T(8,128)S(1)}, u32[]{:S(2)}, u32[]{:S(2)}) collective-permute-start(f32[1,128,768]{2,1,0:T(8,128)S(1)} %lower.3), channel_id=1, source_target_pairs={{0,2},{1,3},{2,0},{3,1},{4,6},{5,7},{6,4},{7,5},{8,10},{9,11},{10,... | collective-permute-start | bytes 1179656 | tf_op jit(solution)/shard_map/ppermute | solution.py:190
  23.0 0.2 upper.4
  23.3 3.3 %collective-permute-done.13.refs_3_ = f32[1,128,768]{2,1,0:T(8,128)S(1)} collective-permute-done((f32[1,128,768]{2,1,0:T(8,128)S(1)}, f32[1,128,768]{2,1,0:T(8,128)S(1)}, u32[]{:S(2)}, u32[]{:S(2)}) %collective-permute-start.13) | collective-permute-done | bytes 393248 | tf_op jit(solution)/shard_map/ppermute | solution.py:193
  26.6 3.0 %collective-permute-start.2 = (f32[1,128,768]{2,1,0:T(8,128)S(1)}, f32[1,128,768]{2,1,0:T(8,128)S(1)}, u32[]{:S(2)}, u32[]{:S(2)}) collective-permute-start(f32[1,128,768]{2,1,0:T(8,128)S(1)} %upper.4), channel_id=1, source_target_pairs={{0,24},{8,16},{16,8},{24,0},{1,25},{9,17},{17,9},{25,1},{2,26},{10... | collective-permute-start | bytes 1179656 | tf_op jit(solution)/shard_map/ppermute | solution.py:193
  29.6 0.2 lower.5
  29.8 1.6 %collective-permute-start.14 = (f32[1,128,768]{2,1,0:T(8,128)S(1)}, f32[1,128,768]{2,1,0:T(8,128)S(1)}, u32[]{:S(2)}, u32[]{:S(2)}) collective-permute-start(f32[1,128,768]{2,1,0:T(8,128)S(1)} %lower.5), channel_id=1, source_target_pairs={{0,2},{1,3},{2,0},{3,1},{4,6},{5,7},{6,4},{7,5},{8,10},{9,11},{10,... | collective-permute-start | bytes 1179656 | tf_op jit(solution)/shard_map/ppermute | solution.py:190
  31.4 3.6 %collective-permute-done.5.refs_3_ = f32[1,128,768]{2,1,0:T(8,128)S(1)} collective-permute-done((f32[1,128,768]{2,1,0:T(8,128)S(1)}, f32[1,128,768]{2,1,0:T(8,128)S(1)}, u32[]{:S(2)}, u32[]{:S(2)}) %collective-permute-start.5) | collective-permute-done | bytes 393248 | tf_op jit(solution)/shard_map/ppermute | solution.py:193
  35.1 0.2 lower.4
  35.3 3.2 %collective-permute-start.10 = (f32[1,128,768]{2,1,0:T(8,128)S(1)}, f32[1,128,768]{2,1,0:T(8,128)S(1)}, u32[]{:S(2)}, u32[]{:S(2)}) collective-permute-start(f32[1,128,768]{2,1,0:T(8,128)S(1)} %lower.4), channel_id=1, source_target_pairs={{0,4},{1,5},{2,6},{3,7},{4,0},{5,1},{6,2},{7,3},{8,12},{9,13},{10,... | collective-permute-start | bytes 1179656 | tf_op jit(solution)/shard_map/ppermute | solution.py:190
  38.5 0.2 base.1.refs_0_
  38.7 4.2 %collective-permute-done.2.refs_1_ = f32[1,128,768]{2,1,0:T(8,128)S(1)} collective-permute-done((f32[1,128,768]{2,1,0:T(8,128)S(1)}, f32[1,128,768]{2,1,0:T(8,128)S(1)}, u32[]{:S(2)}, u32[]{:S(2)}) %collective-permute-start.2) | collective-permute-done | bytes 393248 | tf_op jit(solution)/shard_map/ppermute | solution.py:193
  42.9 11.7 %collective-permute-done.10.refs_2_ = f32[1,128,768]{2,1,0:T(8,128)S(1)} collective-permute-done((f32[1,128,768]{2,1,0:T(8,128)S(1)}, f32[1,128,768]{2,1,0:T(8,128)S(1)}, u32[]{:S(2)}, u32[]{:S(2)}) %collective-permute-start.10) | collective-permute-done | bytes 393248 | tf_op jit(solution)/shard_map/ppermute | solution.py:190
  54.6 0.8 %finish.1 = bf16[1,768,128]{2,1,0:T(8,128)(2,1)} custom-call(f32[1,128,768]{2,1,0:T(8,128)S(1)} %base.1.refs_0_, f32[1,128,768]{2,1,0:T(8,128)S(1)} %collective-permute-done.2.refs_1_, f32[1,128,768]{2,1,0:T(8,128)S(1)} %collective-permute-done.10.refs_2_, f32[1,128,768]{2,1,0:T(8,128)S(1)} %collective-permute-done.14.refs_3_), custom_call_target="tpu_custom_call" | custom-call | tf_op jit(solution)/shard_map/finish/pallas_call | solution.py:173
  (14 shorter events, 0.2 us)
Async XLA Ops:
  0.0 2.7 %copy-start = (bf16[2,1,128,6144]{3,2,1,0:T(8,128)(2,1)S(1)}, bf16[2,1,128,6144]{3,2,1,0:T(8,128)(2,1)}, u32[]{:S(2)}) copy-start(bf16[2,1,128,6144]{3,2,1,0:T(8,128)(2,1)} %refs_0_.23) | copy-start | bytes 9437188
  2.1 2.0 %collective-permute-start.7 = (f32[1,128,768]{2,1,0:T(8,128)S(1)}, f32[1,128,768]{2,1,0:T(8,128)S(1)}, u32[]{:S(2)}, u32[]{:S(2)}) collective-permute-start(f32[1,128,768]{2,1,0:T(8,128)S(1)} %get-tuple-element.18), channel_id=1, source_target_pairs={{0,1},{1,0},{2,3},{3,2},{4,5},{5,4},{6,7},{7,6},{8,9},{9,8},{10,11... | collective-permute-start | bytes 1179656 | tf_op jit(solution)/shard_map/ppermute | solution.py:190
  2.9 5.7 %collective-permute-start.12 = (f32[1,128,768]{2,1,0:T(8,128)S(1)}, f32[1,128,768]{2,1,0:T(8,128)S(1)}, u32[]{:S(2)}, u32[]{:S(2)}) collective-permute-start(f32[1,128,768]{2,1,0:T(8,128)S(1)} %get-tuple-element.20), channel_id=1, source_target_pairs={{0,1},{1,0},{2,3},{3,2},{4,5},{5,4},{6,7},{7,6},{8,9},{9,8},{10,11... | collective-permute-start | bytes 1179656 | tf_op jit(solution)/shard_map/ppermute | solution.py:190
  3.3 6.0 %collective-permute-start.4 = (f32[1,128,768]{2,1,0:T(8,128)S(1)}, f32[1,128,768]{2,1,0:T(8,128)S(1)}, u32[]{:S(2)}, u32[]{:S(2)}) collective-permute-start(f32[1,128,768]{2,1,0:T(8,128)S(1)} %get-tuple-element.17), channel_id=1, source_target_pairs={{0,1},{1,0},{2,3},{3,2},{4,5},{5,4},{6,7},{7,6},{8,9},{9,8},{10,11... | collective-permute-start | bytes 1179656 | tf_op jit(solution)/shard_map/ppermute | solution.py:190
  4.0 5.6 %collective-permute-start.6 = (f32[1,128,768]{2,1,0:T(8,128)S(1)}, f32[1,128,768]{2,1,0:T(8,128)S(1)}, u32[]{:S(2)}, u32[]{:S(2)}) collective-permute-start(f32[1,128,768]{2,1,0:T(8,128)S(1)} %theirs.6), channel_id=1, source_target_pairs={{0,1},{1,0},{2,3},{3,2},{4,5},{5,4},{6,7},{7,6},{8,9},{9,8},{10,11... | collective-permute-start | bytes 1179656 | tf_op jit(solution)/shard_map/ppermute | solution.py:190
  4.3 13.9 %collective-permute-start.8 = (f32[1,128,768]{2,1,0:T(8,128)S(1)}, f32[1,128,768]{2,1,0:T(8,128)S(1)}, u32[]{:S(2)}, u32[]{:S(2)}) collective-permute-start(f32[1,128,768]{2,1,0:T(8,128)S(1)} %upper.6), channel_id=1, source_target_pairs={{0,24},{8,16},{16,8},{24,0},{1,25},{9,17},{17,9},{25,1},{2,26},{10... | collective-permute-start | bytes 1179656 | tf_op jit(solution)/shard_map/ppermute | solution.py:193
  8.6 12.8 %collective-permute-start.1 = (f32[1,128,768]{2,1,0:T(8,128)S(1)}, f32[1,128,768]{2,1,0:T(8,128)S(1)}, u32[]{:S(2)}, u32[]{:S(2)}) collective-permute-start(f32[1,128,768]{2,1,0:T(8,128)S(1)} %get-tuple-element.15), channel_id=1, source_target_pairs={{0,1},{1,0},{2,3},{3,2},{4,5},{5,4},{6,7},{7,6},{8,9},{9,8},{10,11... | collective-permute-start | bytes 1179656 | tf_op jit(solution)/shard_map/ppermute | solution.py:190
  8.6 14.6 %collective-permute-start.11 = (f32[1,128,768]{2,1,0:T(8,128)S(1)}, f32[1,128,768]{2,1,0:T(8,128)S(1)}, u32[]{:S(2)}, u32[]{:S(2)}) collective-permute-start(f32[1,128,768]{2,1,0:T(8,128)S(1)} %get-tuple-element.19), channel_id=1, source_target_pairs={{0,1},{1,0},{2,3},{3,2},{4,5},{5,4},{6,7},{7,6},{8,9},{9,8},{10,11... | collective-permute-start | bytes 1179656 | tf_op jit(solution)/shard_map/ppermute | solution.py:190
  9.3 17.3 %collective-permute-start.13 = (f32[1,128,768]{2,1,0:T(8,128)S(1)}, f32[1,128,768]{2,1,0:T(8,128)S(1)}, u32[]{:S(2)}, u32[]{:S(2)}) collective-permute-start(f32[1,128,768]{2,1,0:T(8,128)S(1)} %upper.7), channel_id=1, source_target_pairs={{0,24},{8,16},{16,8},{24,0},{1,25},{9,17},{17,9},{25,1},{2,26},{10... | collective-permute-start | bytes 1179656 | tf_op jit(solution)/shard_map/ppermute | solution.py:193
  9.7 20.2 %collective-permute-start.3 = (f32[1,128,768]{2,1,0:T(8,128)S(1)}, f32[1,128,768]{2,1,0:T(8,128)S(1)}, u32[]{:S(2)}, u32[]{:S(2)}) collective-permute-start(f32[1,128,768]{2,1,0:T(8,128)S(1)} %get-tuple-element.16), channel_id=1, source_target_pairs={{0,1},{1,0},{2,3},{3,2},{4,5},{5,4},{6,7},{7,6},{8,9},{9,8},{10,11... | collective-permute-start | bytes 1179656 | tf_op jit(solution)/shard_map/ppermute | solution.py:190
  18.2 16.9 %collective-permute-start.5 = (f32[1,128,768]{2,1,0:T(8,128)S(1)}, f32[1,128,768]{2,1,0:T(8,128)S(1)}, u32[]{:S(2)}, u32[]{:S(2)}) collective-permute-start(f32[1,128,768]{2,1,0:T(8,128)S(1)} %upper.5), channel_id=1, source_target_pairs={{0,24},{8,16},{16,8},{24,0},{1,25},{9,17},{17,9},{25,1},{2,26},{10... | collective-permute-start | bytes 1179656 | tf_op jit(solution)/shard_map/ppermute | solution.py:193
  21.4 13.7 %collective-permute-start.9 = (f32[1,128,768]{2,1,0:T(8,128)S(1)}, f32[1,128,768]{2,1,0:T(8,128)S(1)}, u32[]{:S(2)}, u32[]{:S(2)}) collective-permute-start(f32[1,128,768]{2,1,0:T(8,128)S(1)} %lower.3), channel_id=1, source_target_pairs={{0,2},{1,3},{2,0},{3,1},{4,6},{5,7},{6,4},{7,5},{8,10},{9,11},{10,... | collective-permute-start | bytes 1179656 | tf_op jit(solution)/shard_map/ppermute | solution.py:190
  23.2 15.2 %collective-permute-start = (f32[1,128,768]{2,1,0:T(8,128)S(1)}, f32[1,128,768]{2,1,0:T(8,128)S(1)}, u32[]{:S(2)}, u32[]{:S(2)}) collective-permute-start(f32[1,128,768]{2,1,0:T(8,128)S(1)} %get-tuple-element.14), channel_id=1, source_target_pairs={{0,1},{1,0},{2,3},{3,2},{4,5},{5,4},{6,7},{7,6},{8,9},{9,8},{10,11... | collective-permute-start | bytes 1179656 | tf_op jit(solution)/shard_map/ppermute | solution.py:190
  26.6 16.2 %collective-permute-start.2 = (f32[1,128,768]{2,1,0:T(8,128)S(1)}, f32[1,128,768]{2,1,0:T(8,128)S(1)}, u32[]{:S(2)}, u32[]{:S(2)}) collective-permute-start(f32[1,128,768]{2,1,0:T(8,128)S(1)} %upper.4), channel_id=1, source_target_pairs={{0,24},{8,16},{16,8},{24,0},{1,25},{9,17},{17,9},{25,1},{2,26},{10... | collective-permute-start | bytes 1179656 | tf_op jit(solution)/shard_map/ppermute | solution.py:193
  29.8 13.1 %collective-permute-start.14 = (f32[1,128,768]{2,1,0:T(8,128)S(1)}, f32[1,128,768]{2,1,0:T(8,128)S(1)}, u32[]{:S(2)}, u32[]{:S(2)}) collective-permute-start(f32[1,128,768]{2,1,0:T(8,128)S(1)} %lower.5), channel_id=1, source_target_pairs={{0,2},{1,3},{2,0},{3,1},{4,6},{5,7},{6,4},{7,5},{8,10},{9,11},{10,... | collective-permute-start | bytes 1179656 | tf_op jit(solution)/shard_map/ppermute | solution.py:190
  35.3 19.3 %collective-permute-start.10 = (f32[1,128,768]{2,1,0:T(8,128)S(1)}, f32[1,128,768]{2,1,0:T(8,128)S(1)}, u32[]{:S(2)}, u32[]{:S(2)}) collective-permute-start(f32[1,128,768]{2,1,0:T(8,128)S(1)} %lower.4), channel_id=1, source_target_pairs={{0,4},{1,5},{2,6},{3,7},{4,0},{5,1},{6,2},{7,3},{8,12},{9,13},{10,... | collective-permute-start | bytes 1179656 | tf_op jit(solution)/shard_map/ppermute | solution.py:190

commit v4 on v3

v4 whole, which is shorter than its diff:
```python
import functools

import jax
import jax.numpy as jnp
from jax import lax
from jax.experimental import pallas as pl
from jax.experimental.pallas import tpu as pltpu
from jax.sharding import PartitionSpec as P

VMEM = pl.BlockSpec(memory_space=pltpu.VMEM)
SOON = pl.CostEstimate(flops=25_000_000_000, bytes_accessed=1000, transcendentals=0)
SMALL = pltpu.CompilerParams(vmem_limit_bytes=8 << 20)


def grad_v_columns(query_rows, key_rows, grad_rows, segs):
    length, head = query_rows.shape
    scores = lax.dot_general(
        query_rows, key_rows, (((1,), (1,)), ((), ())), preferred_element_type=jnp.float32
    ) / jnp.sqrt(jnp.float32(head))
    shape = (length, length)
    across = jnp.broadcast_to(segs, shape)
    keep = (across == across.T) & (
        lax.broadcasted_iota(jnp.int32, shape, 1) <= lax.broadcasted_iota(jnp.int32, shape, 0)
    )
    masked = jnp.where(keep, scores, jnp.float32(-1e30))
    top = jnp.max(masked, axis=1, keepdims=True)
    weights = jnp.where(keep, jnp.exp(masked - top), jnp.float32(0.0))
    probs = (weights / jnp.sum(weights, axis=1, keepdims=True)).astype(jnp.bfloat16)
    return lax.dot_general(
        grad_rows, probs, (((0,), (0,)), ((), ())), preferred_element_type=jnp.float32
    ).astype(jnp.bfloat16)


def block_columns(flip, width):
    owner = lax.axis_index("dp") ^ flip
    return pl.ds(pl.multiple_of(owner * width, 128), width)


def front_kernel(flip, width, acts, queries, keys, grad_out, segs, grads, first, *scratch):
    columns, ready = scratch[0], scratch[-1]
    sources = [queries, keys, grad_out, segs, acts.at[:, 0, :, block_columns(flip, width)]]
    holders = [*scratch[1:-1], columns]
    copies = [
        pltpu.make_async_copy(source, holder, ready.at[i])
        for i, (source, holder) in enumerate(zip(sources, holders))
    ]
    for copy in copies:
        copy.start()
    for copy in copies[:-1]:
        copy.wait()
    query_rows, key_rows, grad_rows, seg_rows = scratch[1:-1]
    for half in (1, 0):
        grads[half] = grad_v_columns(
            query_rows[half, 0], key_rows[half, 0], grad_rows[half, 0], seg_rows[half, 0]
        )
    copies[-1].wait()
    for slab in range(2):
        first[slab] = jnp.dot(grads[1 - slab], columns[1 - slab], preferred_element_type=jnp.float32)


def front(activations, queries, keys, grad_out, segment_ids, flip, width):
    head, length = queries.shape[3], queries.shape[2]
    if width % 128:
        grads = jnp.stack(
            [
                grad_v_columns(queries[h, 0], keys[h, 0], grad_out[h, 0], segment_ids[h, 0])
                for h in range(2)
            ]
        )
        return grads, *plain_blocks(
            activations,
            grads,
            width,
            [[(slab, 0, head, [(DOT, 1 - slab, flip, 0)]) for slab in range(2)]],
        )
    small = (queries, keys, grad_out, segment_ids)
    return pl.pallas_call(
        functools.partial(front_kernel, flip, width),
        out_shape=(
            jax.ShapeDtypeStruct((2, head, length), jnp.bfloat16),
            jax.ShapeDtypeStruct((2, head, width), jnp.float32),
        ),
        in_specs=[pl.BlockSpec(memory_space=pltpu.HBM)] * 5,
        out_specs=(VMEM, VMEM),
        scratch_shapes=[
            pltpu.VMEM((2, length, width), activations.dtype),
            *(pltpu.VMEM(value.shape, value.dtype) for value in small),
            pltpu.SemaphoreType.DMA((5,)),
        ],
        compiler_params=SMALL,
        cost_estimate=SOON,
        name="front",
    )(*(pltpu.with_memory_space_constraint(x, pltpu.HBM) for x in (activations, *small)))


def extent(segments):
    slabs = max(slab for slab, _, _, _ in segments) + 1
    return slabs, max(low + rows for _, low, rows, _ in segments)


def plain_blocks(acts, grads, width, plan):
    outs = []
    for segments in plan:
        out = jnp.zeros((*extent(segments), width), jnp.float32)
        for slab, low, rows, terms in segments:
            value = None
            for term in terms:
                if term[0] is DOT:
                    _, half, flip, head_low = term
                    owner = lax.axis_index("dp") ^ flip
                    columns = lax.dynamic_slice_in_dim(acts[half, 0], owner * width, width, axis=1)
                    term = jnp.dot(
                        grads[half, head_low : head_low + rows],
                        columns,
                        preferred_element_type=jnp.float32,
                    )
                else:
                    array, place, first = term
                    term = array[place, first : first + rows]
                value = term if value is None else value + term
            out = out.at[slab, low : low + rows].set(value)
        outs.append(out)
    return tuple(outs)


def blocks_kernel(plan, count, width, *refs):
    acts, grads = refs[0], refs[1]
    refs[-1][...] = jnp.zeros_like(refs[-1])
    for out, segments in zip(refs[count:-1], plan):
        for slab, low, rows, terms in segments:
            value = None
            for term in terms:
                if term[0] is DOT:
                    _, half, flip, head_low = term
                    term = jnp.dot(
                        grads[half, head_low : head_low + rows, :],
                        acts[half, 0, :, block_columns(flip, width)],
                        preferred_element_type=jnp.float32,
                    )
                else:
                    operand, place, first = term
                    term = refs[operand][place, first : first + rows, :]
                value = term if value is None else value + term
            out[slab, low : low + rows, :] = value


def number_operands(plan, operands):
    numbers = {}

    def numbered(term):
        if term[0] is DOT:
            return term
        if id(term[0]) not in numbers:
            numbers[id(term[0])] = len(operands)
            operands.append(term[0])
        return (numbers[id(term[0])], *term[1:])

    return [
        [(slab, low, rows, [numbered(term) for term in terms]) for slab, low, rows, terms in segments]
        for segments in plan
    ]


def blocks(name, acts, grads, width, plan, token):
    if width % 128:
        return *plain_blocks(acts, grads, width, plan), None
    operands = [acts, grads]
    static = number_operands(plan, operands)
    if token is not None:
        operands.append(token)
    shapes = [(*extent(segments), width) for segments in static] + [(8, 128)]
    return pl.pallas_call(
        functools.partial(blocks_kernel, static, len(operands), width),
        out_shape=tuple(jax.ShapeDtypeStruct(shape, jnp.float32) for shape in shapes),
        in_specs=[VMEM] * len(operands),
        out_specs=(VMEM,) * len(shapes),
        compiler_params=SMALL,
        cost_estimate=SOON,
        name=name,
    )(*operands)


DOT = object()


def finish_kernel(segments, count, *refs):
    out = refs[count]
    for left in range(0, out.shape[1], 128):
        rows_of = []
        for _, _, rows, terms in segments:
            value = None
            for operand, place, first in terms:
                term = refs[operand][place, first : first + rows, left : left + 128]
                value = term if value is None else value + term
            rows_of.append(value)
        value = jnp.concatenate(rows_of, axis=0) if len(rows_of) > 1 else rows_of[0]
        out[0, left : left + 128, :] = value.T.astype(out.dtype)


def finish(segments, head, width):
    if width % 128:
        (value,) = plain_blocks(None, None, width, [segments])
        return value.swapaxes(1, 2).astype(jnp.bfloat16)
    operands = []
    (static,) = number_operands([segments], operands)
    return pl.pallas_call(
        functools.partial(finish_kernel, static, len(operands)),
        out_shape=jax.ShapeDtypeStruct((1, width, head), jnp.bfloat16),
        in_specs=[VMEM] * len(operands),
        out_specs=VMEM,
        compiler_params=SMALL,
        cost_estimate=SOON,
        name="finish",
    )(*operands)


class Section:
    def __init__(self, half, chips):
        self.half = half
        self.dots = [True] * chips
        self.given = [[] for _ in range(chips)]

    def add(self, block, low, high, array, slab=0):
        self.given[block].append((low, high, array, slab, low))

    def settle(self, block, low, high, array, slab=0):
        kept = []
        for first, last, other, place, top in self.given[block]:
            for start, stop in ((first, min(last, low)), (max(first, high), last)):
                if start < stop:
                    kept.append((start, stop, other, place, top))
        self.given[block] = kept
        self.add(block, low, high, array, slab)

    def segments(self, block, low, high, slab=0):
        edges = {low, high}
        for start, stop, *_ in self.given[block]:
            edges |= {start, stop}
        edges = sorted(edge for edge in edges if low <= edge <= high)
        made = []
        for start, stop in zip(edges, edges[1:]):
            terms = [(DOT, self.half, 2 * block, start)] if self.dots[block] else []
            terms += [
                (array, place, start - top)
                for first, last, array, place, top in self.given[block]
                if first <= start and stop <= last
            ]
            made.append((slab, start - low, stop - start, terms))
        return made


def order(chips, head):
    last = chips - 1
    cut, half = head * 5 // 8, head // 2
    pairs = [(1, block) for block in reversed(range(last))]
    pairs += [(0, block) for block in reversed(range(last))]
    everything = list(reversed(range(chips)))
    if chips < 4:
        events = [("core", *pairs)] if pairs else []
        events += [("up", block, 0, head) for block in everything] + [("base", *everything)]
        return events + [("down", block, 0, head) for block in everything[:-1]]
    events = [
        ("core", *pairs),
        ("up", last, 0, cut),
        ("raw", last, cut, head),
        ("up", last - 1, 0, cut),
        ("up", 1, 0, half),
        ("base", *everything),
        ("down", last, 0, cut),
        ("up", last - 1, cut, head),
    ]
    for block in reversed(range(2, last - 1)):
        events += [("up", block, 0, head), ("down", block + 1, 0, head)]
    return [
        *events,
        ("up", 1, half, head),
        ("down", 1, 0, half),
        ("down", 2, 0, head),
        ("up", 0, 0, head),
        ("down", 1, half, head),
    ]


def body(activations, queries, keys, grad_out, segment_ids):
    ways = lax.axis_size("dp")
    slots = lax.axis_size("pipe")
    chips = ways // 2
    head = queries.shape[3]
    width = activations.shape[3] // ways
    last = chips - 1

    def swap(block, distance):
        return lax.ppermute(block, "dp", [(i, i ^ distance) for i in range(ways)])

    def mirror(block):
        return lax.ppermute(block, "pipe", [(i, slots - 1 - i) for i in range(slots)])

    grads, first = front(
        activations, queries, keys, grad_out, segment_ids, 2 * last + 1, width
    )
    lower, upper = Section(0, chips), Section(1, chips)
    got = swap(first, 1)
    for section in (upper, lower):
        section.add(last, 0, head, got, 1 - section.half)
    token = None

    def make(name, plan):
        nonlocal token
        *made, token = blocks(name, activations, grads, width, plan, token)
        return made

    def exchange(wanted):
        plan = [
            (slab, 0, head, [(DOT, section.half, 2 * block + 1, 0)])
            for slab, (section, block) in enumerate(wanted)
        ]
        got = swap(make("theirs", [plan])[0], 1)
        for slab, (section, block) in enumerate(wanted):
            section.add(block, 0, head, got, slab)

    def send_up(block, low, high):
        (part,) = make("upper", [upper.segments(block, low, high)])
        return mirror(part)

    def send_raw(block, low, high):
        rows = (block, low, high)
        (both,) = make("raw", [upper.segments(*rows, 0) + lower.segments(*rows, 1)])
        bit = block & -block
        got = swap(both, 2 * bit)
        upper.add(block ^ bit, low, high, got, 0)
        lower.add(block ^ bit, low, high, got, 1)

    def send_down(block, low, high):
        (part,) = make("lower", [lower.segments(block, low, high)])
        bit = block & -block
        lower.add(block ^ bit, low, high, swap(part, 2 * bit))

    def settle(blocks_of):
        sums = make("base", [lower.segments(block, 0, head) for block in blocks_of])
        for block, array in zip(blocks_of, sums):
            lower.dots[block] = False
            lower.settle(block, 0, head, array)

    def take(block, low, high):
        (part,) = make("take", [lower.segments(block, low, high)])
        lower.settle(block, low, high, part)

    late = {}

    def arrive(block, low, high):
        for rows in [rows for rows in late if rows[0] == block]:
            if low <= rows[1] and rows[2] <= high:
                lower.add(*rows, late.pop(rows))

    for event, *what in order(chips, head):
        if event == "core":
            exchange([(upper if half else lower, block) for half, block in what])
        elif event == "base":
            settle(what)
        elif event == "up":
            late[tuple(what)] = send_up(*what)
        elif event == "raw":
            send_raw(*what)
        elif event == "down":
            arrive(*what)
            send_down(*what)
        elif event == "take":
            arrive(*what)
            take(*what)
    arrive(0, 0, head)
    assert not late
    return finish(lower.segments(0, 0, head), head, width)


def solution(mesh):
    spec = P(None, "pipe", "dp", None)
    return jax.shard_map(
        body,
        mesh=mesh,
        in_specs=(spec,) * 5,
        out_specs=P("pipe", "dp", None),
        check_vma=False,
    )
```

time: 55.6 us -> 48.6 us (0.87)
  waiting for transfers between devices: 31.3 us -> 20.3 us
  starting transfers between devices: 18.4 us -> 22.3 us
    ppermute x4 -> x6, waiting for transfers between devices: 19.6 us -> 7.13 us  [mirror(): lax.ppermute(block, 'pipe', [(i, slots - 1 - i) for i in range(slots)])]
    ppermute x4 -> x6, starting transfers between devices: 9.96 us -> 12.3 us  [mirror(): lax.ppermute(block, 'pipe', [(i, slots - 1 - i) for i in range(slots)])]
    ppermute x11 -> x7, starting transfers between devices: 8.49 us -> 9.99 us  [swap(): return lax.ppermute(block, 'dp', [(i, i ^ distance) for i in range(ways)])]
    ppermute x11 -> x7, waiting for transfers between devices: 11.7 us -> 13.1 us  [swap(): return lax.ppermute(block, 'dp', [(i, i ^ distance) for i in range(ways)])]
    pallas_call x13 -> x14, Pallas kernels: 3.32 us -> 3.68 us  [the longest x13 2.83 us: blocks(): pl.pallas_call(functools.partial(blocks_kernel, static, len(operands), wi...]
  transfers between devices with their start and end apart: 15 -> 13, of which waited for: 5 -> 5; matrix products, arithmetic and copies ran while one was open for 0% -> 0% of each run, Pallas kernels for 5% -> 6%
where the time goes in v4:
time: 48.6 us; the launch traced here: 48.5 us
  starting transfers between devices  22.3 us (46%)
  waiting for transfers between devices  20.3 us (42%)
  Pallas kernels  5.86 us (12%)
    ppermute x7, waiting for transfers between devices, swap(): return lax.ppermute(block, 'dp', [(i, i ^ distance) for i in range(ways)])  13.1 us
    ppermute x6, starting transfers between devices, mirror(): lax.ppermute(block, 'pipe', [(i, slots - 1 - i) for i in range(slots)])  12.3 us
    ppermute x7, starting transfers between devices, swap(): return lax.ppermute(block, 'dp', [(i, i ^ distance) for i in range(ways)])  9.99 us
    ppermute x6, waiting for transfers between devices, mirror(): lax.ppermute(block, 'pipe', [(i, slots - 1 - i) for i in range(slots)])  7.13 us
    pallas_call x13, Pallas kernels, blocks(): pl.pallas_call(functools.partial(blocks_kernel, static, len(operands), wi...  2.83 us
    pallas_call x1, Pallas kernels, front(): pl.pallas_call(functools.partial(front_kernel, flip, width), out_shape=(j...  2.18 us
  transfers between devices with their start and end apart: 13, of which 5 were waited for; matrix products, arithmetic and copies ran while one was open for 0% of the time, Pallas kernels for 6%

profile of v4, /device:TPU:0, one launch (start us, length us, event | category | flops | bytes accessed | tf_op | source)
XLA Modules:
  0.0 48.5 jit_solution(8114207822263796529)
XLA Ops:
  0.0 2.2 %front.1 = (bf16[2,128,128]{2,1,0:T(8,128)(2,1)S(1)}, f32[2,128,768]{2,1,0:T(8,128)S(1)}) custom-call(bf16[2,1,128,6144]{3,2,1,0:T(8,128)(2,1)} %refs_0_.25, bf16[2,1,128,128]{3,2,1,0:T(8,128)(2,1)} %queries.1, bf16[2,1,128,128]{3,2,1,0:T(8,128)(2,1)} %keys.1, bf16[2,1,128,128]{3,2,1,0:T(8,128)(2,1)} %grad_out.1, s32[2,1,1,128]{3,2,1,0:T(1,128)} %segs.1), custom_call_target="tpu_custom_call" | custom-call | flops 24999999488 | bytes 1000 | tf_op jit(solution)/shard_map/front/pallas_call | solution.py:77
  2.2 0.5 %collective-permute-start = (f32[2,128,768]{2,1,0:T(8,128)S(1)}, f32[2,128,768]{2,1,0:T(8,128)S(1)}, u32[]{:S(2)}, u32[]{:S(2)}) collective-permute-start(f32[2,128,768]{2,1,0:T(8,128)S(1)} %get-tuple-element.36), channel_id=1, source_target_pairs={{0,1},{1,0},{2,3},{3,2},{4,5},{5,4},{6,7},{7,6},{8,9},{9,8},{10,11... | collective-permute-start | bytes 2359304 | tf_op jit(solution)/shard_map/ppermute | solution.py:293
  2.7 0.5 theirs.1
  3.2 0.1 collective-permute-start.1
  3.3 1.3 %collective-permute-done.refs_2_ = f32[2,128,768]{2,1,0:T(8,128)S(1)} collective-permute-done((f32[2,128,768]{2,1,0:T(8,128)S(1)}, f32[2,128,768]{2,1,0:T(8,128)S(1)}, u32[]{:S(2)}, u32[]{:S(2)}) %collective-permute-start) | collective-permute-done | bytes 786464 | tf_op jit(solution)/shard_map/ppermute | solution.py:293
  4.6 0.2 upper.6
  4.8 0.2 raw.1
  5.0 3.0 %collective-permute-start.2 = (f32[2,48,768]{2,1,0:T(8,128)S(1)}, f32[2,48,768]{2,1,0:T(8,128)S(1)}, u32[]{:S(2)}, u32[]{:S(2)}) collective-permute-start(f32[2,48,768]{2,1,0:T(8,128)S(1)} %get-tuple-element.40), channel_id=1, source_target_pairs={{0,2},{1,3},{2,0},{3,1},{4,6},{5,7},{6,4},{7,5},{8,10},{9,11},{10,... | collective-permute-start | bytes 884744 | tf_op jit(solution)/shard_map/ppermute | solution.py:293
  8.0 2.4 %collective-permute-start.4 = (f32[1,80,768]{2,1,0:T(8,128)S(1)}, f32[1,80,768]{2,1,0:T(8,128)S(1)}, u32[]{:S(2)}, u32[]{:S(2)}) collective-permute-start(f32[1,80,768]{2,1,0:T(8,128)S(1)} %get-tuple-element.48), channel_id=1, source_target_pairs={{0,24},{8,16},{16,8},{24,0},{1,25},{9,17},{17,9},{25,1},{2,26},{10... | collective-permute-start | bytes 737288 | tf_op jit(solution)/shard_map/ppermute | solution.py:296
  10.5 0.0 collective-permute-done.1.refs_2_.refs_3_
  10.5 0.2 upper.7
  10.6 0.2 upper.8
  10.8 1.4 %collective-permute-start.3 = (f32[1,64,768]{2,1,0:T(8,128)S(1)}, f32[1,64,768]{2,1,0:T(8,128)S(1)}, u32[]{:S(2)}, u32[]{:S(2)}) collective-permute-start(f32[1,64,768]{2,1,0:T(8,128)S(1)} %get-tuple-element.46), channel_id=1, source_target_pairs={{0,24},{8,16},{16,8},{24,0},{1,25},{9,17},{17,9},{25,1},{2,26},{10... | collective-permute-start | bytes 589832 | tf_op jit(solution)/shard_map/ppermute | solution.py:296
  12.2 3.1 %collective-permute-done.2.refs_4_.refs_3_ = f32[2,48,768]{2,1,0:T(8,128)S(1)} collective-permute-done((f32[2,48,768]{2,1,0:T(8,128)S(1)}, f32[2,48,768]{2,1,0:T(8,128)S(1)}, u32[]{:S(2)}, u32[]{:S(2)}) %collective-permute-start.2) | collective-permute-done | bytes 294944 | tf_op jit(solution)/shard_map/ppermute | solution.py:293
  15.3 0.4 base.1
  15.7 2.0 %collective-permute-done.4.refs_3_ = f32[1,80,768]{2,1,0:T(8,128)S(1)} collective-permute-done((f32[1,80,768]{2,1,0:T(8,128)S(1)}, f32[1,80,768]{2,1,0:T(8,128)S(1)}, u32[]{:S(2)}, u32[]{:S(2)}) %collective-permute-start.4) | collective-permute-done | bytes 245792 | tf_op jit(solution)/shard_map/ppermute | solution.py:296
  17.8 0.1 collective-permute-start.6
  17.9 2.9 %collective-permute-start.7 = (f32[1,80,768]{2,1,0:T(8,128)S(1)}, f32[1,80,768]{2,1,0:T(8,128)S(1)}, u32[]{:S(2)}, u32[]{:S(2)}) collective-permute-start(f32[1,80,768]{2,1,0:T(8,128)S(1)} %get-tuple-element.56), channel_id=1, source_target_pairs={{0,24},{8,16},{16,8},{24,0},{1,25},{9,17},{17,9},{25,1},{2,26},{10... | collective-permute-start | bytes 737288 | tf_op jit(solution)/shard_map/ppermute | solution.py:296
  20.8 0.2 upper.9
  20.9 0.2 collective-permute-start.8
  21.1 0.2 upper.10
  21.3 2.9 %collective-permute-start.11 = (f32[1,64,768]{2,1,0:T(8,128)S(1)}, f32[1,64,768]{2,1,0:T(8,128)S(1)}, u32[]{:S(2)}, u32[]{:S(2)}) collective-permute-start(f32[1,64,768]{2,1,0:T(8,128)S(1)} %get-tuple-element.62), channel_id=1, source_target_pairs={{0,24},{8,16},{16,8},{24,0},{1,25},{9,17},{17,9},{25,1},{2,26},{10... | collective-permute-start | bytes 589832 | tf_op jit(solution)/shard_map/ppermute | solution.py:296
  24.2 1.6 %collective-permute-start.5 = (f32[1,64,768]{2,1,0:T(8,128)S(1)}, f32[1,64,768]{2,1,0:T(8,128)S(1)}, u32[]{:S(2)}, u32[]{:S(2)}) collective-permute-start(f32[1,64,768]{2,1,0:T(8,128)S(1)} %get-tuple-element.53), channel_id=1, source_target_pairs={{0,2},{1,3},{2,0},{3,1},{4,6},{5,7},{6,4},{7,5},{8,10},{9,11},{10,... | collective-permute-start | bytes 589832 | tf_op jit(solution)/shard_map/ppermute | solution.py:293
  25.8 5.1 %collective-permute-done.8.refs_5_ = f32[1,48,768]{2,1,0:T(8,128)S(1)} collective-permute-done((f32[1,48,768]{2,1,0:T(8,128)S(1)}, f32[1,48,768]{2,1,0:T(8,128)S(1)}, u32[]{:S(2)}, u32[]{:S(2)}) %collective-permute-start.8) | collective-permute-done | bytes 147488 | tf_op jit(solution)/shard_map/ppermute | solution.py:296
  30.9 0.1 lower.6
  31.0 3.0 %collective-permute-start.9 = (f32[1,128,768]{2,1,0:T(8,128)S(1)}, f32[1,128,768]{2,1,0:T(8,128)S(1)}, u32[]{:S(2)}, u32[]{:S(2)}) collective-permute-start(f32[1,128,768]{2,1,0:T(8,128)S(1)} %get-tuple-element.59), channel_id=1, source_target_pairs={{0,4},{1,5},{2,6},{3,7},{4,0},{5,1},{6,2},{7,3},{8,12},{9,13},{10,... | collective-permute-start | bytes 1179656 | tf_op jit(solution)/shard_map/ppermute | solution.py:293
  34.0 0.2 upper.11
  34.2 2.5 %collective-permute-start.10 = (f32[1,128,768]{2,1,0:T(8,128)S(1)}, f32[1,128,768]{2,1,0:T(8,128)S(1)}, u32[]{:S(2)}, u32[]{:S(2)}) collective-permute-start(f32[1,128,768]{2,1,0:T(8,128)S(1)} %get-tuple-element.61), channel_id=1, source_target_pairs={{0,24},{8,16},{16,8},{24,0},{1,25},{9,17},{17,9},{25,1},{2,26},{10... | collective-permute-start | bytes 1179656 | tf_op jit(solution)/shard_map/ppermute | solution.py:296
  36.7 0.6 %lower.7 = (f32[1,64,768]{2,1,0:T(8,128)S(1)}, f32[8,128]{1,0:T(8,128)}) custom-call(bf16[2,1,128,6144]{3,2,1,0:T(8,128)(2,1)S(1)} %copy-done, bf16[2,128,128]{2,1,0:T(8,128)(2,1)S(1)} %get-tuple-element.35.refs_1_, f32[1,128,768]{2,1,0:T(8,128)S(1)} %get-tuple-element.45.refs_2_, f32[1,64,768]{2,1,0:T(8,128)S(1)} %collective-permute-done.11.refs_3_, ...), custom_call_target="tpu_custom_call" | custom-call | flops 24999999488 | bytes 1000 | tf_op jit(solution)/shard_map/lower/pallas_call | solution.py:172
  37.3 1.6 %collective-permute-start.12 = (f32[1,64,768]{2,1,0:T(8,128)S(1)}, f32[1,64,768]{2,1,0:T(8,128)S(1)}, u32[]{:S(2)}, u32[]{:S(2)}) collective-permute-start(f32[1,64,768]{2,1,0:T(8,128)S(1)} %get-tuple-element.64), channel_id=1, source_target_pairs={{0,2},{1,3},{2,0},{3,1},{4,6},{5,7},{6,4},{7,5},{8,10},{9,11},{10,... | collective-permute-start | bytes 589832 | tf_op jit(solution)/shard_map/ppermute | solution.py:293
  38.9 8.7 %collective-permute-done.12.refs_4_ = f32[1,64,768]{2,1,0:T(8,128)S(1)} collective-permute-done((f32[1,64,768]{2,1,0:T(8,128)S(1)}, f32[1,64,768]{2,1,0:T(8,128)S(1)}, u32[]{:S(2)}, u32[]{:S(2)}) %collective-permute-start.12) | collective-permute-done | bytes 196640 | tf_op jit(solution)/shard_map/ppermute | solution.py:293
  47.6 0.8 %finish.1 = bf16[1,768,128]{2,1,0:T(8,128)(2,1)} custom-call(f32[1,128,768]{2,1,0:T(8,128)S(1)} %get-tuple-element.44.refs_0_, f32[1,64,768]{2,1,0:T(8,128)S(1)} %collective-permute-done.5.refs_1_, f32[1,128,768]{2,1,0:T(8,128)S(1)} %collective-permute-done.9.refs_2_, f32[1,128,768]{2,1,0:T(8,128)S(1)} %collective-permute-done.10.refs_3_, ...), custom_call_target="tpu_custom_call" | custom-call | flops 24999999488 | bytes 1000 | tf_op jit(solution)/shard_map/finish/pallas_call | solution.py:206
  (11 shorter events, 0.1 us)
Async XLA Ops:
  0.0 2.7 %copy-start = (bf16[2,1,128,6144]{3,2,1,0:T(8,128)(2,1)S(1)}, bf16[2,1,128,6144]{3,2,1,0:T(8,128)(2,1)}, u32[]{:S(2)}) copy-start(bf16[2,1,128,6144]{3,2,1,0:T(8,128)(2,1)} %refs_0_.25) | copy-start | bytes 9437188
  2.2 2.4 %collective-permute-start = (f32[2,128,768]{2,1,0:T(8,128)S(1)}, f32[2,128,768]{2,1,0:T(8,128)S(1)}, u32[]{:S(2)}, u32[]{:S(2)}) collective-permute-start(f32[2,128,768]{2,1,0:T(8,128)S(1)} %get-tuple-element.36), channel_id=1, source_target_pairs={{0,1},{1,0},{2,3},{3,2},{4,5},{5,4},{6,7},{7,6},{8,9},{9,8},{10,11... | collective-permute-start | bytes 2359304 | tf_op jit(solution)/shard_map/ppermute | solution.py:293
  3.2 7.3 %collective-permute-start.1 = (f32[6,128,768]{2,1,0:T(8,128)S(1)}, f32[6,128,768]{2,1,0:T(8,128)S(1)}, u32[]{:S(2)}, u32[]{:S(2)}) collective-permute-start(f32[6,128,768]{2,1,0:T(8,128)S(1)} %get-tuple-element.37), channel_id=1, source_target_pairs={{0,1},{1,0},{2,3},{3,2},{4,5},{5,4},{6,7},{7,6},{8,9},{9,8},{10,11... | collective-permute-start | bytes 7077896 | tf_op jit(solution)/shard_map/ppermute | solution.py:293
  5.0 10.3 %collective-permute-start.2 = (f32[2,48,768]{2,1,0:T(8,128)S(1)}, f32[2,48,768]{2,1,0:T(8,128)S(1)}, u32[]{:S(2)}, u32[]{:S(2)}) collective-permute-start(f32[2,48,768]{2,1,0:T(8,128)S(1)} %get-tuple-element.40), channel_id=1, source_target_pairs={{0,2},{1,3},{2,0},{3,1},{4,6},{5,7},{6,4},{7,5},{8,10},{9,11},{10,... | collective-permute-start | bytes 884744 | tf_op jit(solution)/shard_map/ppermute | solution.py:293
  8.0 9.7 %collective-permute-start.4 = (f32[1,80,768]{2,1,0:T(8,128)S(1)}, f32[1,80,768]{2,1,0:T(8,128)S(1)}, u32[]{:S(2)}, u32[]{:S(2)}) collective-permute-start(f32[1,80,768]{2,1,0:T(8,128)S(1)} %get-tuple-element.48), channel_id=1, source_target_pairs={{0,24},{8,16},{16,8},{24,0},{1,25},{9,17},{17,9},{25,1},{2,26},{10... | collective-permute-start | bytes 737288 | tf_op jit(solution)/shard_map/ppermute | solution.py:296
  10.8 13.3 %collective-permute-start.3 = (f32[1,64,768]{2,1,0:T(8,128)S(1)}, f32[1,64,768]{2,1,0:T(8,128)S(1)}, u32[]{:S(2)}, u32[]{:S(2)}) collective-permute-start(f32[1,64,768]{2,1,0:T(8,128)S(1)} %get-tuple-element.46), channel_id=1, source_target_pairs={{0,24},{8,16},{16,8},{24,0},{1,25},{9,17},{17,9},{25,1},{2,26},{10... | collective-permute-start | bytes 589832 | tf_op jit(solution)/shard_map/ppermute | solution.py:296
  17.8 13.1 %collective-permute-start.6 = (f32[1,80,768]{2,1,0:T(8,128)S(1)}, f32[1,80,768]{2,1,0:T(8,128)S(1)}, u32[]{:S(2)}, u32[]{:S(2)}) collective-permute-start(f32[1,80,768]{2,1,0:T(8,128)S(1)} %get-tuple-element.55), channel_id=1, source_target_pairs={{0,2},{1,3},{2,0},{3,1},{4,6},{5,7},{6,4},{7,5},{8,10},{9,11},{10,... | collective-permute-start | bytes 737288 | tf_op jit(solution)/shard_map/ppermute | solution.py:293
  17.9 13.0 %collective-permute-start.7 = (f32[1,80,768]{2,1,0:T(8,128)S(1)}, f32[1,80,768]{2,1,0:T(8,128)S(1)}, u32[]{:S(2)}, u32[]{:S(2)}) collective-permute-start(f32[1,80,768]{2,1,0:T(8,128)S(1)} %get-tuple-element.56), channel_id=1, source_target_pairs={{0,24},{8,16},{16,8},{24,0},{1,25},{9,17},{17,9},{25,1},{2,26},{10... | collective-permute-start | bytes 737288 | tf_op jit(solution)/shard_map/ppermute | solution.py:296
  20.9 10.0 %collective-permute-start.8 = (f32[1,48,768]{2,1,0:T(8,128)S(1)}, f32[1,48,768]{2,1,0:T(8,128)S(1)}, u32[]{:S(2)}, u32[]{:S(2)}) collective-permute-start(f32[1,48,768]{2,1,0:T(8,128)S(1)} %get-tuple-element.57), channel_id=1, source_target_pairs={{0,24},{8,16},{16,8},{24,0},{1,25},{9,17},{17,9},{25,1},{2,26},{10... | collective-permute-start | bytes 442376 | tf_op jit(solution)/shard_map/ppermute | solution.py:296
  21.3 15.4 %collective-permute-start.11 = (f32[1,64,768]{2,1,0:T(8,128)S(1)}, f32[1,64,768]{2,1,0:T(8,128)S(1)}, u32[]{:S(2)}, u32[]{:S(2)}) collective-permute-start(f32[1,64,768]{2,1,0:T(8,128)S(1)} %get-tuple-element.62), channel_id=1, source_target_pairs={{0,24},{8,16},{16,8},{24,0},{1,25},{9,17},{17,9},{25,1},{2,26},{10... | collective-permute-start | bytes 589832 | tf_op jit(solution)/shard_map/ppermute | solution.py:296
  24.2 14.7 %collective-permute-start.5 = (f32[1,64,768]{2,1,0:T(8,128)S(1)}, f32[1,64,768]{2,1,0:T(8,128)S(1)}, u32[]{:S(2)}, u32[]{:S(2)}) collective-permute-start(f32[1,64,768]{2,1,0:T(8,128)S(1)} %get-tuple-element.53), channel_id=1, source_target_pairs={{0,2},{1,3},{2,0},{3,1},{4,6},{5,7},{6,4},{7,5},{8,10},{9,11},{10,... | collective-permute-start | bytes 589832 | tf_op jit(solution)/shard_map/ppermute | solution.py:293
  31.0 16.7 %collective-permute-start.9 = (f32[1,128,768]{2,1,0:T(8,128)S(1)}, f32[1,128,768]{2,1,0:T(8,128)S(1)}, u32[]{:S(2)}, u32[]{:S(2)}) collective-permute-start(f32[1,128,768]{2,1,0:T(8,128)S(1)} %get-tuple-element.59), channel_id=1, source_target_pairs={{0,4},{1,5},{2,6},{3,7},{4,0},{5,1},{6,2},{7,3},{8,12},{9,13},{10,... | collective-permute-start | bytes 1179656 | tf_op jit(solution)/shard_map/ppermute | solution.py:293
  34.2 13.4 %collective-permute-start.10 = (f32[1,128,768]{2,1,0:T(8,128)S(1)}, f32[1,128,768]{2,1,0:T(8,128)S(1)}, u32[]{:S(2)}, u32[]{:S(2)}) collective-permute-start(f32[1,128,768]{2,1,0:T(8,128)S(1)} %get-tuple-element.61), channel_id=1, source_target_pairs={{0,24},{8,16},{16,8},{24,0},{1,25},{9,17},{17,9},{25,1},{2,26},{10... | collective-permute-start | bytes 1179656 | tf_op jit(solution)/shard_map/ppermute | solution.py:296
  37.3 10.3 %collective-permute-start.12 = (f32[1,64,768]{2,1,0:T(8,128)S(1)}, f32[1,64,768]{2,1,0:T(8,128)S(1)}, u32[]{:S(2)}, u32[]{:S(2)}) collective-permute-start(f32[1,64,768]{2,1,0:T(8,128)S(1)} %get-tuple-element.64), channel_id=1, source_target_pairs={{0,2},{1,3},{2,0},{3,1},{4,6},{5,7},{6,4},{7,5},{8,10},{9,11},{10,... | collective-permute-start | bytes 589832 | tf_op jit(solution)/shard_map/ppermute | solution.py:293

commit v5 on v4

--- a/solution.py
+++ b/solution.py
@@ -8,7 +8,7 @@
 from jax.sharding import PartitionSpec as P
 
 VMEM = pl.BlockSpec(memory_space=pltpu.VMEM)
-SOON = pl.CostEstimate(flops=25_000_000_000, bytes_accessed=1000, transcendentals=0)
+SOON = pl.CostEstimate(flops=10_000_000_000, bytes_accessed=1000, transcendentals=0)
 SMALL = pltpu.CompilerParams(vmem_limit_bytes=8 << 20)
 
 
@@ -251,34 +251,30 @@
 
 def order(chips, head):
     last = chips - 1
-    cut, half = head * 5 // 8, head // 2
-    pairs = [(1, block) for block in reversed(range(last))]
-    pairs += [(0, block) for block in reversed(range(last))]
+    half = head // 2
     everything = list(reversed(range(chips)))
+    pairs = [(1, block) for block in everything[1:]] + [(0, block) for block in everything[1:]]
     if chips < 4:
         events = [("core", *pairs)] if pairs else []
         events += [("up", block, 0, head) for block in everything] + [("base", *everything)]
         return events + [("down", block, 0, head) for block in everything[:-1]]
     events = [
         ("core", *pairs),
-        ("up", last, 0, cut),
-        ("raw", last, cut, head),
-        ("up", last - 1, 0, cut),
+        ("up", last, 0, half),
+        ("raw", last, half, head),
+        ("up", last - 1, 0, half),
         ("up", 1, 0, half),
         ("base", *everything),
-        ("down", last, 0, cut),
-        ("up", last - 1, cut, head),
+        ("down", last, 0, half),
+        ("up", last - 1, half, head),
     ]
     for block in reversed(range(2, last - 1)):
         events += [("up", block, 0, head), ("down", block + 1, 0, head)]
-    return [
-        *events,
-        ("up", 1, half, head),
-        ("down", 1, 0, half),
-        ("down", 2, 0, head),
-        ("up", 0, 0, head),
-        ("down", 1, half, head),
-    ]
+    parts = [(0, half), (half, head)] if last - 1 == 2 else [(0, head)]
+    events += [("down", 2, *parts[0]), ("down", 1, 0, half), ("up", 1, half, head)]
+    events += [("down", 2, *part) for part in parts[1:]]
+    events += [("up", 0, 0, head), ("down", 1, half, head)]
+    return events + [("take", 0, *part, "down2") for part in parts]
 
 
 def body(activations, queries, keys, grad_out, segment_ids):
@@ -328,12 +324,12 @@
         bit = block & -block
         got = swap(both, 2 * bit)
         upper.add(block ^ bit, low, high, got, 0)
-        lower.add(block ^ bit, low, high, got, 1)
+        late.append((block ^ bit, low, high, got, 1, "raw"))
 
     def send_down(block, low, high):
         (part,) = make("lower", [lower.segments(block, low, high)])
         bit = block & -block
-        lower.add(block ^ bit, low, high, swap(part, 2 * bit))
+        late.append((block ^ bit, low, high, swap(part, 2 * bit), 0, f"down{block}"))
 
     def settle(blocks_of):
         sums = make("base", [lower.segments(block, 0, head) for block in blocks_of])
@@ -345,12 +341,17 @@
         (part,) = make("take", [lower.segments(block, low, high)])
         lower.settle(block, low, high, part)
 
-    late = {}
-
-    def arrive(block, low, high):
-        for rows in [rows for rows in late if rows[0] == block]:
-            if low <= rows[1] and rows[2] <= high:
-                lower.add(*rows, late.pop(rows))
+    late = []
+
+    def arrive(block, low, high, kind=None):
+        waiting = late[:]
+        late.clear()
+        for entry in waiting:
+            inside = entry[0] == block and low <= entry[1] and entry[2] <= high
+            if inside and kind in (None, entry[5]):
+                lower.add(*entry[:5])
+            else:
+                late.append(entry)
 
     for event, *what in order(chips, head):
         if event == "core":
@@ -358,7 +359,7 @@
         elif event == "base":
             settle(what)
         elif event == "up":
-            late[tuple(what)] = send_up(*what)
+            late.append((*what, send_up(*what), 0, "up"))
         elif event == "raw":
             send_raw(*what)
         elif event == "down":
@@ -366,7 +367,7 @@
             send_down(*what)
         elif event == "take":
             arrive(*what)
-            take(*what)
+            take(*what[:3])
     arrive(0, 0, head)
     assert not late
     return finish(lower.segments(0, 0, head), head, width)

time: 48.6 us -> 45.2 us (0.930)
  waiting for transfers between devices: 20.3 us -> 15.3 us
  starting transfers between devices: 22.3 us -> 23.7 us
    ppermute x6, waiting for transfers between devices: 7.13 us -> 3.06 us  [mirror(): lax.ppermute(block, 'pipe', [(i, slots - 1 - i) for i in range(slots)])]
    ppermute x7 -> x8, starting transfers between devices: 9.99 us -> 12.7 us  [swap(): return lax.ppermute(block, 'dp', [(i, i ^ distance) for i in range(ways)])]
    ppermute x6, starting transfers between devices: 12.3 us -> 11 us  [mirror(): lax.ppermute(block, 'pipe', [(i, slots - 1 - i) for i in range(slots)])]
    ppermute x7 -> x8, waiting for transfers between devices: 13.1 us -> 12.3 us  [swap(): return lax.ppermute(block, 'dp', [(i, i ^ distance) for i in range(ways)])]
    pallas_call x13 -> x16, Pallas kernels: 2.83 us -> 2.87 us  [blocks(): pl.pallas_call(functools.partial(blocks_kernel, static, len(operands), wi...]
  transfers between devices with their start and end apart: 13 -> 14, of which waited for: 5 -> 8; matrix products, arithmetic and copies ran while one was open for 0% -> 0% of each run, Pallas kernels for 6% -> 6%
where the time goes in v5:
time: 45.2 us; the launch traced here: 45.1 us
  starting transfers between devices  23.7 us (52%)
  waiting for transfers between devices  15.3 us (34%)
  Pallas kernels  5.88 us (13%)
    ppermute x8, starting transfers between devices, swap(): return lax.ppermute(block, 'dp', [(i, i ^ distance) for i in range(ways)])  12.7 us
    ppermute x8, waiting for transfers between devices, swap(): return lax.ppermute(block, 'dp', [(i, i ^ distance) for i in range(ways)])  12.3 us
    ppermute x6, starting transfers between devices, mirror(): lax.ppermute(block, 'pipe', [(i, slots - 1 - i) for i in range(slots)])  11 us
    ppermute x6, waiting for transfers between devices, mirror(): lax.ppermute(block, 'pipe', [(i, slots - 1 - i) for i in range(slots)])  3.06 us
    pallas_call x16, Pallas kernels, blocks(): pl.pallas_call(functools.partial(blocks_kernel, static, len(operands), wi...  2.87 us
    pallas_call x1, Pallas kernels, front(): pl.pallas_call(functools.partial(front_kernel, flip, width), out_shape=(j...  2.18 us
  transfers between devices with their start and end apart: 14, of which 8 were waited for; matrix products, arithmetic and copies ran while one was open for 0% of the time, Pallas kernels for 6%

profile of v5, /device:TPU:0, one launch (start us, length us, event | category | flops | bytes accessed | tf_op | source)
XLA Modules:
  0.0 45.1 jit_solution(8122104039541351809)
XLA Ops:
  0.0 2.2 %front.1 = (bf16[2,128,128]{2,1,0:T(8,128)(2,1)S(1)}, f32[2,128,768]{2,1,0:T(8,128)S(1)}) custom-call(bf16[2,1,128,6144]{3,2,1,0:T(8,128)(2,1)} %refs_0_.31, bf16[2,1,128,128]{3,2,1,0:T(8,128)(2,1)} %queries.1, bf16[2,1,128,128]{3,2,1,0:T(8,128)(2,1)} %keys.1, bf16[2,1,128,128]{3,2,1,0:T(8,128)(2,1)} %grad_out.1, s32[2,1,1,128]{3,2,1,0:T(1,128)} %segs.1), custom_call_target="tpu_custom_call" | custom-call | flops 10000000000 | bytes 1000 | tf_op jit(solution)/shard_map/front/pallas_call | solution.py:77
  2.2 0.5 %collective-permute-start = (f32[2,128,768]{2,1,0:T(8,128)S(1)}, f32[2,128,768]{2,1,0:T(8,128)S(1)}, u32[]{:S(2)}, u32[]{:S(2)}) collective-permute-start(f32[2,128,768]{2,1,0:T(8,128)S(1)} %get-tuple-element.42), channel_id=1, source_target_pairs={{0,1},{1,0},{2,3},{3,2},{4,5},{5,4},{6,7},{7,6},{8,9},{9,8},{10,11... | collective-permute-start | bytes 2359304 | tf_op jit(solution)/shard_map/ppermute | solution.py:289
  2.7 0.5 %theirs.1 = (f32[6,128,768]{2,1,0:T(8,128)S(1)}, f32[8,128]{1,0:T(8,128)S(1)}) custom-call(bf16[2,1,128,6144]{3,2,1,0:T(8,128)(2,1)S(1)} %copy-done, bf16[2,128,128]{2,1,0:T(8,128)(2,1)S(1)} %get-tuple-element.41.refs_1_), custom_call_target="tpu_custom_call" | custom-call | flops 10000000000 | bytes 1000 | tf_op jit(solution)/shard_map/theirs/pallas_call | solution.py:172
  3.2 0.1 collective-permute-start.1
  3.3 1.3 %collective-permute-done.refs_2_ = f32[2,128,768]{2,1,0:T(8,128)S(1)} collective-permute-done((f32[2,128,768]{2,1,0:T(8,128)S(1)}, f32[2,128,768]{2,1,0:T(8,128)S(1)}, u32[]{:S(2)}, u32[]{:S(2)}) %collective-permute-start) | collective-permute-done | bytes 786464 | tf_op jit(solution)/shard_map/ppermute | solution.py:289
  4.6 0.2 upper.6
  4.8 3.9 %collective-permute-start.3 = (f32[1,64,768]{2,1,0:T(8,128)S(1)}, f32[1,64,768]{2,1,0:T(8,128)S(1)}, u32[]{:S(2)}, u32[]{:S(2)}) collective-permute-start(f32[1,64,768]{2,1,0:T(8,128)S(1)} %get-tuple-element.53), channel_id=1, source_target_pairs={{0,24},{8,16},{16,8},{24,0},{1,25},{9,17},{17,9},{25,1},{2,26},{10... | collective-permute-start | bytes 589832 | tf_op jit(solution)/shard_map/ppermute | solution.py:292
  8.7 0.2 raw.1
  8.9 1.6 %collective-permute-start.5 = (f32[2,64,768]{2,1,0:T(8,128)S(1)}, f32[2,64,768]{2,1,0:T(8,128)S(1)}, u32[]{:S(2)}, u32[]{:S(2)}) collective-permute-start(f32[2,64,768]{2,1,0:T(8,128)S(1)} %get-tuple-element.56), channel_id=1, source_target_pairs={{0,2},{1,3},{2,0},{3,1},{4,6},{5,7},{6,4},{7,5},{8,10},{9,11},{10,... | collective-permute-start | bytes 1179656 | tf_op jit(solution)/shard_map/ppermute | solution.py:289
  10.5 0.2 upper.7
  10.7 1.4 %collective-permute-start.2 = (f32[1,64,768]{2,1,0:T(8,128)S(1)}, f32[1,64,768]{2,1,0:T(8,128)S(1)}, u32[]{:S(2)}, u32[]{:S(2)}) collective-permute-start(f32[1,64,768]{2,1,0:T(8,128)S(1)} %get-tuple-element.51), channel_id=1, source_target_pairs={{0,24},{8,16},{16,8},{24,0},{1,25},{9,17},{17,9},{25,1},{2,26},{10... | collective-permute-start | bytes 589832 | tf_op jit(solution)/shard_map/ppermute | solution.py:292
  12.1 0.2 upper.8
  12.2 0.4 base.1
  12.6 1.3 %collective-permute-done.3.refs_3_ = f32[1,64,768]{2,1,0:T(8,128)S(1)} collective-permute-done((f32[1,64,768]{2,1,0:T(8,128)S(1)}, f32[1,64,768]{2,1,0:T(8,128)S(1)}, u32[]{:S(2)}, u32[]{:S(2)}) %collective-permute-start.3) | collective-permute-done | bytes 196640 | tf_op jit(solution)/shard_map/ppermute | solution.py:292
  14.0 2.6 %collective-permute-start.4 = (f32[1,64,768]{2,1,0:T(8,128)S(1)}, f32[1,64,768]{2,1,0:T(8,128)S(1)}, u32[]{:S(2)}, u32[]{:S(2)}) collective-permute-start(f32[1,64,768]{2,1,0:T(8,128)S(1)} %get-tuple-element.55), channel_id=1, source_target_pairs={{0,2},{1,3},{2,0},{3,1},{4,6},{5,7},{6,4},{7,5},{8,10},{9,11},{10,... | collective-permute-start | bytes 589832 | tf_op jit(solution)/shard_map/ppermute | solution.py:289
  16.5 2.4 %collective-permute-start.7 = (f32[1,64,768]{2,1,0:T(8,128)S(1)}, f32[1,64,768]{2,1,0:T(8,128)S(1)}, u32[]{:S(2)}, u32[]{:S(2)}) collective-permute-start(f32[1,64,768]{2,1,0:T(8,128)S(1)} %get-tuple-element.61), channel_id=1, source_target_pairs={{0,24},{8,16},{16,8},{24,0},{1,25},{9,17},{17,9},{25,1},{2,26},{10... | collective-permute-start | bytes 589832 | tf_op jit(solution)/shard_map/ppermute | solution.py:292
  19.0 2.0 %collective-permute-done.5.refs_3_ = f32[2,64,768]{2,1,0:T(8,128)S(1)} collective-permute-done((f32[2,64,768]{2,1,0:T(8,128)S(1)}, f32[2,64,768]{2,1,0:T(8,128)S(1)}, u32[]{:S(2)}, u32[]{:S(2)}) %collective-permute-start.5) | collective-permute-done | bytes 393248 | tf_op jit(solution)/shard_map/ppermute | solution.py:289
  21.0 0.2 upper.9
  21.2 2.8 %collective-permute-done.4.refs_4_ = f32[1,64,768]{2,1,0:T(8,128)S(1)} collective-permute-done((f32[1,64,768]{2,1,0:T(8,128)S(1)}, f32[1,64,768]{2,1,0:T(8,128)S(1)}, u32[]{:S(2)}, u32[]{:S(2)}) %collective-permute-start.4) | collective-permute-done | bytes 196640 | tf_op jit(solution)/shard_map/ppermute | solution.py:289
  24.1 2.6 %collective-permute-start.6 = (f32[1,64,768]{2,1,0:T(8,128)S(1)}, f32[1,64,768]{2,1,0:T(8,128)S(1)}, u32[]{:S(2)}, u32[]{:S(2)}) collective-permute-start(f32[1,64,768]{2,1,0:T(8,128)S(1)} %get-tuple-element.59), channel_id=1, source_target_pairs={{0,4},{1,5},{2,6},{3,7},{4,0},{5,1},{6,2},{7,3},{8,12},{9,13},{10,... | collective-permute-start | bytes 589832 | tf_op jit(solution)/shard_map/ppermute | solution.py:289
  26.8 0.2 upper.10
  26.9 0.7 %collective-permute-start.8 = (f32[1,64,768]{2,1,0:T(8,128)S(1)}, f32[1,64,768]{2,1,0:T(8,128)S(1)}, u32[]{:S(2)}, u32[]{:S(2)}) collective-permute-start(f32[1,64,768]{2,1,0:T(8,128)S(1)} %get-tuple-element.64), channel_id=1, source_target_pairs={{0,24},{8,16},{16,8},{24,0},{1,25},{9,17},{17,9},{25,1},{2,26},{10... | collective-permute-start | bytes 589832 | tf_op jit(solution)/shard_map/ppermute | solution.py:292
  27.7 1.4 %collective-permute-start.10 = (f32[1,64,768]{2,1,0:T(8,128)S(1)}, f32[1,64,768]{2,1,0:T(8,128)S(1)}, u32[]{:S(2)}, u32[]{:S(2)}) collective-permute-start(f32[1,64,768]{2,1,0:T(8,128)S(1)} %get-tuple-element.71), channel_id=1, source_target_pairs={{0,2},{1,3},{2,0},{3,1},{4,6},{5,7},{6,4},{7,5},{8,10},{9,11},{10,... | collective-permute-start | bytes 589832 | tf_op jit(solution)/shard_map/ppermute | solution.py:289
  29.1 0.2 upper.11
  29.3 2.5 %collective-permute-start.11 = (f32[1,128,768]{2,1,0:T(8,128)S(1)}, f32[1,128,768]{2,1,0:T(8,128)S(1)}, u32[]{:S(2)}, u32[]{:S(2)}) collective-permute-start(f32[1,128,768]{2,1,0:T(8,128)S(1)} %get-tuple-element.72), channel_id=1, source_target_pairs={{0,24},{8,16},{16,8},{24,0},{1,25},{9,17},{17,9},{25,1},{2,26},{10... | collective-permute-start | bytes 1179656 | tf_op jit(solution)/shard_map/ppermute | solution.py:292
  31.8 2.2 %collective-permute-start.12 = (f32[1,64,768]{2,1,0:T(8,128)S(1)}, f32[1,64,768]{2,1,0:T(8,128)S(1)}, u32[]{:S(2)}, u32[]{:S(2)}) collective-permute-start(f32[1,64,768]{2,1,0:T(8,128)S(1)} %get-tuple-element.73), channel_id=1, source_target_pairs={{0,4},{1,5},{2,6},{3,7},{4,0},{5,1},{6,2},{7,3},{8,12},{9,13},{10,... | collective-permute-start | bytes 589832 | tf_op jit(solution)/shard_map/ppermute | solution.py:289
  34.0 1.7 %collective-permute-done.8.refs_3_ = f32[1,64,768]{2,1,0:T(8,128)S(1)} collective-permute-done((f32[1,64,768]{2,1,0:T(8,128)S(1)}, f32[1,64,768]{2,1,0:T(8,128)S(1)}, u32[]{:S(2)}, u32[]{:S(2)}) %collective-permute-start.8) | collective-permute-done | bytes 196640 | tf_op jit(solution)/shard_map/ppermute | solution.py:292
  35.8 1.6 %collective-permute-start.13 = (f32[1,64,768]{2,1,0:T(8,128)S(1)}, f32[1,64,768]{2,1,0:T(8,128)S(1)}, u32[]{:S(2)}, u32[]{:S(2)}) collective-permute-start(f32[1,64,768]{2,1,0:T(8,128)S(1)} %get-tuple-element.76), channel_id=1, source_target_pairs={{0,2},{1,3},{2,0},{3,1},{4,6},{5,7},{6,4},{7,5},{8,10},{9,11},{10,... | collective-permute-start | bytes 589832 | tf_op jit(solution)/shard_map/ppermute | solution.py:289
  37.4 1.1 %collective-permute-done.6.refs_3_ = f32[1,64,768]{2,1,0:T(8,128)S(1)} collective-permute-done((f32[1,64,768]{2,1,0:T(8,128)S(1)}, f32[1,64,768]{2,1,0:T(8,128)S(1)}, u32[]{:S(2)}, u32[]{:S(2)}) %collective-permute-start.6) | collective-permute-done | bytes 196640 | tf_op jit(solution)/shard_map/ppermute | solution.py:289
  38.6 5.0 %collective-permute-done.12.refs_3_ = f32[1,64,768]{2,1,0:T(8,128)S(1)} collective-permute-done((f32[1,64,768]{2,1,0:T(8,128)S(1)}, f32[1,64,768]{2,1,0:T(8,128)S(1)}, u32[]{:S(2)}, u32[]{:S(2)}) %collective-permute-start.12) | collective-permute-done | bytes 196640 | tf_op jit(solution)/shard_map/ppermute | solution.py:289
  43.5 0.6 %take.3 = (f32[1,64,768]{2,1,0:T(8,128)S(1)}, f32[8,128]{1,0:T(8,128)}) custom-call(bf16[2,1,128,6144]{3,2,1,0:T(8,128)(2,1)S(1)} %copy-done, bf16[2,128,128]{2,1,0:T(8,128)(2,1)S(1)} %get-tuple-element.41.refs_1_, f32[1,128,768]{2,1,0:T(8,128)S(1)} %get-tuple-element.49.refs_2_, f32[1,64,768]{2,1,0:T(8,128)S(1)} %collective-permute-done.12.refs_3_, ...), custom_call_target="tpu_custom_call" | custom-call | flops 10000000000 | bytes 1000 | tf_op jit(solution)/shard_map/take/pallas_call | solution.py:172
  44.2 0.8 %finish.1 = bf16[1,768,128]{2,1,0:T(8,128)(2,1)} custom-call(f32[1,64,768]{2,1,0:T(8,128)S(1)} %get-tuple-element.70.refs_0_, f32[1,64,768]{2,1,0:T(8,128)S(1)} %collective-permute-done.10.refs_1_, f32[1,128,768]{2,1,0:T(8,128)S(1)} %collective-permute-done.11.refs_2_, f32[1,64,768]{2,1,0:T(8,128)S(1)} %get-tuple-element.75.refs_3_, ...), custom_call_target="tpu_custom_call" | custom-call | flops 10000000000 | bytes 1000 | tf_op jit(solution)/shard_map/finish/pallas_call | solution.py:206
  (16 shorter events, 0.4 us)
Async XLA Ops:
  0.0 2.7 %copy-start = (bf16[2,1,128,6144]{3,2,1,0:T(8,128)(2,1)S(1)}, bf16[2,1,128,6144]{3,2,1,0:T(8,128)(2,1)}, u32[]{:S(2)}) copy-start(bf16[2,1,128,6144]{3,2,1,0:T(8,128)(2,1)} %refs_0_.31) | copy-start | bytes 9437188
  2.2 2.4 %collective-permute-start = (f32[2,128,768]{2,1,0:T(8,128)S(1)}, f32[2,128,768]{2,1,0:T(8,128)S(1)}, u32[]{:S(2)}, u32[]{:S(2)}) collective-permute-start(f32[2,128,768]{2,1,0:T(8,128)S(1)} %get-tuple-element.42), channel_id=1, source_target_pairs={{0,1},{1,0},{2,3},{3,2},{4,5},{5,4},{6,7},{7,6},{8,9},{9,8},{10,11... | collective-permute-start | bytes 2359304 | tf_op jit(solution)/shard_map/ppermute | solution.py:289
  3.2 7.3 %collective-permute-start.1 = (f32[6,128,768]{2,1,0:T(8,128)S(1)}, f32[6,128,768]{2,1,0:T(8,128)S(1)}, u32[]{:S(2)}, u32[]{:S(2)}) collective-permute-start(f32[6,128,768]{2,1,0:T(8,128)S(1)} %get-tuple-element.43), channel_id=1, source_target_pairs={{0,1},{1,0},{2,3},{3,2},{4,5},{5,4},{6,7},{7,6},{8,9},{9,8},{10,11... | collective-permute-start | bytes 7077896 | tf_op jit(solution)/shard_map/ppermute | solution.py:289
  4.8 9.1 %collective-permute-start.3 = (f32[1,64,768]{2,1,0:T(8,128)S(1)}, f32[1,64,768]{2,1,0:T(8,128)S(1)}, u32[]{:S(2)}, u32[]{:S(2)}) collective-permute-start(f32[1,64,768]{2,1,0:T(8,128)S(1)} %get-tuple-element.53), channel_id=1, source_target_pairs={{0,24},{8,16},{16,8},{24,0},{1,25},{9,17},{17,9},{25,1},{2,26},{10... | collective-permute-start | bytes 589832 | tf_op jit(solution)/shard_map/ppermute | solution.py:292
  8.9 12.1 %collective-permute-start.5 = (f32[2,64,768]{2,1,0:T(8,128)S(1)}, f32[2,64,768]{2,1,0:T(8,128)S(1)}, u32[]{:S(2)}, u32[]{:S(2)}) collective-permute-start(f32[2,64,768]{2,1,0:T(8,128)S(1)} %get-tuple-element.56), channel_id=1, source_target_pairs={{0,2},{1,3},{2,0},{3,1},{4,6},{5,7},{6,4},{7,5},{8,10},{9,11},{10,... | collective-permute-start | bytes 1179656 | tf_op jit(solution)/shard_map/ppermute | solution.py:289
  10.7 10.5 %collective-permute-start.2 = (f32[1,64,768]{2,1,0:T(8,128)S(1)}, f32[1,64,768]{2,1,0:T(8,128)S(1)}, u32[]{:S(2)}, u32[]{:S(2)}) collective-permute-start(f32[1,64,768]{2,1,0:T(8,128)S(1)} %get-tuple-element.51), channel_id=1, source_target_pairs={{0,24},{8,16},{16,8},{24,0},{1,25},{9,17},{17,9},{25,1},{2,26},{10... | collective-permute-start | bytes 589832 | tf_op jit(solution)/shard_map/ppermute | solution.py:292
  14.0 10.1 %collective-permute-start.4 = (f32[1,64,768]{2,1,0:T(8,128)S(1)}, f32[1,64,768]{2,1,0:T(8,128)S(1)}, u32[]{:S(2)}, u32[]{:S(2)}) collective-permute-start(f32[1,64,768]{2,1,0:T(8,128)S(1)} %get-tuple-element.55), channel_id=1, source_target_pairs={{0,2},{1,3},{2,0},{3,1},{4,6},{5,7},{6,4},{7,5},{8,10},{9,11},{10,... | collective-permute-start | bytes 589832 | tf_op jit(solution)/shard_map/ppermute | solution.py:289
  16.5 10.2 %collective-permute-start.7 = (f32[1,64,768]{2,1,0:T(8,128)S(1)}, f32[1,64,768]{2,1,0:T(8,128)S(1)}, u32[]{:S(2)}, u32[]{:S(2)}) collective-permute-start(f32[1,64,768]{2,1,0:T(8,128)S(1)} %get-tuple-element.61), channel_id=1, source_target_pairs={{0,24},{8,16},{16,8},{24,0},{1,25},{9,17},{17,9},{25,1},{2,26},{10... | collective-permute-start | bytes 589832 | tf_op jit(solution)/shard_map/ppermute | solution.py:292
  21.1 7.9 %collective-permute-start.9 = (f32[1,64,768]{2,1,0:T(8,128)S(1)}, f32[1,64,768]{2,1,0:T(8,128)S(1)}, u32[]{:S(2)}, u32[]{:S(2)}) collective-permute-start(f32[1,64,768]{2,1,0:T(8,128)S(1)} %get-tuple-element.65), channel_id=1, source_target_pairs={{0,24},{8,16},{16,8},{24,0},{1,25},{9,17},{17,9},{25,1},{2,26},{10... | collective-permute-start | bytes 589832 | tf_op jit(solution)/shard_map/ppermute | solution.py:292
  24.1 14.5 %collective-permute-start.6 = (f32[1,64,768]{2,1,0:T(8,128)S(1)}, f32[1,64,768]{2,1,0:T(8,128)S(1)}, u32[]{:S(2)}, u32[]{:S(2)}) collective-permute-start(f32[1,64,768]{2,1,0:T(8,128)S(1)} %get-tuple-element.59), channel_id=1, source_target_pairs={{0,4},{1,5},{2,6},{3,7},{4,0},{5,1},{6,2},{7,3},{8,12},{9,13},{10,... | collective-permute-start | bytes 589832 | tf_op jit(solution)/shard_map/ppermute | solution.py:289
  26.9 8.8 %collective-permute-start.8 = (f32[1,64,768]{2,1,0:T(8,128)S(1)}, f32[1,64,768]{2,1,0:T(8,128)S(1)}, u32[]{:S(2)}, u32[]{:S(2)}) collective-permute-start(f32[1,64,768]{2,1,0:T(8,128)S(1)} %get-tuple-element.64), channel_id=1, source_target_pairs={{0,24},{8,16},{16,8},{24,0},{1,25},{9,17},{17,9},{25,1},{2,26},{10... | collective-permute-start | bytes 589832 | tf_op jit(solution)/shard_map/ppermute | solution.py:292
  27.7 16.5 %collective-permute-start.10 = (f32[1,64,768]{2,1,0:T(8,128)S(1)}, f32[1,64,768]{2,1,0:T(8,128)S(1)}, u32[]{:S(2)}, u32[]{:S(2)}) collective-permute-start(f32[1,64,768]{2,1,0:T(8,128)S(1)} %get-tuple-element.71), channel_id=1, source_target_pairs={{0,2},{1,3},{2,0},{3,1},{4,6},{5,7},{6,4},{7,5},{8,10},{9,11},{10,... | collective-permute-start | bytes 589832 | tf_op jit(solution)/shard_map/ppermute | solution.py:289
  29.3 14.8 %collective-permute-start.11 = (f32[1,128,768]{2,1,0:T(8,128)S(1)}, f32[1,128,768]{2,1,0:T(8,128)S(1)}, u32[]{:S(2)}, u32[]{:S(2)}) collective-permute-start(f32[1,128,768]{2,1,0:T(8,128)S(1)} %get-tuple-element.72), channel_id=1, source_target_pairs={{0,24},{8,16},{16,8},{24,0},{1,25},{9,17},{17,9},{25,1},{2,26},{10... | collective-permute-start | bytes 1179656 | tf_op jit(solution)/shard_map/ppermute | solution.py:292
  31.8 11.7 %collective-permute-start.12 = (f32[1,64,768]{2,1,0:T(8,128)S(1)}, f32[1,64,768]{2,1,0:T(8,128)S(1)}, u32[]{:S(2)}, u32[]{:S(2)}) collective-permute-start(f32[1,64,768]{2,1,0:T(8,128)S(1)} %get-tuple-element.73), channel_id=1, source_target_pairs={{0,4},{1,5},{2,6},{3,7},{4,0},{5,1},{6,2},{7,3},{8,12},{9,13},{10,... | collective-permute-start | bytes 589832 | tf_op jit(solution)/shard_map/ppermute | solution.py:289
  35.8 8.5 %collective-permute-start.13 = (f32[1,64,768]{2,1,0:T(8,128)S(1)}, f32[1,64,768]{2,1,0:T(8,128)S(1)}, u32[]{:S(2)}, u32[]{:S(2)}) collective-permute-start(f32[1,64,768]{2,1,0:T(8,128)S(1)} %get-tuple-element.76), channel_id=1, source_target_pairs={{0,2},{1,3},{2,0},{3,1},{4,6},{5,7},{6,4},{7,5},{8,10},{9,11},{10,... | collective-permute-start | bytes 589832 | tf_op jit(solution)/shard_map/ppermute | solution.py:289

commit v6 on v5

--- a/solution.py
+++ b/solution.py
@@ -13,22 +13,33 @@
 
 
 def grad_v_columns(query_rows, key_rows, grad_rows, segs):
-    length, head = query_rows.shape
-    scores = lax.dot_general(
-        query_rows, key_rows, (((1,), (1,)), ((), ())), preferred_element_type=jnp.float32
-    ) / jnp.sqrt(jnp.float32(head))
-    shape = (length, length)
-    across = jnp.broadcast_to(segs, shape)
-    keep = (across == across.T) & (
-        lax.broadcasted_iota(jnp.int32, shape, 1) <= lax.broadcasted_iota(jnp.int32, shape, 0)
+    length, head = query_rows[0].shape
+    count = len(query_rows)
+    scores = [
+        lax.dot_general(q, k, (((1,), (1,)), ((), ())), preferred_element_type=jnp.float32)
+        for q, k in zip(query_rows, key_rows)
+    ]
+    scores = jnp.concatenate(scores, axis=0) / jnp.sqrt(jnp.float32(head))
+    square = (length, length)
+    across = [jnp.broadcast_to(row, square) for row in segs]
+    same = jnp.concatenate(across, axis=0) == jnp.concatenate([x.T for x in across], axis=0)
+    before = lax.broadcasted_iota(jnp.int32, square, 1) <= lax.broadcasted_iota(
+        jnp.int32, square, 0
     )
+    keep = same & jnp.concatenate([before] * count, axis=0)
     masked = jnp.where(keep, scores, jnp.float32(-1e30))
     top = jnp.max(masked, axis=1, keepdims=True)
     weights = jnp.where(keep, jnp.exp(masked - top), jnp.float32(0.0))
     probs = (weights / jnp.sum(weights, axis=1, keepdims=True)).astype(jnp.bfloat16)
-    return lax.dot_general(
-        grad_rows, probs, (((0,), (0,)), ((), ())), preferred_element_type=jnp.float32
-    ).astype(jnp.bfloat16)
+    return [
+        lax.dot_general(
+            grad,
+            probs[i * length : (i + 1) * length],
+            (((0,), (0,)), ((), ())),
+            preferred_element_type=jnp.float32,
+        ).astype(jnp.bfloat16)
+        for i, grad in enumerate(grad_rows)
+    ]
 
 
 def block_columns(flip, width):
@@ -48,25 +59,19 @@
         copy.start()
     for copy in copies[:-1]:
         copy.wait()
-    query_rows, key_rows, grad_rows, seg_rows = scratch[1:-1]
-    for half in (1, 0):
-        grads[half] = grad_v_columns(
-            query_rows[half, 0], key_rows[half, 0], grad_rows[half, 0], seg_rows[half, 0]
-        )
+    made = grad_v_columns(*([holder[half, 0] for half in range(2)] for holder in scratch[1:-1]))
+    for half in range(2):
+        grads[half] = made[half]
     copies[-1].wait()
     for slab in range(2):
-        first[slab] = jnp.dot(grads[1 - slab], columns[1 - slab], preferred_element_type=jnp.float32)
+        first[slab] = jnp.dot(made[1 - slab], columns[1 - slab], preferred_element_type=jnp.float32)
 
 
 def front(activations, queries, keys, grad_out, segment_ids, flip, width):
     head, length = queries.shape[3], queries.shape[2]
     if width % 128:
-        grads = jnp.stack(
-            [
-                grad_v_columns(queries[h, 0], keys[h, 0], grad_out[h, 0], segment_ids[h, 0])
-                for h in range(2)
-            ]
-        )
+        small = (queries, keys, grad_out, segment_ids)
+        grads = jnp.stack(grad_v_columns(*([x[half, 0] for half in range(2)] for x in small)))
         return grads, *plain_blocks(
             activations,
             grads,
@@ -197,12 +202,13 @@
         out[0, left : left + 128, :] = value.T.astype(out.dtype)
 
 
-def finish(segments, head, width):
+def finish(segments, head, width, token):
     if width % 128:
         (value,) = plain_blocks(None, None, width, [segments])
         return value.swapaxes(1, 2).astype(jnp.bfloat16)
     operands = []
     (static,) = number_operands([segments], operands)
+    operands.append(token)
     return pl.pallas_call(
         functools.partial(finish_kernel, static, len(operands)),
         out_shape=jax.ShapeDtypeStruct((1, width, head), jnp.bfloat16),
@@ -256,25 +262,24 @@
     pairs = [(1, block) for block in everything[1:]] + [(0, block) for block in everything[1:]]
     if chips < 4:
         events = [("core", *pairs)] if pairs else []
-        events += [("up", block, 0, head) for block in everything] + [("base", *everything)]
-        return events + [("down", block, 0, head) for block in everything[:-1]]
+        events += [("up", (block, 0, head)) for block in everything] + [("base", *everything)]
+        return events + [("down", (block, 0, head)) for block in everything[:-1]]
     events = [
         ("core", *pairs),
-        ("up", last, 0, half),
-        ("raw", last, half, head),
-        ("up", last - 1, 0, half),
-        ("up", 1, 0, half),
+        ("up", (last, 0, half)),
+        ("raw upper", last, half, head),
+        ("up", (last - 1, 0, half), (1, 0, half)),
         ("base", *everything),
-        ("down", last, 0, half),
-        ("up", last - 1, half, head),
+        ("down", (last, 0, half)),
+        ("raw lower", last, half, head),
+        ("up", (last - 1, half, head), (1, half, head)),
     ]
     for block in reversed(range(2, last - 1)):
-        events += [("up", block, 0, head), ("down", block + 1, 0, head)]
+        events += [("up", (block, 0, head)), ("down", (block + 1, 0, head))]
     parts = [(0, half), (half, head)] if last - 1 == 2 else [(0, head)]
-    events += [("down", 2, *parts[0]), ("down", 1, 0, half), ("up", 1, half, head)]
-    events += [("down", 2, *part) for part in parts[1:]]
-    events += [("up", 0, 0, head), ("down", 1, half, head)]
-    return events + [("take", 0, *part, "down2") for part in parts]
+    events += [("down", (2, *parts[0])), ("down", (1, 0, half)), ("up", (0, 0, head))]
+    events += [("down", (2, *part)) for part in parts[1:]]
+    return events + [("down", (1, half, head))]
 
 
 def body(activations, queries, keys, grad_out, segment_ids):
@@ -314,22 +319,38 @@
         for slab, (section, block) in enumerate(wanted):
             section.add(block, 0, head, got, slab)
 
-    def send_up(block, low, high):
-        (part,) = make("upper", [upper.segments(block, low, high)])
-        return mirror(part)
-
-    def send_raw(block, low, high):
-        rows = (block, low, high)
-        (both,) = make("raw", [upper.segments(*rows, 0) + lower.segments(*rows, 1)])
+    def send_up(*wanted):
+        plan = []
+        for slab, rows in enumerate(wanted):
+            plan += upper.segments(*rows, slab)
+        (part,) = make("upper", [plan])
+        got = mirror(part)
+        for slab, rows in enumerate(wanted):
+            late.append((*rows, got, slab))
+
+    def send_raw(name, block, low, high):
         bit = block & -block
-        got = swap(both, 2 * bit)
-        upper.add(block ^ bit, low, high, got, 0)
-        late.append((block ^ bit, low, high, got, 1, "raw"))
-
-    def send_down(block, low, high):
-        (part,) = make("lower", [lower.segments(block, low, high)])
-        bit = block & -block
-        late.append((block ^ bit, low, high, swap(part, 2 * bit), 0, f"down{block}"))
+        sections = {"raw": (upper, lower), "raw upper": (upper,), "raw lower": (lower,)}[name]
+        plan = []
+        for slab, section in enumerate(sections):
+            plan += section.segments(block, low, high, slab)
+        got = swap(make("raw", [plan])[0], 2 * bit)
+        for slab, section in enumerate(sections):
+            if section is upper:
+                upper.add(block ^ bit, low, high, got, slab)
+            else:
+                late.append((block ^ bit, low, high, got, slab))
+
+    def send_down(*wanted):
+        bit = wanted[0][0] & -wanted[0][0]
+        plan = []
+        for slab, rows in enumerate(wanted):
+            arrive(*rows)
+            plan += lower.segments(*rows, slab)
+        (part,) = make("lower", [plan])
+        got = swap(part, 2 * bit)
+        for slab, (block, low, high) in enumerate(wanted):
+            late.append((block ^ bit, low, high, got, slab))
 
     def settle(blocks_of):
         sums = make("base", [lower.segments(block, 0, head) for block in blocks_of])
@@ -337,19 +358,14 @@
             lower.dots[block] = False
             lower.settle(block, 0, head, array)
 
-    def take(block, low, high):
-        (part,) = make("take", [lower.segments(block, low, high)])
-        lower.settle(block, low, high, part)
-
     late = []
 
-    def arrive(block, low, high, kind=None):
+    def arrive(block, low, high):
         waiting = late[:]
         late.clear()
         for entry in waiting:
-            inside = entry[0] == block and low <= entry[1] and entry[2] <= high
-            if inside and kind in (None, entry[5]):
-                lower.add(*entry[:5])
+            if entry[0] == block and low <= entry[1] and entry[2] <= high:
+                lower.add(*entry)
             else:
                 late.append(entry)
 
@@ -359,18 +375,14 @@
         elif event == "base":
             settle(what)
         elif event == "up":
-            late.append((*what, send_up(*what), 0, "up"))
-        elif event == "raw":
-            send_raw(*what)
+            send_up(*what)
+        elif event.startswith("raw"):
+            send_raw(event, *what)
         elif event == "down":
-            arrive(*what)
             send_down(*what)
-        elif event == "take":
-            arrive(*what)
-            take(*what[:3])
     arrive(0, 0, head)
     assert not late
-    return finish(lower.segments(0, 0, head), head, width)
+    return finish(lower.segments(0, 0, head), head, width, token)
 
 
 def solution(mesh):

time: 45.2 us -> 43.1 us (0.954)
  Pallas kernels: 5.88 us -> 4.66 us
  waiting for transfers between devices: 15.3 us -> 14.6 us
    ppermute x8 -> x9, waiting for transfers between devices: 12.3 us -> 10.1 us  [swap(): return lax.ppermute(block, 'dp', [(i, i ^ distance) for i in range(ways)])]
    ppermute x6 -> x4, waiting for transfers between devices: 3.06 us -> 4.48 us  [mirror(): lax.ppermute(block, 'pipe', [(i, slots - 1 - i) for i in range(slots)])]
    pallas_call x16 -> x13, Pallas kernels: 2.87 us -> 1.94 us  [blocks(): pl.pallas_call(functools.partial(blocks_kernel, static, len(operands), wi...]
    ppermute x6 -> x4, starting transfers between devices: 11 us -> 10.7 us  [mirror(): lax.ppermute(block, 'pipe', [(i, slots - 1 - i) for i in range(slots)])]
    ppermute x8 -> x9, starting transfers between devices: 12.7 us -> 12.9 us  [swap(): return lax.ppermute(block, 'dp', [(i, i ^ distance) for i in range(ways)])]
  transfers between devices with their start and end apart: 14 -> 13, of which waited for: 8 -> 7; matrix products, arithmetic and copies ran while one was open for 0% -> 0% of each run, Pallas kernels for 6% -> 5%
where the time goes in v6:
time: 43.1 us; the launch traced here: 42.9 us
  starting transfers between devices  23.6 us (55%)
  waiting for transfers between devices  14.6 us (34%)
  Pallas kernels  4.66 us (11%)
    ppermute x9, starting transfers between devices, swap(): return lax.ppermute(block, 'dp', [(i, i ^ distance) for i in range(ways)])  12.9 us
    ppermute x4, starting transfers between devices, mirror(): lax.ppermute(block, 'pipe', [(i, slots - 1 - i) for i in range(slots)])  10.7 us
    ppermute x9, waiting for transfers between devices, swap(): return lax.ppermute(block, 'dp', [(i, i ^ distance) for i in range(ways)])  10.1 us
    ppermute x4, waiting for transfers between devices, mirror(): lax.ppermute(block, 'pipe', [(i, slots - 1 - i) for i in range(slots)])  4.48 us
    pallas_call x13, Pallas kernels, blocks(): pl.pallas_call(functools.partial(blocks_kernel, static, len(operands), wi...  1.94 us
    pallas_call x1, Pallas kernels, front(): pl.pallas_call(functools.partial(front_kernel, flip, width), out_shape=(j...  1.85 us
    pallas_call x1, Pallas kernels, finish(): pl.pallas_call(functools.partial(finish_kernel, static, len(operands)), o...  0.87 us
  transfers between devices with their start and end apart: 13, of which 7 were waited for; matrix products, arithmetic and copies ran while one was open for 0% of the time, Pallas kernels for 5%

profile of v6, /device:TPU:0, one launch (start us, length us, event | category | flops | bytes accessed | tf_op | source)
XLA Modules:
  0.0 42.9 jit_solution(9835215825635092556)
XLA Ops:
  0.0 1.8 %front.1 = (bf16[2,128,128]{2,1,0:T(8,128)(2,1)S(1)}, f32[2,128,768]{2,1,0:T(8,128)S(1)}) custom-call(bf16[2,1,128,6144]{3,2,1,0:T(8,128)(2,1)} %refs_0_.25, bf16[2,1,128,128]{3,2,1,0:T(8,128)(2,1)} %queries.1, bf16[2,1,128,128]{3,2,1,0:T(8,128)(2,1)} %keys.1, bf16[2,1,128,128]{3,2,1,0:T(8,128)(2,1)} %grad_out.1, s32[2,1,1,128]{3,2,1,0:T(1,128)} %segs.1), custom_call_target="tpu_custom_call" | custom-call | flops 10000000000 | bytes 1000 | tf_op jit(solution)/shard_map/front/pallas_call | solution.py:82
  1.9 0.5 %collective-permute-start = (f32[2,128,768]{2,1,0:T(8,128)S(1)}, f32[2,128,768]{2,1,0:T(8,128)S(1)}, u32[]{:S(2)}, u32[]{:S(2)}) collective-permute-start(f32[2,128,768]{2,1,0:T(8,128)S(1)} %get-tuple-element.37), channel_id=1, source_target_pairs={{0,1},{1,0},{2,3},{3,2},{4,5},{5,4},{6,7},{7,6},{8,9},{9,8},{10,11... | collective-permute-start | bytes 2359304 | tf_op jit(solution)/shard_map/ppermute | solution.py:294
  2.4 0.5 %theirs.1 = (f32[6,128,768]{2,1,0:T(8,128)S(1)}, f32[8,128]{1,0:T(8,128)S(1)}) custom-call(bf16[2,1,128,6144]{3,2,1,0:T(8,128)(2,1)S(1)} %copy-done, bf16[2,128,128]{2,1,0:T(8,128)(2,1)S(1)} %get-tuple-element.36.refs_1_), custom_call_target="tpu_custom_call" | custom-call | flops 10000000000 | bytes 1000 | tf_op jit(solution)/shard_map/theirs/pallas_call | solution.py:177
  2.8 0.3 collective-permute-start.1
  3.1 1.2 %collective-permute-done.refs_2_ = f32[2,128,768]{2,1,0:T(8,128)S(1)} collective-permute-done((f32[2,128,768]{2,1,0:T(8,128)S(1)}, f32[2,128,768]{2,1,0:T(8,128)S(1)}, u32[]{:S(2)}, u32[]{:S(2)}) %collective-permute-start) | collective-permute-done | bytes 786464 | tf_op jit(solution)/shard_map/ppermute | solution.py:294
  4.3 0.2 upper.4
  4.5 3.9 %collective-permute-start.3 = (f32[1,64,768]{2,1,0:T(8,128)S(1)}, f32[1,64,768]{2,1,0:T(8,128)S(1)}, u32[]{:S(2)}, u32[]{:S(2)}) collective-permute-start(f32[1,64,768]{2,1,0:T(8,128)S(1)} %get-tuple-element.47), channel_id=1, source_target_pairs={{0,24},{8,16},{16,8},{24,0},{1,25},{9,17},{17,9},{25,1},{2,26},{10... | collective-permute-start | bytes 589832 | tf_op jit(solution)/shard_map/ppermute | solution.py:297
  8.3 0.2 raw.2
  8.5 1.6 %collective-permute-start.5 = (f32[1,64,768]{2,1,0:T(8,128)S(1)}, f32[1,64,768]{2,1,0:T(8,128)S(1)}, u32[]{:S(2)}, u32[]{:S(2)}) collective-permute-start(f32[1,64,768]{2,1,0:T(8,128)S(1)} %get-tuple-element.50), channel_id=1, source_target_pairs={{0,2},{1,3},{2,0},{3,1},{4,6},{5,7},{6,4},{7,5},{8,10},{9,11},{10,... | collective-permute-start | bytes 589832 | tf_op jit(solution)/shard_map/ppermute | solution.py:294
  10.2 0.0 collective-permute-done.1.refs_2_.refs_3_
  10.2 0.2 upper.5
  10.4 1.4 %collective-permute-start.2 = (f32[2,64,768]{2,1,0:T(8,128)S(1)}, f32[2,64,768]{2,1,0:T(8,128)S(1)}, u32[]{:S(2)}, u32[]{:S(2)}) collective-permute-start(f32[2,64,768]{2,1,0:T(8,128)S(1)} %get-tuple-element.45), channel_id=1, source_target_pairs={{0,24},{8,16},{16,8},{24,0},{1,25},{9,17},{17,9},{25,1},{2,26},{10... | collective-permute-start | bytes 1179656 | tf_op jit(solution)/shard_map/ppermute | solution.py:297
  11.8 0.4 base.1
  12.1 1.4 %collective-permute-done.3.refs_3_ = f32[1,64,768]{2,1,0:T(8,128)S(1)} collective-permute-done((f32[1,64,768]{2,1,0:T(8,128)S(1)}, f32[1,64,768]{2,1,0:T(8,128)S(1)}, u32[]{:S(2)}, u32[]{:S(2)}) %collective-permute-start.3) | collective-permute-done | bytes 196640 | tf_op jit(solution)/shard_map/ppermute | solution.py:297
  13.6 2.6 %collective-permute-start.4 = (f32[1,64,768]{2,1,0:T(8,128)S(1)}, f32[1,64,768]{2,1,0:T(8,128)S(1)}, u32[]{:S(2)}, u32[]{:S(2)}) collective-permute-start(f32[1,64,768]{2,1,0:T(8,128)S(1)} %get-tuple-element.49), channel_id=1, source_target_pairs={{0,2},{1,3},{2,0},{3,1},{4,6},{5,7},{6,4},{7,5},{8,10},{9,11},{10,... | collective-permute-start | bytes 589832 | tf_op jit(solution)/shard_map/ppermute | solution.py:294
  16.2 0.1 collective-permute-start.9
  16.2 0.0 collective-permute-done.5.refs_3_
  16.2 0.2 upper.6
  16.5 2.9 %collective-permute-start.10 = (f32[2,64,768]{2,1,0:T(8,128)S(1)}, f32[2,64,768]{2,1,0:T(8,128)S(1)}, u32[]{:S(2)}, u32[]{:S(2)}) collective-permute-start(f32[2,64,768]{2,1,0:T(8,128)S(1)} %get-tuple-element.61), channel_id=1, source_target_pairs={{0,24},{8,16},{16,8},{24,0},{1,25},{9,17},{17,9},{25,1},{2,26},{10... | collective-permute-start | bytes 1179656 | tf_op jit(solution)/shard_map/ppermute | solution.py:297
  19.4 2.6 %collective-permute-done.4.refs_4_ = f32[1,64,768]{2,1,0:T(8,128)S(1)} collective-permute-done((f32[1,64,768]{2,1,0:T(8,128)S(1)}, f32[1,64,768]{2,1,0:T(8,128)S(1)}, u32[]{:S(2)}, u32[]{:S(2)}) %collective-permute-start.4) | collective-permute-done | bytes 196640 | tf_op jit(solution)/shard_map/ppermute | solution.py:294
  22.0 1.4 %collective-permute-done.2.refs_3_ = f32[2,64,768]{2,1,0:T(8,128)S(1)} collective-permute-done((f32[2,64,768]{2,1,0:T(8,128)S(1)}, f32[2,64,768]{2,1,0:T(8,128)S(1)}, u32[]{:S(2)}, u32[]{:S(2)}) %collective-permute-start.2) | collective-permute-done | bytes 393248 | tf_op jit(solution)/shard_map/ppermute | solution.py:297
  23.4 2.7 %collective-permute-start.6 = (f32[1,64,768]{2,1,0:T(8,128)S(1)}, f32[1,64,768]{2,1,0:T(8,128)S(1)}, u32[]{:S(2)}, u32[]{:S(2)}) collective-permute-start(f32[1,64,768]{2,1,0:T(8,128)S(1)} %get-tuple-element.54), channel_id=1, source_target_pairs={{0,4},{1,5},{2,6},{3,7},{4,0},{5,1},{6,2},{7,3},{8,12},{9,13},{10,... | collective-permute-start | bytes 589832 | tf_op jit(solution)/shard_map/ppermute | solution.py:294
  26.1 1.2 %collective-permute-start.7 = (f32[1,64,768]{2,1,0:T(8,128)S(1)}, f32[1,64,768]{2,1,0:T(8,128)S(1)}, u32[]{:S(2)}, u32[]{:S(2)}) collective-permute-start(f32[1,64,768]{2,1,0:T(8,128)S(1)} %get-tuple-element.57), channel_id=1, source_target_pairs={{0,2},{1,3},{2,0},{3,1},{4,6},{5,7},{6,4},{7,5},{8,10},{9,11},{10,... | collective-permute-start | bytes 589832 | tf_op jit(solution)/shard_map/ppermute | solution.py:294
  27.3 0.2 upper.7
  27.5 2.5 %collective-permute-start.8 = (f32[1,128,768]{2,1,0:T(8,128)S(1)}, f32[1,128,768]{2,1,0:T(8,128)S(1)}, u32[]{:S(2)}, u32[]{:S(2)}) collective-permute-start(f32[1,128,768]{2,1,0:T(8,128)S(1)} %get-tuple-element.59), channel_id=1, source_target_pairs={{0,24},{8,16},{16,8},{24,0},{1,25},{9,17},{17,9},{25,1},{2,26},{10... | collective-permute-start | bytes 1179656 | tf_op jit(solution)/shard_map/ppermute | solution.py:297
  30.0 1.6 %collective-permute-done.10.refs_4_.refs_3_ = f32[2,64,768]{2,1,0:T(8,128)S(1)} collective-permute-done((f32[2,64,768]{2,1,0:T(8,128)S(1)}, f32[2,64,768]{2,1,0:T(8,128)S(1)}, u32[]{:S(2)}, u32[]{:S(2)}) %collective-permute-start.10) | collective-permute-done | bytes 393248 | tf_op jit(solution)/shard_map/ppermute | solution.py:297
  31.7 2.8 %collective-permute-start.11 = (f32[1,64,768]{2,1,0:T(8,128)S(1)}, f32[1,64,768]{2,1,0:T(8,128)S(1)}, u32[]{:S(2)}, u32[]{:S(2)}) collective-permute-start(f32[1,64,768]{2,1,0:T(8,128)S(1)} %get-tuple-element.63), channel_id=1, source_target_pairs={{0,4},{1,5},{2,6},{3,7},{4,0},{5,1},{6,2},{7,3},{8,12},{9,13},{10,... | collective-permute-start | bytes 589832 | tf_op jit(solution)/shard_map/ppermute | solution.py:294
  34.5 1.2 %collective-permute-start.12 = (f32[1,64,768]{2,1,0:T(8,128)S(1)}, f32[1,64,768]{2,1,0:T(8,128)S(1)}, u32[]{:S(2)}, u32[]{:S(2)}) collective-permute-start(f32[1,64,768]{2,1,0:T(8,128)S(1)} %get-tuple-element.65), channel_id=1, source_target_pairs={{0,2},{1,3},{2,0},{3,1},{4,6},{5,7},{6,4},{7,5},{8,10},{9,11},{10,... | collective-permute-start | bytes 589832 | tf_op jit(solution)/shard_map/ppermute | solution.py:294
  35.7 0.0 collective-permute-done.7.refs_2_
  35.7 5.8 %collective-permute-done.11.refs_4_ = f32[1,64,768]{2,1,0:T(8,128)S(1)} collective-permute-done((f32[1,64,768]{2,1,0:T(8,128)S(1)}, f32[1,64,768]{2,1,0:T(8,128)S(1)}, u32[]{:S(2)}, u32[]{:S(2)}) %collective-permute-start.11) | collective-permute-done | bytes 196640 | tf_op jit(solution)/shard_map/ppermute | solution.py:294
  41.5 0.5 %collective-permute-done.12.refs_5_ = f32[1,64,768]{2,1,0:T(8,128)S(1)} collective-permute-done((f32[1,64,768]{2,1,0:T(8,128)S(1)}, f32[1,64,768]{2,1,0:T(8,128)S(1)}, u32[]{:S(2)}, u32[]{:S(2)}) %collective-permute-start.12) | collective-permute-done | bytes 196640 | tf_op jit(solution)/shard_map/ppermute | solution.py:294
  42.1 0.9 %finish.1 = bf16[1,768,128]{2,1,0:T(8,128)(2,1)} custom-call(f32[1,128,768]{2,1,0:T(8,128)S(1)} %get-tuple-element.43.refs_0_, f32[1,64,768]{2,1,0:T(8,128)S(1)} %collective-permute-done.6.refs_1_, f32[1,64,768]{2,1,0:T(8,128)S(1)} %collective-permute-done.7.refs_2_, f32[1,128,768]{2,1,0:T(8,128)S(1)} %collective-permute-done.8.refs_3_, ...), custom_call_target="tpu_custom_call" | custom-call | flops 10000000000 | bytes 1000 | tf_op jit(solution)/shard_map/finish/pallas_call | solution.py:212
  (11 shorter events, 0.2 us)
Async XLA Ops:
  0.0 2.4 %copy-start = (bf16[2,1,128,6144]{3,2,1,0:T(8,128)(2,1)S(1)}, bf16[2,1,128,6144]{3,2,1,0:T(8,128)(2,1)}, u32[]{:S(2)}) copy-start(bf16[2,1,128,6144]{3,2,1,0:T(8,128)(2,1)} %refs_0_.25) | copy-start | bytes 9437188
  1.9 2.4 %collective-permute-start = (f32[2,128,768]{2,1,0:T(8,128)S(1)}, f32[2,128,768]{2,1,0:T(8,128)S(1)}, u32[]{:S(2)}, u32[]{:S(2)}) collective-permute-start(f32[2,128,768]{2,1,0:T(8,128)S(1)} %get-tuple-element.37), channel_id=1, source_target_pairs={{0,1},{1,0},{2,3},{3,2},{4,5},{5,4},{6,7},{7,6},{8,9},{9,8},{10,11... | collective-permute-start | bytes 2359304 | tf_op jit(solution)/shard_map/ppermute | solution.py:294
  2.8 7.3 %collective-permute-start.1 = (f32[6,128,768]{2,1,0:T(8,128)S(1)}, f32[6,128,768]{2,1,0:T(8,128)S(1)}, u32[]{:S(2)}, u32[]{:S(2)}) collective-permute-start(f32[6,128,768]{2,1,0:T(8,128)S(1)} %get-tuple-element.38), channel_id=1, source_target_pairs={{0,1},{1,0},{2,3},{3,2},{4,5},{5,4},{6,7},{7,6},{8,9},{9,8},{10,11... | collective-permute-start | bytes 7077896 | tf_op jit(solution)/shard_map/ppermute | solution.py:294
  4.5 9.1 %collective-permute-start.3 = (f32[1,64,768]{2,1,0:T(8,128)S(1)}, f32[1,64,768]{2,1,0:T(8,128)S(1)}, u32[]{:S(2)}, u32[]{:S(2)}) collective-permute-start(f32[1,64,768]{2,1,0:T(8,128)S(1)} %get-tuple-element.47), channel_id=1, source_target_pairs={{0,24},{8,16},{16,8},{24,0},{1,25},{9,17},{17,9},{25,1},{2,26},{10... | collective-permute-start | bytes 589832 | tf_op jit(solution)/shard_map/ppermute | solution.py:297
  8.5 7.7 %collective-permute-start.5 = (f32[1,64,768]{2,1,0:T(8,128)S(1)}, f32[1,64,768]{2,1,0:T(8,128)S(1)}, u32[]{:S(2)}, u32[]{:S(2)}) collective-permute-start(f32[1,64,768]{2,1,0:T(8,128)S(1)} %get-tuple-element.50), channel_id=1, source_target_pairs={{0,2},{1,3},{2,0},{3,1},{4,6},{5,7},{6,4},{7,5},{8,10},{9,11},{10,... | collective-permute-start | bytes 589832 | tf_op jit(solution)/shard_map/ppermute | solution.py:294
  10.4 13.0 %collective-permute-start.2 = (f32[2,64,768]{2,1,0:T(8,128)S(1)}, f32[2,64,768]{2,1,0:T(8,128)S(1)}, u32[]{:S(2)}, u32[]{:S(2)}) collective-permute-start(f32[2,64,768]{2,1,0:T(8,128)S(1)} %get-tuple-element.45), channel_id=1, source_target_pairs={{0,24},{8,16},{16,8},{24,0},{1,25},{9,17},{17,9},{25,1},{2,26},{10... | collective-permute-start | bytes 1179656 | tf_op jit(solution)/shard_map/ppermute | solution.py:297
  13.6 8.4 %collective-permute-start.4 = (f32[1,64,768]{2,1,0:T(8,128)S(1)}, f32[1,64,768]{2,1,0:T(8,128)S(1)}, u32[]{:S(2)}, u32[]{:S(2)}) collective-permute-start(f32[1,64,768]{2,1,0:T(8,128)S(1)} %get-tuple-element.49), channel_id=1, source_target_pairs={{0,2},{1,3},{2,0},{3,1},{4,6},{5,7},{6,4},{7,5},{8,10},{9,11},{10,... | collective-permute-start | bytes 589832 | tf_op jit(solution)/shard_map/ppermute | solution.py:294
  16.2 13.8 %collective-permute-start.9 = (f32[1,64,768]{2,1,0:T(8,128)S(1)}, f32[1,64,768]{2,1,0:T(8,128)S(1)}, u32[]{:S(2)}, u32[]{:S(2)}) collective-permute-start(f32[1,64,768]{2,1,0:T(8,128)S(1)} %get-tuple-element.60), channel_id=1, source_target_pairs={{0,2},{1,3},{2,0},{3,1},{4,6},{5,7},{6,4},{7,5},{8,10},{9,11},{10,... | collective-permute-start | bytes 589832 | tf_op jit(solution)/shard_map/ppermute | solution.py:294
  16.5 15.2 %collective-permute-start.10 = (f32[2,64,768]{2,1,0:T(8,128)S(1)}, f32[2,64,768]{2,1,0:T(8,128)S(1)}, u32[]{:S(2)}, u32[]{:S(2)}) collective-permute-start(f32[2,64,768]{2,1,0:T(8,128)S(1)} %get-tuple-element.61), channel_id=1, source_target_pairs={{0,24},{8,16},{16,8},{24,0},{1,25},{9,17},{17,9},{25,1},{2,26},{10... | collective-permute-start | bytes 1179656 | tf_op jit(solution)/shard_map/ppermute | solution.py:297
  23.4 12.3 %collective-permute-start.6 = (f32[1,64,768]{2,1,0:T(8,128)S(1)}, f32[1,64,768]{2,1,0:T(8,128)S(1)}, u32[]{:S(2)}, u32[]{:S(2)}) collective-permute-start(f32[1,64,768]{2,1,0:T(8,128)S(1)} %get-tuple-element.54), channel_id=1, source_target_pairs={{0,4},{1,5},{2,6},{3,7},{4,0},{5,1},{6,2},{7,3},{8,12},{9,13},{10,... | collective-permute-start | bytes 589832 | tf_op jit(solution)/shard_map/ppermute | solution.py:294
  26.1 9.6 %collective-permute-start.7 = (f32[1,64,768]{2,1,0:T(8,128)S(1)}, f32[1,64,768]{2,1,0:T(8,128)S(1)}, u32[]{:S(2)}, u32[]{:S(2)}) collective-permute-start(f32[1,64,768]{2,1,0:T(8,128)S(1)} %get-tuple-element.57), channel_id=1, source_target_pairs={{0,2},{1,3},{2,0},{3,1},{4,6},{5,7},{6,4},{7,5},{8,10},{9,11},{10,... | collective-permute-start | bytes 589832 | tf_op jit(solution)/shard_map/ppermute | solution.py:294
  27.5 14.6 %collective-permute-start.8 = (f32[1,128,768]{2,1,0:T(8,128)S(1)}, f32[1,128,768]{2,1,0:T(8,128)S(1)}, u32[]{:S(2)}, u32[]{:S(2)}) collective-permute-start(f32[1,128,768]{2,1,0:T(8,128)S(1)} %get-tuple-element.59), channel_id=1, source_target_pairs={{0,24},{8,16},{16,8},{24,0},{1,25},{9,17},{17,9},{25,1},{2,26},{10... | collective-permute-start | bytes 1179656 | tf_op jit(solution)/shard_map/ppermute | solution.py:297
  31.7 9.8 %collective-permute-start.11 = (f32[1,64,768]{2,1,0:T(8,128)S(1)}, f32[1,64,768]{2,1,0:T(8,128)S(1)}, u32[]{:S(2)}, u32[]{:S(2)}) collective-permute-start(f32[1,64,768]{2,1,0:T(8,128)S(1)} %get-tuple-element.63), channel_id=1, source_target_pairs={{0,4},{1,5},{2,6},{3,7},{4,0},{5,1},{6,2},{7,3},{8,12},{9,13},{10,... | collective-permute-start | bytes 589832 | tf_op jit(solution)/shard_map/ppermute | solution.py:294
  34.5 7.5 %collective-permute-start.12 = (f32[1,64,768]{2,1,0:T(8,128)S(1)}, f32[1,64,768]{2,1,0:T(8,128)S(1)}, u32[]{:S(2)}, u32[]{:S(2)}) collective-permute-start(f32[1,64,768]{2,1,0:T(8,128)S(1)} %get-tuple-element.65), channel_id=1, source_target_pairs={{0,2},{1,3},{2,0},{3,1},{4,6},{5,7},{6,4},{7,5},{8,10},{9,11},{10,... | collective-permute-start | bytes 589832 | tf_op jit(solution)/shard_map/ppermute | solution.py:294

commit v7 on v6

--- a/solution.py
+++ b/solution.py
@@ -8,7 +8,7 @@
 from jax.sharding import PartitionSpec as P
 
 VMEM = pl.BlockSpec(memory_space=pltpu.VMEM)
-SOON = pl.CostEstimate(flops=10_000_000_000, bytes_accessed=1000, transcendentals=0)
+SOON = pl.CostEstimate(flops=25_000_000_000, bytes_accessed=1000, transcendentals=0)
 SMALL = pltpu.CompilerParams(vmem_limit_bytes=8 << 20)
 
 
@@ -49,7 +49,7 @@
 
 def front_kernel(flip, width, acts, queries, keys, grad_out, segs, grads, first, *scratch):
     columns, ready = scratch[0], scratch[-1]
-    sources = [queries, keys, grad_out, segs, acts.at[:, 0, :, block_columns(flip, width)]]
+    sources = [queries, keys, grad_out, segs, acts.at[1, 0, :, block_columns(flip, width)]]
     holders = [*scratch[1:-1], columns]
     copies = [
         pltpu.make_async_copy(source, holder, ready.at[i])
@@ -63,8 +63,7 @@
     for half in range(2):
         grads[half] = made[half]
     copies[-1].wait()
-    for slab in range(2):
-        first[slab] = jnp.dot(made[1 - slab], columns[1 - slab], preferred_element_type=jnp.float32)
+    first[0] = jnp.dot(made[1], columns[...], preferred_element_type=jnp.float32)
 
 
 def front(activations, queries, keys, grad_out, segment_ids, flip, width):
@@ -72,23 +71,19 @@
     if width % 128:
         small = (queries, keys, grad_out, segment_ids)
         grads = jnp.stack(grad_v_columns(*([x[half, 0] for half in range(2)] for x in small)))
-        return grads, *plain_blocks(
-            activations,
-            grads,
-            width,
-            [[(slab, 0, head, [(DOT, 1 - slab, flip, 0)]) for slab in range(2)]],
-        )
+        plan = [[(0, 0, head, [(DOT, 1, flip, 0)])]]
+        return grads, *plain_blocks(activations, grads, width, plan)
     small = (queries, keys, grad_out, segment_ids)
     return pl.pallas_call(
         functools.partial(front_kernel, flip, width),
         out_shape=(
             jax.ShapeDtypeStruct((2, head, length), jnp.bfloat16),
-            jax.ShapeDtypeStruct((2, head, width), jnp.float32),
+            jax.ShapeDtypeStruct((1, head, width), jnp.float32),
         ),
         in_specs=[pl.BlockSpec(memory_space=pltpu.HBM)] * 5,
         out_specs=(VMEM, VMEM),
         scratch_shapes=[
-            pltpu.VMEM((2, length, width), activations.dtype),
+            pltpu.VMEM((length, width), activations.dtype),
             *(pltpu.VMEM(value.shape, value.dtype) for value in small),
             pltpu.SemaphoreType.DMA((5,)),
         ],
@@ -259,9 +254,9 @@
     last = chips - 1
     half = head // 2
     everything = list(reversed(range(chips)))
-    pairs = [(1, block) for block in everything[1:]] + [(0, block) for block in everything[1:]]
+    pairs = [(1, block) for block in everything[1:]] + [(0, block) for block in everything]
     if chips < 4:
-        events = [("core", *pairs)] if pairs else []
+        events = [("core", *pairs)]
         events += [("up", (block, 0, head)) for block in everything] + [("base", *everything)]
         return events + [("down", (block, 0, head)) for block in everything[:-1]]
     events = [
@@ -300,9 +295,7 @@
         activations, queries, keys, grad_out, segment_ids, 2 * last + 1, width
     )
     lower, upper = Section(0, chips), Section(1, chips)
-    got = swap(first, 1)
-    for section in (upper, lower):
-        section.add(last, 0, head, got, 1 - section.half)
+    upper.add(last, 0, head, swap(first, 1))
     token = None
 
     def make(name, plan):

time: 43.1 us -> 42.6 us (0.988)
  starting transfers between devices: 23.6 us -> 21.4 us
  waiting for transfers between devices: 14.6 us -> 16.3 us
    ppermute x9, starting transfers between devices: 12.9 us -> 11.7 us  [swap(): return lax.ppermute(block, 'dp', [(i, i ^ distance) for i in range(ways)])]
    ppermute x4, starting transfers between devices: 10.7 us -> 9.68 us  [mirror(): lax.ppermute(block, 'pipe', [(i, slots - 1 - i) for i in range(slots)])]
    ppermute x4, waiting for transfers between devices: 4.48 us -> 5.41 us  [mirror(): lax.ppermute(block, 'pipe', [(i, slots - 1 - i) for i in range(slots)])]
    ppermute x9, waiting for transfers between devices: 10.1 us -> 10.9 us  [swap(): return lax.ppermute(block, 'dp', [(i, i ^ distance) for i in range(ways)])]
  transfers between devices with their start and end apart: 13 -> 13, of which waited for: 7 -> 6; matrix products, arithmetic and copies ran while one was open for 0% -> 0% of each run, Pallas kernels for 5% -> 5%
where the time goes in v7:
time: 42.6 us; the launch traced here: 42.5 us
  starting transfers between devices  21.4 us (50%)
  waiting for transfers between devices  16.3 us (38%)
  Pallas kernels  4.65 us (11%)
    ppermute x9, starting transfers between devices, swap(): return lax.ppermute(block, 'dp', [(i, i ^ distance) for i in range(ways)])  11.7 us
    ppermute x9, waiting for transfers between devices, swap(): return lax.ppermute(block, 'dp', [(i, i ^ distance) for i in range(ways)])  10.9 us
    ppermute x4, starting transfers between devices, mirror(): lax.ppermute(block, 'pipe', [(i, slots - 1 - i) for i in range(slots)])  9.68 us
    ppermute x4, waiting for transfers between devices, mirror(): lax.ppermute(block, 'pipe', [(i, slots - 1 - i) for i in range(slots)])  5.41 us
    pallas_call x13, Pallas kernels, blocks(): pl.pallas_call(functools.partial(blocks_kernel, static, len(operands), wi...  1.97 us
    pallas_call x1, Pallas kernels, front(): pl.pallas_call(functools.partial(front_kernel, flip, width), out_shape=(j...  1.83 us
  transfers between devices with their start and end apart: 13, of which 6 were waited for; matrix products, arithmetic and copies ran while one was open for 0% of the time, Pallas kernels for 5%

profile of v7, /device:TPU:0, one launch (start us, length us, event | category | flops | bytes accessed | tf_op | source)
XLA Modules:
  0.0 42.5 jit_solution(3899622587986328215)
XLA Ops:
  0.0 1.8 %front.1 = (bf16[2,128,128]{2,1,0:T(8,128)(2,1)S(1)}, f32[1,128,768]{2,1,0:T(8,128)S(1)}) custom-call(bf16[2,1,128,6144]{3,2,1,0:T(8,128)(2,1)} %refs_0_.25, bf16[2,1,128,128]{3,2,1,0:T(8,128)(2,1)} %queries.1, bf16[2,1,128,128]{3,2,1,0:T(8,128)(2,1)} %keys.1, bf16[2,1,128,128]{3,2,1,0:T(8,128)(2,1)} %grad_out.1, s32[2,1,1,128]{3,2,1,0:T(1,128)} %segs.1), custom_call_target="tpu_custom_call" | custom-call | flops 24999999488 | bytes 1000 | tf_op jit(solution)/shard_map/front/pallas_call | solution.py:77
  1.8 0.5 %collective-permute-start.1 = (f32[1,128,768]{2,1,0:T(8,128)S(1)}, f32[1,128,768]{2,1,0:T(8,128)S(1)}, u32[]{:S(2)}, u32[]{:S(2)}) collective-permute-start(f32[1,128,768]{2,1,0:T(8,128)S(1)} %get-tuple-element.38), channel_id=1, source_target_pairs={{0,1},{1,0},{2,3},{3,2},{4,5},{5,4},{6,7},{7,6},{8,9},{9,8},{10,11... | collective-permute-start | bytes 1179656 | tf_op jit(solution)/shard_map/ppermute | solution.py:289
  2.4 0.5 %theirs.1 = (f32[7,128,768]{2,1,0:T(8,128)S(1)}, f32[8,128]{1,0:T(8,128)S(1)}) custom-call(bf16[2,1,128,6144]{3,2,1,0:T(8,128)(2,1)S(1)} %copy-done, bf16[2,128,128]{2,1,0:T(8,128)(2,1)S(1)} %get-tuple-element.36.refs_1_), custom_call_target="tpu_custom_call" | custom-call | flops 24999999488 | bytes 1000 | tf_op jit(solution)/shard_map/theirs/pallas_call | solution.py:172
  2.9 0.3 collective-permute-start
  3.1 0.6 %collective-permute-done.1.refs_2_ = f32[1,128,768]{2,1,0:T(8,128)S(1)} collective-permute-done((f32[1,128,768]{2,1,0:T(8,128)S(1)}, f32[1,128,768]{2,1,0:T(8,128)S(1)}, u32[]{:S(2)}, u32[]{:S(2)}) %collective-permute-start.1) | collective-permute-done | bytes 393248 | tf_op jit(solution)/shard_map/ppermute | solution.py:289
  3.7 0.2 upper.4
  3.9 0.2 raw.2
  4.1 3.0 %collective-permute-start.5 = (f32[1,64,768]{2,1,0:T(8,128)S(1)}, f32[1,64,768]{2,1,0:T(8,128)S(1)}, u32[]{:S(2)}, u32[]{:S(2)}) collective-permute-start(f32[1,64,768]{2,1,0:T(8,128)S(1)} %get-tuple-element.50), channel_id=1, source_target_pairs={{0,2},{1,3},{2,0},{3,1},{4,6},{5,7},{6,4},{7,5},{8,10},{9,11},{10,... | collective-permute-start | bytes 589832 | tf_op jit(solution)/shard_map/ppermute | solution.py:289
  7.1 2.4 %collective-permute-start.3 = (f32[1,64,768]{2,1,0:T(8,128)S(1)}, f32[1,64,768]{2,1,0:T(8,128)S(1)}, u32[]{:S(2)}, u32[]{:S(2)}) collective-permute-start(f32[1,64,768]{2,1,0:T(8,128)S(1)} %get-tuple-element.47), channel_id=1, source_target_pairs={{0,24},{8,16},{16,8},{24,0},{1,25},{9,17},{17,9},{25,1},{2,26},{10... | collective-permute-start | bytes 589832 | tf_op jit(solution)/shard_map/ppermute | solution.py:292
  9.5 0.0 collective-permute-done.refs_2_
  9.5 0.2 upper.5
  9.7 2.2 %collective-permute-start.2 = (f32[2,64,768]{2,1,0:T(8,128)S(1)}, f32[2,64,768]{2,1,0:T(8,128)S(1)}, u32[]{:S(2)}, u32[]{:S(2)}) collective-permute-start(f32[2,64,768]{2,1,0:T(8,128)S(1)} %get-tuple-element.45), channel_id=1, source_target_pairs={{0,24},{8,16},{16,8},{24,0},{1,25},{9,17},{17,9},{25,1},{2,26},{10... | collective-permute-start | bytes 1179656 | tf_op jit(solution)/shard_map/ppermute | solution.py:292
  11.9 0.4 base.1
  12.3 3.4 %collective-permute-done.3.refs_3_ = f32[1,64,768]{2,1,0:T(8,128)S(1)} collective-permute-done((f32[1,64,768]{2,1,0:T(8,128)S(1)}, f32[1,64,768]{2,1,0:T(8,128)S(1)}, u32[]{:S(2)}, u32[]{:S(2)}) %collective-permute-start.3) | collective-permute-done | bytes 196640 | tf_op jit(solution)/shard_map/ppermute | solution.py:292
  15.8 0.1 collective-permute-start.9
  15.9 2.0 %collective-permute-start.4 = (f32[1,64,768]{2,1,0:T(8,128)S(1)}, f32[1,64,768]{2,1,0:T(8,128)S(1)}, u32[]{:S(2)}, u32[]{:S(2)}) collective-permute-start(f32[1,64,768]{2,1,0:T(8,128)S(1)} %get-tuple-element.49), channel_id=1, source_target_pairs={{0,2},{1,3},{2,0},{3,1},{4,6},{5,7},{6,4},{7,5},{8,10},{9,11},{10,... | collective-permute-start | bytes 589832 | tf_op jit(solution)/shard_map/ppermute | solution.py:289
  17.9 0.2 upper.6
  18.1 2.5 %collective-permute-start.10 = (f32[2,64,768]{2,1,0:T(8,128)S(1)}, f32[2,64,768]{2,1,0:T(8,128)S(1)}, u32[]{:S(2)}, u32[]{:S(2)}) collective-permute-start(f32[2,64,768]{2,1,0:T(8,128)S(1)} %get-tuple-element.61), channel_id=1, source_target_pairs={{0,24},{8,16},{16,8},{24,0},{1,25},{9,17},{17,9},{25,1},{2,26},{10... | collective-permute-start | bytes 1179656 | tf_op jit(solution)/shard_map/ppermute | solution.py:292
  20.6 4.1 %collective-permute-done.4.refs_4_ = f32[1,64,768]{2,1,0:T(8,128)S(1)} collective-permute-done((f32[1,64,768]{2,1,0:T(8,128)S(1)}, f32[1,64,768]{2,1,0:T(8,128)S(1)}, u32[]{:S(2)}, u32[]{:S(2)}) %collective-permute-start.4) | collective-permute-done | bytes 196640 | tf_op jit(solution)/shard_map/ppermute | solution.py:289
  24.8 0.0 collective-permute-done.2.refs_3_
  24.8 0.7 %collective-permute-start.7 = (f32[1,64,768]{2,1,0:T(8,128)S(1)}, f32[1,64,768]{2,1,0:T(8,128)S(1)}, u32[]{:S(2)}, u32[]{:S(2)}) collective-permute-start(f32[1,64,768]{2,1,0:T(8,128)S(1)} %get-tuple-element.57), channel_id=1, source_target_pairs={{0,2},{1,3},{2,0},{3,1},{4,6},{5,7},{6,4},{7,5},{8,10},{9,11},{10,... | collective-permute-start | bytes 589832 | tf_op jit(solution)/shard_map/ppermute | solution.py:289
  25.6 2.4 %collective-permute-start.6 = (f32[1,64,768]{2,1,0:T(8,128)S(1)}, f32[1,64,768]{2,1,0:T(8,128)S(1)}, u32[]{:S(2)}, u32[]{:S(2)}) collective-permute-start(f32[1,64,768]{2,1,0:T(8,128)S(1)} %get-tuple-element.54), channel_id=1, source_target_pairs={{0,4},{1,5},{2,6},{3,7},{4,0},{5,1},{6,2},{7,3},{8,12},{9,13},{10,... | collective-permute-start | bytes 589832 | tf_op jit(solution)/shard_map/ppermute | solution.py:289
  27.9 0.2 upper.7
  28.1 2.5 %collective-permute-start.8 = (f32[1,128,768]{2,1,0:T(8,128)S(1)}, f32[1,128,768]{2,1,0:T(8,128)S(1)}, u32[]{:S(2)}, u32[]{:S(2)}) collective-permute-start(f32[1,128,768]{2,1,0:T(8,128)S(1)} %get-tuple-element.59), channel_id=1, source_target_pairs={{0,24},{8,16},{16,8},{24,0},{1,25},{9,17},{17,9},{25,1},{2,26},{10... | collective-permute-start | bytes 1179656 | tf_op jit(solution)/shard_map/ppermute | solution.py:292
  30.6 2.0 %collective-permute-done.10.refs_4_.refs_3_ = f32[2,64,768]{2,1,0:T(8,128)S(1)} collective-permute-done((f32[2,64,768]{2,1,0:T(8,128)S(1)}, f32[2,64,768]{2,1,0:T(8,128)S(1)}, u32[]{:S(2)}, u32[]{:S(2)}) %collective-permute-start.10) | collective-permute-done | bytes 393248 | tf_op jit(solution)/shard_map/ppermute | solution.py:292
  32.7 0.1 collective-permute-start.12
  32.8 2.7 %collective-permute-start.11 = (f32[1,64,768]{2,1,0:T(8,128)S(1)}, f32[1,64,768]{2,1,0:T(8,128)S(1)}, u32[]{:S(2)}, u32[]{:S(2)}) collective-permute-start(f32[1,64,768]{2,1,0:T(8,128)S(1)} %get-tuple-element.63), channel_id=1, source_target_pairs={{0,4},{1,5},{2,6},{3,7},{4,0},{5,1},{6,2},{7,3},{8,12},{9,13},{10,... | collective-permute-start | bytes 589832 | tf_op jit(solution)/shard_map/ppermute | solution.py:289
  35.4 0.0 collective-permute-done.7.refs_2_
  35.4 5.2 %collective-permute-done.12.refs_5_ = f32[1,64,768]{2,1,0:T(8,128)S(1)} collective-permute-done((f32[1,64,768]{2,1,0:T(8,128)S(1)}, f32[1,64,768]{2,1,0:T(8,128)S(1)}, u32[]{:S(2)}, u32[]{:S(2)}) %collective-permute-start.12) | collective-permute-done | bytes 196640 | tf_op jit(solution)/shard_map/ppermute | solution.py:289
  40.6 1.0 %collective-permute-done.11.refs_4_ = f32[1,64,768]{2,1,0:T(8,128)S(1)} collective-permute-done((f32[1,64,768]{2,1,0:T(8,128)S(1)}, f32[1,64,768]{2,1,0:T(8,128)S(1)}, u32[]{:S(2)}, u32[]{:S(2)}) %collective-permute-start.11) | collective-permute-done | bytes 196640 | tf_op jit(solution)/shard_map/ppermute | solution.py:289
  41.6 0.0 collective-permute-done.8.refs_3_
  41.6 0.9 %finish.1 = bf16[1,768,128]{2,1,0:T(8,128)(2,1)} custom-call(f32[1,128,768]{2,1,0:T(8,128)S(1)} %get-tuple-element.43.refs_0_, f32[1,64,768]{2,1,0:T(8,128)S(1)} %collective-permute-done.6.refs_1_, f32[1,64,768]{2,1,0:T(8,128)S(1)} %collective-permute-done.7.refs_2_, f32[1,128,768]{2,1,0:T(8,128)S(1)} %collective-permute-done.8.refs_3_, ...), custom_call_target="tpu_custom_call" | custom-call | flops 24999999488 | bytes 1000 | tf_op jit(solution)/shard_map/finish/pallas_call | solution.py:207
  (11 shorter events, 0.2 us)
Async XLA Ops:
  0.0 2.4 %copy-start = (bf16[2,1,128,6144]{3,2,1,0:T(8,128)(2,1)S(1)}, bf16[2,1,128,6144]{3,2,1,0:T(8,128)(2,1)}, u32[]{:S(2)}) copy-start(bf16[2,1,128,6144]{3,2,1,0:T(8,128)(2,1)} %refs_0_.25) | copy-start | bytes 9437188
  1.8 1.9 %collective-permute-start.1 = (f32[1,128,768]{2,1,0:T(8,128)S(1)}, f32[1,128,768]{2,1,0:T(8,128)S(1)}, u32[]{:S(2)}, u32[]{:S(2)}) collective-permute-start(f32[1,128,768]{2,1,0:T(8,128)S(1)} %get-tuple-element.38), channel_id=1, source_target_pairs={{0,1},{1,0},{2,3},{3,2},{4,5},{5,4},{6,7},{7,6},{8,9},{9,8},{10,11... | collective-permute-start | bytes 1179656 | tf_op jit(solution)/shard_map/ppermute | solution.py:289
  2.9 6.7 %collective-permute-start = (f32[7,128,768]{2,1,0:T(8,128)S(1)}, f32[7,128,768]{2,1,0:T(8,128)S(1)}, u32[]{:S(2)}, u32[]{:S(2)}) collective-permute-start(f32[7,128,768]{2,1,0:T(8,128)S(1)} %get-tuple-element.37), channel_id=1, source_target_pairs={{0,1},{1,0},{2,3},{3,2},{4,5},{5,4},{6,7},{7,6},{8,9},{9,8},{10,11... | collective-permute-start | bytes 8257544 | tf_op jit(solution)/shard_map/ppermute | solution.py:289
  4.1 13.8 %collective-permute-start.5 = (f32[1,64,768]{2,1,0:T(8,128)S(1)}, f32[1,64,768]{2,1,0:T(8,128)S(1)}, u32[]{:S(2)}, u32[]{:S(2)}) collective-permute-start(f32[1,64,768]{2,1,0:T(8,128)S(1)} %get-tuple-element.50), channel_id=1, source_target_pairs={{0,2},{1,3},{2,0},{3,1},{4,6},{5,7},{6,4},{7,5},{8,10},{9,11},{10,... | collective-permute-start | bytes 589832 | tf_op jit(solution)/shard_map/ppermute | solution.py:289
  7.1 8.7 %collective-permute-start.3 = (f32[1,64,768]{2,1,0:T(8,128)S(1)}, f32[1,64,768]{2,1,0:T(8,128)S(1)}, u32[]{:S(2)}, u32[]{:S(2)}) collective-permute-start(f32[1,64,768]{2,1,0:T(8,128)S(1)} %get-tuple-element.47), channel_id=1, source_target_pairs={{0,24},{8,16},{16,8},{24,0},{1,25},{9,17},{17,9},{25,1},{2,26},{10... | collective-permute-start | bytes 589832 | tf_op jit(solution)/shard_map/ppermute | solution.py:292
  9.7 15.0 %collective-permute-start.2 = (f32[2,64,768]{2,1,0:T(8,128)S(1)}, f32[2,64,768]{2,1,0:T(8,128)S(1)}, u32[]{:S(2)}, u32[]{:S(2)}) collective-permute-start(f32[2,64,768]{2,1,0:T(8,128)S(1)} %get-tuple-element.45), channel_id=1, source_target_pairs={{0,24},{8,16},{16,8},{24,0},{1,25},{9,17},{17,9},{25,1},{2,26},{10... | collective-permute-start | bytes 1179656 | tf_op jit(solution)/shard_map/ppermute | solution.py:292
  15.8 14.8 %collective-permute-start.9 = (f32[1,64,768]{2,1,0:T(8,128)S(1)}, f32[1,64,768]{2,1,0:T(8,128)S(1)}, u32[]{:S(2)}, u32[]{:S(2)}) collective-permute-start(f32[1,64,768]{2,1,0:T(8,128)S(1)} %get-tuple-element.60), channel_id=1, source_target_pairs={{0,2},{1,3},{2,0},{3,1},{4,6},{5,7},{6,4},{7,5},{8,10},{9,11},{10,... | collective-permute-start | bytes 589832 | tf_op jit(solution)/shard_map/ppermute | solution.py:289
  15.9 8.9 %collective-permute-start.4 = (f32[1,64,768]{2,1,0:T(8,128)S(1)}, f32[1,64,768]{2,1,0:T(8,128)S(1)}, u32[]{:S(2)}, u32[]{:S(2)}) collective-permute-start(f32[1,64,768]{2,1,0:T(8,128)S(1)} %get-tuple-element.49), channel_id=1, source_target_pairs={{0,2},{1,3},{2,0},{3,1},{4,6},{5,7},{6,4},{7,5},{8,10},{9,11},{10,... | collective-permute-start | bytes 589832 | tf_op jit(solution)/shard_map/ppermute | solution.py:289
  18.1 14.5 %collective-permute-start.10 = (f32[2,64,768]{2,1,0:T(8,128)S(1)}, f32[2,64,768]{2,1,0:T(8,128)S(1)}, u32[]{:S(2)}, u32[]{:S(2)}) collective-permute-start(f32[2,64,768]{2,1,0:T(8,128)S(1)} %get-tuple-element.61), channel_id=1, source_target_pairs={{0,24},{8,16},{16,8},{24,0},{1,25},{9,17},{17,9},{25,1},{2,26},{10... | collective-permute-start | bytes 1179656 | tf_op jit(solution)/shard_map/ppermute | solution.py:292
  24.8 10.6 %collective-permute-start.7 = (f32[1,64,768]{2,1,0:T(8,128)S(1)}, f32[1,64,768]{2,1,0:T(8,128)S(1)}, u32[]{:S(2)}, u32[]{:S(2)}) collective-permute-start(f32[1,64,768]{2,1,0:T(8,128)S(1)} %get-tuple-element.57), channel_id=1, source_target_pairs={{0,2},{1,3},{2,0},{3,1},{4,6},{5,7},{6,4},{7,5},{8,10},{9,11},{10,... | collective-permute-start | bytes 589832 | tf_op jit(solution)/shard_map/ppermute | solution.py:289
  25.6 9.8 %collective-permute-start.6 = (f32[1,64,768]{2,1,0:T(8,128)S(1)}, f32[1,64,768]{2,1,0:T(8,128)S(1)}, u32[]{:S(2)}, u32[]{:S(2)}) collective-permute-start(f32[1,64,768]{2,1,0:T(8,128)S(1)} %get-tuple-element.54), channel_id=1, source_target_pairs={{0,4},{1,5},{2,6},{3,7},{4,0},{5,1},{6,2},{7,3},{8,12},{9,13},{10,... | collective-permute-start | bytes 589832 | tf_op jit(solution)/shard_map/ppermute | solution.py:289
  28.1 13.5 %collective-permute-start.8 = (f32[1,128,768]{2,1,0:T(8,128)S(1)}, f32[1,128,768]{2,1,0:T(8,128)S(1)}, u32[]{:S(2)}, u32[]{:S(2)}) collective-permute-start(f32[1,128,768]{2,1,0:T(8,128)S(1)} %get-tuple-element.59), channel_id=1, source_target_pairs={{0,24},{8,16},{16,8},{24,0},{1,25},{9,17},{17,9},{25,1},{2,26},{10... | collective-permute-start | bytes 1179656 | tf_op jit(solution)/shard_map/ppermute | solution.py:292
  32.7 7.9 %collective-permute-start.12 = (f32[1,64,768]{2,1,0:T(8,128)S(1)}, f32[1,64,768]{2,1,0:T(8,128)S(1)}, u32[]{:S(2)}, u32[]{:S(2)}) collective-permute-start(f32[1,64,768]{2,1,0:T(8,128)S(1)} %get-tuple-element.65), channel_id=1, source_target_pairs={{0,2},{1,3},{2,0},{3,1},{4,6},{5,7},{6,4},{7,5},{8,10},{9,11},{10,... | collective-permute-start | bytes 589832 | tf_op jit(solution)/shard_map/ppermute | solution.py:289
  32.8 8.9 %collective-permute-start.11 = (f32[1,64,768]{2,1,0:T(8,128)S(1)}, f32[1,64,768]{2,1,0:T(8,128)S(1)}, u32[]{:S(2)}, u32[]{:S(2)}) collective-permute-start(f32[1,64,768]{2,1,0:T(8,128)S(1)} %get-tuple-element.63), channel_id=1, source_target_pairs={{0,4},{1,5},{2,6},{3,7},{4,0},{5,1},{6,2},{7,3},{8,12},{9,13},{10,... | collective-permute-start | bytes 589832 | tf_op jit(solution)/shard_map/ppermute | solution.py:289

commit v8 on v7

--- a/solution.py
+++ b/solution.py
@@ -16,26 +16,26 @@
     length, head = query_rows[0].shape
     count = len(query_rows)
     scores = [
-        lax.dot_general(q, k, (((1,), (1,)), ((), ())), preferred_element_type=jnp.float32)
+        lax.dot_general(k, q, (((1,), (1,)), ((), ())), preferred_element_type=jnp.float32)
         for q, k in zip(query_rows, key_rows)
     ]
-    scores = jnp.concatenate(scores, axis=0) / jnp.sqrt(jnp.float32(head))
+    scores = jnp.concatenate(scores, axis=1) / jnp.sqrt(jnp.float32(head))
     square = (length, length)
     across = [jnp.broadcast_to(row, square) for row in segs]
-    same = jnp.concatenate(across, axis=0) == jnp.concatenate([x.T for x in across], axis=0)
-    before = lax.broadcasted_iota(jnp.int32, square, 1) <= lax.broadcasted_iota(
-        jnp.int32, square, 0
+    same = jnp.concatenate(across, axis=1) == jnp.concatenate([x.T for x in across], axis=1)
+    before = lax.broadcasted_iota(jnp.int32, square, 0) <= lax.broadcasted_iota(
+        jnp.int32, square, 1
     )
-    keep = same & jnp.concatenate([before] * count, axis=0)
+    keep = same & jnp.concatenate([before] * count, axis=1)
     masked = jnp.where(keep, scores, jnp.float32(-1e30))
-    top = jnp.max(masked, axis=1, keepdims=True)
+    top = jnp.max(masked, axis=0, keepdims=True)
     weights = jnp.where(keep, jnp.exp(masked - top), jnp.float32(0.0))
-    probs = (weights / jnp.sum(weights, axis=1, keepdims=True)).astype(jnp.bfloat16)
+    probs = (weights / jnp.sum(weights, axis=0, keepdims=True)).astype(jnp.bfloat16)
     return [
         lax.dot_general(
-            grad,
-            probs[i * length : (i + 1) * length],
-            (((0,), (0,)), ((), ())),
+            grad.astype(jnp.float32).T.astype(jnp.bfloat16),
+            probs[:, i * length : (i + 1) * length],
+            (((1,), (1,)), ((), ())),
             preferred_element_type=jnp.float32,
         ).astype(jnp.bfloat16)
         for i, grad in enumerate(grad_rows)

time: 42.6 us -> 42.5 us (level)
  no operation moved by 1% of the time
where the time goes in v8:
time: 42.5 us; the launch traced here: 42.4 us
  starting transfers between devices  21.6 us (51%)
  waiting for transfers between devices  16.1 us (38%)
  Pallas kernels  4.54 us (11%)
    ppermute x9, starting transfers between devices, swap(): return lax.ppermute(block, 'dp', [(i, i ^ distance) for i in range(ways)])  11.8 us
    ppermute x9, waiting for transfers between devices, swap(): return lax.ppermute(block, 'dp', [(i, i ^ distance) for i in range(ways)])  10.8 us
    ppermute x4, starting transfers between devices, mirror(): lax.ppermute(block, 'pipe', [(i, slots - 1 - i) for i in range(slots)])  9.81 us
    ppermute x4, waiting for transfers between devices, mirror(): lax.ppermute(block, 'pipe', [(i, slots - 1 - i) for i in range(slots)])  5.27 us
    pallas_call x13, Pallas kernels, blocks(): pl.pallas_call(functools.partial(blocks_kernel, static, len(operands), wi...  1.99 us
    pallas_call x1, Pallas kernels, front(): pl.pallas_call(functools.partial(front_kernel, flip, width), out_shape=(j...  1.7 us
    pallas_call x1, Pallas kernels, finish(): pl.pallas_call(functools.partial(finish_kernel, static, len(operands)), o...  0.85 us
  transfers between devices with their start and end apart: 13, of which 6 were waited for; matrix products, arithmetic and copies ran while one was open for 0% of the time, Pallas kernels for 5%

profile of v8, /device:TPU:0, one launch (start us, length us, event | category | flops | bytes accessed | tf_op | source)
XLA Modules:
  0.0 42.4 jit_solution(16153126887070635206)
XLA Ops:
  0.0 1.7 %front.1 = (bf16[2,128,128]{2,1,0:T(8,128)(2,1)S(1)}, f32[1,128,768]{2,1,0:T(8,128)S(1)}) custom-call(bf16[2,1,128,6144]{3,2,1,0:T(8,128)(2,1)} %refs_0_.25, bf16[2,1,128,128]{3,2,1,0:T(8,128)(2,1)} %queries.1, bf16[2,1,128,128]{3,2,1,0:T(8,128)(2,1)} %keys.1, bf16[2,1,128,128]{3,2,1,0:T(8,128)(2,1)} %grad_out.1, s32[2,1,1,128]{3,2,1,0:T(1,128)} %segs.1), custom_call_target="tpu_custom_call" | custom-call | flops 24999999488 | bytes 1000 | tf_op jit(solution)/shard_map/front/pallas_call | solution.py:77
  1.7 0.5 %collective-permute-start.1 = (f32[1,128,768]{2,1,0:T(8,128)S(1)}, f32[1,128,768]{2,1,0:T(8,128)S(1)}, u32[]{:S(2)}, u32[]{:S(2)}) collective-permute-start(f32[1,128,768]{2,1,0:T(8,128)S(1)} %get-tuple-element.38), channel_id=1, source_target_pairs={{0,1},{1,0},{2,3},{3,2},{4,5},{5,4},{6,7},{7,6},{8,9},{9,8},{10,11... | collective-permute-start | bytes 1179656 | tf_op jit(solution)/shard_map/ppermute | solution.py:289
  2.2 0.5 %theirs.1 = (f32[7,128,768]{2,1,0:T(8,128)S(1)}, f32[8,128]{1,0:T(8,128)S(1)}) custom-call(bf16[2,1,128,6144]{3,2,1,0:T(8,128)(2,1)S(1)} %copy-done, bf16[2,128,128]{2,1,0:T(8,128)(2,1)S(1)} %get-tuple-element.36.refs_1_), custom_call_target="tpu_custom_call" | custom-call | flops 24999999488 | bytes 1000 | tf_op jit(solution)/shard_map/theirs/pallas_call | solution.py:172
  2.8 0.4 collective-permute-start
  3.1 0.4 %collective-permute-done.1.refs_2_ = f32[1,128,768]{2,1,0:T(8,128)S(1)} collective-permute-done((f32[1,128,768]{2,1,0:T(8,128)S(1)}, f32[1,128,768]{2,1,0:T(8,128)S(1)}, u32[]{:S(2)}, u32[]{:S(2)}) %collective-permute-start.1) | collective-permute-done | bytes 393248 | tf_op jit(solution)/shard_map/ppermute | solution.py:289
  3.6 0.2 upper.4
  3.7 0.2 raw.2
  3.9 3.0 %collective-permute-start.5 = (f32[1,64,768]{2,1,0:T(8,128)S(1)}, f32[1,64,768]{2,1,0:T(8,128)S(1)}, u32[]{:S(2)}, u32[]{:S(2)}) collective-permute-start(f32[1,64,768]{2,1,0:T(8,128)S(1)} %get-tuple-element.50), channel_id=1, source_target_pairs={{0,2},{1,3},{2,0},{3,1},{4,6},{5,7},{6,4},{7,5},{8,10},{9,11},{10,... | collective-permute-start | bytes 589832 | tf_op jit(solution)/shard_map/ppermute | solution.py:289
  6.9 2.4 %collective-permute-start.3 = (f32[1,64,768]{2,1,0:T(8,128)S(1)}, f32[1,64,768]{2,1,0:T(8,128)S(1)}, u32[]{:S(2)}, u32[]{:S(2)}) collective-permute-start(f32[1,64,768]{2,1,0:T(8,128)S(1)} %get-tuple-element.47), channel_id=1, source_target_pairs={{0,24},{8,16},{16,8},{24,0},{1,25},{9,17},{17,9},{25,1},{2,26},{10... | collective-permute-start | bytes 589832 | tf_op jit(solution)/shard_map/ppermute | solution.py:292
  9.4 0.0 collective-permute-done.refs_2_
  9.4 0.2 upper.5
  9.6 2.3 %collective-permute-start.2 = (f32[2,64,768]{2,1,0:T(8,128)S(1)}, f32[2,64,768]{2,1,0:T(8,128)S(1)}, u32[]{:S(2)}, u32[]{:S(2)}) collective-permute-start(f32[2,64,768]{2,1,0:T(8,128)S(1)} %get-tuple-element.45), channel_id=1, source_target_pairs={{0,24},{8,16},{16,8},{24,0},{1,25},{9,17},{17,9},{25,1},{2,26},{10... | collective-permute-start | bytes 1179656 | tf_op jit(solution)/shard_map/ppermute | solution.py:292
  11.9 0.4 base.1
  12.3 3.3 %collective-permute-done.3.refs_3_ = f32[1,64,768]{2,1,0:T(8,128)S(1)} collective-permute-done((f32[1,64,768]{2,1,0:T(8,128)S(1)}, f32[1,64,768]{2,1,0:T(8,128)S(1)}, u32[]{:S(2)}, u32[]{:S(2)}) %collective-permute-start.3) | collective-permute-done | bytes 196640 | tf_op jit(solution)/shard_map/ppermute | solution.py:292
  15.7 0.1 collective-permute-start.9
  15.8 2.0 %collective-permute-start.4 = (f32[1,64,768]{2,1,0:T(8,128)S(1)}, f32[1,64,768]{2,1,0:T(8,128)S(1)}, u32[]{:S(2)}, u32[]{:S(2)}) collective-permute-start(f32[1,64,768]{2,1,0:T(8,128)S(1)} %get-tuple-element.49), channel_id=1, source_target_pairs={{0,2},{1,3},{2,0},{3,1},{4,6},{5,7},{6,4},{7,5},{8,10},{9,11},{10,... | collective-permute-start | bytes 589832 | tf_op jit(solution)/shard_map/ppermute | solution.py:289
  17.8 0.0 collective-permute-done.5.refs_3_
  17.8 0.2 upper.6
  18.0 2.5 %collective-permute-start.10 = (f32[2,64,768]{2,1,0:T(8,128)S(1)}, f32[2,64,768]{2,1,0:T(8,128)S(1)}, u32[]{:S(2)}, u32[]{:S(2)}) collective-permute-start(f32[2,64,768]{2,1,0:T(8,128)S(1)} %get-tuple-element.61), channel_id=1, source_target_pairs={{0,24},{8,16},{16,8},{24,0},{1,25},{9,17},{17,9},{25,1},{2,26},{10... | collective-permute-start | bytes 1179656 | tf_op jit(solution)/shard_map/ppermute | solution.py:292
  20.5 4.1 %collective-permute-done.4.refs_4_ = f32[1,64,768]{2,1,0:T(8,128)S(1)} collective-permute-done((f32[1,64,768]{2,1,0:T(8,128)S(1)}, f32[1,64,768]{2,1,0:T(8,128)S(1)}, u32[]{:S(2)}, u32[]{:S(2)}) %collective-permute-start.4) | collective-permute-done | bytes 196640 | tf_op jit(solution)/shard_map/ppermute | solution.py:289
  24.6 0.0 collective-permute-done.2.refs_3_
  24.7 0.7 %collective-permute-start.7 = (f32[1,64,768]{2,1,0:T(8,128)S(1)}, f32[1,64,768]{2,1,0:T(8,128)S(1)}, u32[]{:S(2)}, u32[]{:S(2)}) collective-permute-start(f32[1,64,768]{2,1,0:T(8,128)S(1)} %get-tuple-element.57), channel_id=1, source_target_pairs={{0,2},{1,3},{2,0},{3,1},{4,6},{5,7},{6,4},{7,5},{8,10},{9,11},{10,... | collective-permute-start | bytes 589832 | tf_op jit(solution)/shard_map/ppermute | solution.py:289
  25.5 2.4 %collective-permute-start.6 = (f32[1,64,768]{2,1,0:T(8,128)S(1)}, f32[1,64,768]{2,1,0:T(8,128)S(1)}, u32[]{:S(2)}, u32[]{:S(2)}) collective-permute-start(f32[1,64,768]{2,1,0:T(8,128)S(1)} %get-tuple-element.54), channel_id=1, source_target_pairs={{0,4},{1,5},{2,6},{3,7},{4,0},{5,1},{6,2},{7,3},{8,12},{9,13},{10,... | collective-permute-start | bytes 589832 | tf_op jit(solution)/shard_map/ppermute | solution.py:289
  27.8 0.2 upper.7
  28.0 2.5 %collective-permute-start.8 = (f32[1,128,768]{2,1,0:T(8,128)S(1)}, f32[1,128,768]{2,1,0:T(8,128)S(1)}, u32[]{:S(2)}, u32[]{:S(2)}) collective-permute-start(f32[1,128,768]{2,1,0:T(8,128)S(1)} %get-tuple-element.59), channel_id=1, source_target_pairs={{0,24},{8,16},{16,8},{24,0},{1,25},{9,17},{17,9},{25,1},{2,26},{10... | collective-permute-start | bytes 1179656 | tf_op jit(solution)/shard_map/ppermute | solution.py:292
  30.5 0.0 collective-permute-done.9.refs_3_
  30.5 1.9 %collective-permute-done.10.refs_4_.refs_3_ = f32[2,64,768]{2,1,0:T(8,128)S(1)} collective-permute-done((f32[2,64,768]{2,1,0:T(8,128)S(1)}, f32[2,64,768]{2,1,0:T(8,128)S(1)}, u32[]{:S(2)}, u32[]{:S(2)}) %collective-permute-start.10) | collective-permute-done | bytes 393248 | tf_op jit(solution)/shard_map/ppermute | solution.py:292
  32.5 0.1 collective-permute-start.12
  32.6 2.6 %collective-permute-start.11 = (f32[1,64,768]{2,1,0:T(8,128)S(1)}, f32[1,64,768]{2,1,0:T(8,128)S(1)}, u32[]{:S(2)}, u32[]{:S(2)}) collective-permute-start(f32[1,64,768]{2,1,0:T(8,128)S(1)} %get-tuple-element.63), channel_id=1, source_target_pairs={{0,4},{1,5},{2,6},{3,7},{4,0},{5,1},{6,2},{7,3},{8,12},{9,13},{10,... | collective-permute-start | bytes 589832 | tf_op jit(solution)/shard_map/ppermute | solution.py:289
  35.3 5.2 %collective-permute-done.12.refs_5_ = f32[1,64,768]{2,1,0:T(8,128)S(1)} collective-permute-done((f32[1,64,768]{2,1,0:T(8,128)S(1)}, f32[1,64,768]{2,1,0:T(8,128)S(1)}, u32[]{:S(2)}, u32[]{:S(2)}) %collective-permute-start.12) | collective-permute-done | bytes 196640 | tf_op jit(solution)/shard_map/ppermute | solution.py:289
  40.5 1.0 %collective-permute-done.11.refs_4_ = f32[1,64,768]{2,1,0:T(8,128)S(1)} collective-permute-done((f32[1,64,768]{2,1,0:T(8,128)S(1)}, f32[1,64,768]{2,1,0:T(8,128)S(1)}, u32[]{:S(2)}, u32[]{:S(2)}) %collective-permute-start.11) | collective-permute-done | bytes 196640 | tf_op jit(solution)/shard_map/ppermute | solution.py:289
  41.5 0.9 %finish.1 = bf16[1,768,128]{2,1,0:T(8,128)(2,1)} custom-call(f32[1,128,768]{2,1,0:T(8,128)S(1)} %get-tuple-element.43.refs_0_, f32[1,64,768]{2,1,0:T(8,128)S(1)} %collective-permute-done.6.refs_1_, f32[1,64,768]{2,1,0:T(8,128)S(1)} %collective-permute-done.7.refs_2_, f32[1,128,768]{2,1,0:T(8,128)S(1)} %collective-permute-done.8.refs_3_, ...), custom_call_target="tpu_custom_call" | custom-call | flops 24999999488 | bytes 1000 | tf_op jit(solution)/shard_map/finish/pallas_call | solution.py:207
  (11 shorter events, 0.2 us)
Async XLA Ops:
  0.0 2.2 %copy-start = (bf16[2,1,128,6144]{3,2,1,0:T(8,128)(2,1)S(1)}, bf16[2,1,128,6144]{3,2,1,0:T(8,128)(2,1)}, u32[]{:S(2)}) copy-start(bf16[2,1,128,6144]{3,2,1,0:T(8,128)(2,1)} %refs_0_.25) | copy-start | bytes 9437188
  1.7 1.9 %collective-permute-start.1 = (f32[1,128,768]{2,1,0:T(8,128)S(1)}, f32[1,128,768]{2,1,0:T(8,128)S(1)}, u32[]{:S(2)}, u32[]{:S(2)}) collective-permute-start(f32[1,128,768]{2,1,0:T(8,128)S(1)} %get-tuple-element.38), channel_id=1, source_target_pairs={{0,1},{1,0},{2,3},{3,2},{4,5},{5,4},{6,7},{7,6},{8,9},{9,8},{10,11... | collective-permute-start | bytes 1179656 | tf_op jit(solution)/shard_map/ppermute | solution.py:289
  2.8 6.6 %collective-permute-start = (f32[7,128,768]{2,1,0:T(8,128)S(1)}, f32[7,128,768]{2,1,0:T(8,128)S(1)}, u32[]{:S(2)}, u32[]{:S(2)}) collective-permute-start(f32[7,128,768]{2,1,0:T(8,128)S(1)} %get-tuple-element.37), channel_id=1, source_target_pairs={{0,1},{1,0},{2,3},{3,2},{4,5},{5,4},{6,7},{7,6},{8,9},{9,8},{10,11... | collective-permute-start | bytes 8257544 | tf_op jit(solution)/shard_map/ppermute | solution.py:289
  3.9 13.8 %collective-permute-start.5 = (f32[1,64,768]{2,1,0:T(8,128)S(1)}, f32[1,64,768]{2,1,0:T(8,128)S(1)}, u32[]{:S(2)}, u32[]{:S(2)}) collective-permute-start(f32[1,64,768]{2,1,0:T(8,128)S(1)} %get-tuple-element.50), channel_id=1, source_target_pairs={{0,2},{1,3},{2,0},{3,1},{4,6},{5,7},{6,4},{7,5},{8,10},{9,11},{10,... | collective-permute-start | bytes 589832 | tf_op jit(solution)/shard_map/ppermute | solution.py:289
  6.9 8.7 %collective-permute-start.3 = (f32[1,64,768]{2,1,0:T(8,128)S(1)}, f32[1,64,768]{2,1,0:T(8,128)S(1)}, u32[]{:S(2)}, u32[]{:S(2)}) collective-permute-start(f32[1,64,768]{2,1,0:T(8,128)S(1)} %get-tuple-element.47), channel_id=1, source_target_pairs={{0,24},{8,16},{16,8},{24,0},{1,25},{9,17},{17,9},{25,1},{2,26},{10... | collective-permute-start | bytes 589832 | tf_op jit(solution)/shard_map/ppermute | solution.py:292
  9.6 15.0 %collective-permute-start.2 = (f32[2,64,768]{2,1,0:T(8,128)S(1)}, f32[2,64,768]{2,1,0:T(8,128)S(1)}, u32[]{:S(2)}, u32[]{:S(2)}) collective-permute-start(f32[2,64,768]{2,1,0:T(8,128)S(1)} %get-tuple-element.45), channel_id=1, source_target_pairs={{0,24},{8,16},{16,8},{24,0},{1,25},{9,17},{17,9},{25,1},{2,26},{10... | collective-permute-start | bytes 1179656 | tf_op jit(solution)/shard_map/ppermute | solution.py:292
  15.7 14.9 %collective-permute-start.9 = (f32[1,64,768]{2,1,0:T(8,128)S(1)}, f32[1,64,768]{2,1,0:T(8,128)S(1)}, u32[]{:S(2)}, u32[]{:S(2)}) collective-permute-start(f32[1,64,768]{2,1,0:T(8,128)S(1)} %get-tuple-element.60), channel_id=1, source_target_pairs={{0,2},{1,3},{2,0},{3,1},{4,6},{5,7},{6,4},{7,5},{8,10},{9,11},{10,... | collective-permute-start | bytes 589832 | tf_op jit(solution)/shard_map/ppermute | solution.py:289
  15.8 8.9 %collective-permute-start.4 = (f32[1,64,768]{2,1,0:T(8,128)S(1)}, f32[1,64,768]{2,1,0:T(8,128)S(1)}, u32[]{:S(2)}, u32[]{:S(2)}) collective-permute-start(f32[1,64,768]{2,1,0:T(8,128)S(1)} %get-tuple-element.49), channel_id=1, source_target_pairs={{0,2},{1,3},{2,0},{3,1},{4,6},{5,7},{6,4},{7,5},{8,10},{9,11},{10,... | collective-permute-start | bytes 589832 | tf_op jit(solution)/shard_map/ppermute | solution.py:289
  18.0 14.5 %collective-permute-start.10 = (f32[2,64,768]{2,1,0:T(8,128)S(1)}, f32[2,64,768]{2,1,0:T(8,128)S(1)}, u32[]{:S(2)}, u32[]{:S(2)}) collective-permute-start(f32[2,64,768]{2,1,0:T(8,128)S(1)} %get-tuple-element.61), channel_id=1, source_target_pairs={{0,24},{8,16},{16,8},{24,0},{1,25},{9,17},{17,9},{25,1},{2,26},{10... | collective-permute-start | bytes 1179656 | tf_op jit(solution)/shard_map/ppermute | solution.py:292
  24.7 10.6 %collective-permute-start.7 = (f32[1,64,768]{2,1,0:T(8,128)S(1)}, f32[1,64,768]{2,1,0:T(8,128)S(1)}, u32[]{:S(2)}, u32[]{:S(2)}) collective-permute-start(f32[1,64,768]{2,1,0:T(8,128)S(1)} %get-tuple-element.57), channel_id=1, source_target_pairs={{0,2},{1,3},{2,0},{3,1},{4,6},{5,7},{6,4},{7,5},{8,10},{9,11},{10,... | collective-permute-start | bytes 589832 | tf_op jit(solution)/shard_map/ppermute | solution.py:289
  25.5 9.8 %collective-permute-start.6 = (f32[1,64,768]{2,1,0:T(8,128)S(1)}, f32[1,64,768]{2,1,0:T(8,128)S(1)}, u32[]{:S(2)}, u32[]{:S(2)}) collective-permute-start(f32[1,64,768]{2,1,0:T(8,128)S(1)} %get-tuple-element.54), channel_id=1, source_target_pairs={{0,4},{1,5},{2,6},{3,7},{4,0},{5,1},{6,2},{7,3},{8,12},{9,13},{10,... | collective-permute-start | bytes 589832 | tf_op jit(solution)/shard_map/ppermute | solution.py:289
  28.0 13.5 %collective-permute-start.8 = (f32[1,128,768]{2,1,0:T(8,128)S(1)}, f32[1,128,768]{2,1,0:T(8,128)S(1)}, u32[]{:S(2)}, u32[]{:S(2)}) collective-permute-start(f32[1,128,768]{2,1,0:T(8,128)S(1)} %get-tuple-element.59), channel_id=1, source_target_pairs={{0,24},{8,16},{16,8},{24,0},{1,25},{9,17},{17,9},{25,1},{2,26},{10... | collective-permute-start | bytes 1179656 | tf_op jit(solution)/shard_map/ppermute | solution.py:292
  32.5 7.9 %collective-permute-start.12 = (f32[1,64,768]{2,1,0:T(8,128)S(1)}, f32[1,64,768]{2,1,0:T(8,128)S(1)}, u32[]{:S(2)}, u32[]{:S(2)}) collective-permute-start(f32[1,64,768]{2,1,0:T(8,128)S(1)} %get-tuple-element.65), channel_id=1, source_target_pairs={{0,2},{1,3},{2,0},{3,1},{4,6},{5,7},{6,4},{7,5},{8,10},{9,11},{10,... | collective-permute-start | bytes 589832 | tf_op jit(solution)/shard_map/ppermute | solution.py:289
  32.6 8.9 %collective-permute-start.11 = (f32[1,64,768]{2,1,0:T(8,128)S(1)}, f32[1,64,768]{2,1,0:T(8,128)S(1)}, u32[]{:S(2)}, u32[]{:S(2)}) collective-permute-start(f32[1,64,768]{2,1,0:T(8,128)S(1)} %get-tuple-element.63), channel_id=1, source_target_pairs={{0,4},{1,5},{2,6},{3,7},{4,0},{5,1},{6,2},{7,3},{8,12},{9,13},{10,... | collective-permute-start | bytes 589832 | tf_op jit(solution)/shard_map/ppermute | solution.py:289

commit v9 on v8

--- a/solution.py
+++ b/solution.py
@@ -272,7 +272,7 @@
     for block in reversed(range(2, last - 1)):
         events += [("up", (block, 0, head)), ("down", (block + 1, 0, head))]
     parts = [(0, half), (half, head)] if last - 1 == 2 else [(0, head)]
-    events += [("down", (2, *parts[0])), ("down", (1, 0, half)), ("up", (0, 0, head))]
+    events += [("down", (1, 0, half)), ("down", (2, *parts[0])), ("up", (0, 0, head))]
     events += [("down", (2, *part)) for part in parts[1:]]
     return events + [("down", (1, half, head))]
 

time: 42.5 us -> 42.5 us (level)
    ppermute x4, waiting for transfers between devices: 5.27 us -> 9.31 us  [mirror(): lax.ppermute(block, 'pipe', [(i, slots - 1 - i) for i in range(slots)])]
    ppermute x9, waiting for transfers between devices: 10.8 us -> 7.15 us  [swap(): return lax.ppermute(block, 'dp', [(i, i ^ distance) for i in range(ways)])]
  transfers between devices with their start and end apart: 13 -> 13, of which waited for: 6 -> 7; matrix products, arithmetic and copies ran while one was open for 0% -> 0% of each run, Pallas kernels for 5% -> 5%
where the time goes in v9:
time: 42.5 us; the launch traced here: 42.4 us
  starting transfers between devices  21.2 us (50%)
  waiting for transfers between devices  16.5 us (39%)
  Pallas kernels  4.54 us (11%)
    ppermute x9, starting transfers between devices, swap(): return lax.ppermute(block, 'dp', [(i, i ^ distance) for i in range(ways)])  11.4 us
    ppermute x4, starting transfers between devices, mirror(): lax.ppermute(block, 'pipe', [(i, slots - 1 - i) for i in range(slots)])  9.81 us
    ppermute x4, waiting for transfers between devices, mirror(): lax.ppermute(block, 'pipe', [(i, slots - 1 - i) for i in range(slots)])  9.31 us
    ppermute x9, waiting for transfers between devices, swap(): return lax.ppermute(block, 'dp', [(i, i ^ distance) for i in range(ways)])  7.15 us
    pallas_call x13, Pallas kernels, blocks(): pl.pallas_call(functools.partial(blocks_kernel, static, len(operands), wi...  1.99 us
    pallas_call x1, Pallas kernels, front(): pl.pallas_call(functools.partial(front_kernel, flip, width), out_shape=(j...  1.7 us
    pallas_call x1, Pallas kernels, finish(): pl.pallas_call(functools.partial(finish_kernel, static, len(operands)), o...  0.85 us
  transfers between devices with their start and end apart: 13, of which 7 were waited for; matrix products, arithmetic and copies ran while one was open for 0% of the time, Pallas kernels for 5%

profile of v9, /device:TPU:0, one launch (start us, length us, event | category | flops | bytes accessed | tf_op | source)
XLA Modules:
  0.0 42.4 jit_solution(15005812695123294847)
XLA Ops:
  0.0 1.7 %front.1 = (bf16[2,128,128]{2,1,0:T(8,128)(2,1)S(1)}, f32[1,128,768]{2,1,0:T(8,128)S(1)}) custom-call(bf16[2,1,128,6144]{3,2,1,0:T(8,128)(2,1)} %refs_0_.25, bf16[2,1,128,128]{3,2,1,0:T(8,128)(2,1)} %queries.1, bf16[2,1,128,128]{3,2,1,0:T(8,128)(2,1)} %keys.1, bf16[2,1,128,128]{3,2,1,0:T(8,128)(2,1)} %grad_out.1, s32[2,1,1,128]{3,2,1,0:T(1,128)} %segs.1), custom_call_target="tpu_custom_call" | custom-call | flops 24999999488 | bytes 1000 | tf_op jit(solution)/shard_map/front/pallas_call | solution.py:77
  1.7 0.5 %collective-permute-start.1 = (f32[1,128,768]{2,1,0:T(8,128)S(1)}, f32[1,128,768]{2,1,0:T(8,128)S(1)}, u32[]{:S(2)}, u32[]{:S(2)}) collective-permute-start(f32[1,128,768]{2,1,0:T(8,128)S(1)} %get-tuple-element.38), channel_id=1, source_target_pairs={{0,1},{1,0},{2,3},{3,2},{4,5},{5,4},{6,7},{7,6},{8,9},{9,8},{10,11... | collective-permute-start | bytes 1179656 | tf_op jit(solution)/shard_map/ppermute | solution.py:289
  2.2 0.5 %theirs.1 = (f32[7,128,768]{2,1,0:T(8,128)S(1)}, f32[8,128]{1,0:T(8,128)S(1)}) custom-call(bf16[2,1,128,6144]{3,2,1,0:T(8,128)(2,1)S(1)} %copy-done, bf16[2,128,128]{2,1,0:T(8,128)(2,1)S(1)} %get-tuple-element.36.refs_1_), custom_call_target="tpu_custom_call" | custom-call | flops 24999999488 | bytes 1000 | tf_op jit(solution)/shard_map/theirs/pallas_call | solution.py:172
  2.8 0.4 collective-permute-start
  3.1 0.4 %collective-permute-done.1.refs_2_ = f32[1,128,768]{2,1,0:T(8,128)S(1)} collective-permute-done((f32[1,128,768]{2,1,0:T(8,128)S(1)}, f32[1,128,768]{2,1,0:T(8,128)S(1)}, u32[]{:S(2)}, u32[]{:S(2)}) %collective-permute-start.1) | collective-permute-done | bytes 393248 | tf_op jit(solution)/shard_map/ppermute | solution.py:289
  3.6 0.2 upper.4
  3.7 0.2 raw.2
  3.9 3.0 %collective-permute-start.3 = (f32[1,64,768]{2,1,0:T(8,128)S(1)}, f32[1,64,768]{2,1,0:T(8,128)S(1)}, u32[]{:S(2)}, u32[]{:S(2)}) collective-permute-start(f32[1,64,768]{2,1,0:T(8,128)S(1)} %get-tuple-element.46), channel_id=1, source_target_pairs={{0,2},{1,3},{2,0},{3,1},{4,6},{5,7},{6,4},{7,5},{8,10},{9,11},{10,... | collective-permute-start | bytes 589832 | tf_op jit(solution)/shard_map/ppermute | solution.py:289
  6.9 2.4 %collective-permute-start.4 = (f32[1,64,768]{2,1,0:T(8,128)S(1)}, f32[1,64,768]{2,1,0:T(8,128)S(1)}, u32[]{:S(2)}, u32[]{:S(2)}) collective-permute-start(f32[1,64,768]{2,1,0:T(8,128)S(1)} %get-tuple-element.48), channel_id=1, source_target_pairs={{0,24},{8,16},{16,8},{24,0},{1,25},{9,17},{17,9},{25,1},{2,26},{10... | collective-permute-start | bytes 589832 | tf_op jit(solution)/shard_map/ppermute | solution.py:292
  9.4 0.0 collective-permute-done.refs_2_
  9.4 0.2 upper.5
  9.6 2.3 %collective-permute-start.2 = (f32[2,64,768]{2,1,0:T(8,128)S(1)}, f32[2,64,768]{2,1,0:T(8,128)S(1)}, u32[]{:S(2)}, u32[]{:S(2)}) collective-permute-start(f32[2,64,768]{2,1,0:T(8,128)S(1)} %get-tuple-element.45), channel_id=1, source_target_pairs={{0,24},{8,16},{16,8},{24,0},{1,25},{9,17},{17,9},{25,1},{2,26},{10... | collective-permute-start | bytes 1179656 | tf_op jit(solution)/shard_map/ppermute | solution.py:292
  11.9 0.4 base.1
  12.3 3.3 %collective-permute-done.4.refs_3_ = f32[1,64,768]{2,1,0:T(8,128)S(1)} collective-permute-done((f32[1,64,768]{2,1,0:T(8,128)S(1)}, f32[1,64,768]{2,1,0:T(8,128)S(1)}, u32[]{:S(2)}, u32[]{:S(2)}) %collective-permute-start.4) | collective-permute-done | bytes 196640 | tf_op jit(solution)/shard_map/ppermute | solution.py:292
  15.7 0.1 collective-permute-start.9
  15.8 2.0 %collective-permute-start.6 = (f32[1,64,768]{2,1,0:T(8,128)S(1)}, f32[1,64,768]{2,1,0:T(8,128)S(1)}, u32[]{:S(2)}, u32[]{:S(2)}) collective-permute-start(f32[1,64,768]{2,1,0:T(8,128)S(1)} %get-tuple-element.55), channel_id=1, source_target_pairs={{0,2},{1,3},{2,0},{3,1},{4,6},{5,7},{6,4},{7,5},{8,10},{9,11},{10,... | collective-permute-start | bytes 589832 | tf_op jit(solution)/shard_map/ppermute | solution.py:289
  17.8 0.2 upper.6
  18.0 2.5 %collective-permute-start.10 = (f32[2,64,768]{2,1,0:T(8,128)S(1)}, f32[2,64,768]{2,1,0:T(8,128)S(1)}, u32[]{:S(2)}, u32[]{:S(2)}) collective-permute-start(f32[2,64,768]{2,1,0:T(8,128)S(1)} %get-tuple-element.61), channel_id=1, source_target_pairs={{0,24},{8,16},{16,8},{24,0},{1,25},{9,17},{17,9},{25,1},{2,26},{10... | collective-permute-start | bytes 1179656 | tf_op jit(solution)/shard_map/ppermute | solution.py:292
  20.5 3.6 %collective-permute-done.2.refs_3_ = f32[2,64,768]{2,1,0:T(8,128)S(1)} collective-permute-done((f32[2,64,768]{2,1,0:T(8,128)S(1)}, f32[2,64,768]{2,1,0:T(8,128)S(1)}, u32[]{:S(2)}, u32[]{:S(2)}) %collective-permute-start.2) | collective-permute-done | bytes 393248 | tf_op jit(solution)/shard_map/ppermute | solution.py:292
  24.1 0.1 collective-permute-start.5
  24.2 0.5 %collective-permute-done.6.refs_4_ = f32[1,64,768]{2,1,0:T(8,128)S(1)} collective-permute-done((f32[1,64,768]{2,1,0:T(8,128)S(1)}, f32[1,64,768]{2,1,0:T(8,128)S(1)}, u32[]{:S(2)}, u32[]{:S(2)}) %collective-permute-start.6) | collective-permute-done | bytes 196640 | tf_op jit(solution)/shard_map/ppermute | solution.py:289
  24.7 2.6 %collective-permute-start.7 = (f32[1,64,768]{2,1,0:T(8,128)S(1)}, f32[1,64,768]{2,1,0:T(8,128)S(1)}, u32[]{:S(2)}, u32[]{:S(2)}) collective-permute-start(f32[1,64,768]{2,1,0:T(8,128)S(1)} %get-tuple-element.57), channel_id=1, source_target_pairs={{0,4},{1,5},{2,6},{3,7},{4,0},{5,1},{6,2},{7,3},{8,12},{9,13},{10,... | collective-permute-start | bytes 589832 | tf_op jit(solution)/shard_map/ppermute | solution.py:289
  27.3 0.2 upper.7
  27.5 2.5 %collective-permute-start.8 = (f32[1,128,768]{2,1,0:T(8,128)S(1)}, f32[1,128,768]{2,1,0:T(8,128)S(1)}, u32[]{:S(2)}, u32[]{:S(2)}) collective-permute-start(f32[1,128,768]{2,1,0:T(8,128)S(1)} %get-tuple-element.59), channel_id=1, source_target_pairs={{0,24},{8,16},{16,8},{24,0},{1,25},{9,17},{17,9},{25,1},{2,26},{10... | collective-permute-start | bytes 1179656 | tf_op jit(solution)/shard_map/ppermute | solution.py:292
  30.0 0.0 collective-permute-done.9.refs_3_
  30.0 2.4 %collective-permute-done.10.refs_4_.refs_3_ = f32[2,64,768]{2,1,0:T(8,128)S(1)} collective-permute-done((f32[2,64,768]{2,1,0:T(8,128)S(1)}, f32[2,64,768]{2,1,0:T(8,128)S(1)}, u32[]{:S(2)}, u32[]{:S(2)}) %collective-permute-start.10) | collective-permute-done | bytes 393248 | tf_op jit(solution)/shard_map/ppermute | solution.py:292
  32.5 0.1 collective-permute-start.12
  32.6 2.6 %collective-permute-start.11 = (f32[1,64,768]{2,1,0:T(8,128)S(1)}, f32[1,64,768]{2,1,0:T(8,128)S(1)}, u32[]{:S(2)}, u32[]{:S(2)}) collective-permute-start(f32[1,64,768]{2,1,0:T(8,128)S(1)} %get-tuple-element.63), channel_id=1, source_target_pairs={{0,4},{1,5},{2,6},{3,7},{4,0},{5,1},{6,2},{7,3},{8,12},{9,13},{10,... | collective-permute-start | bytes 589832 | tf_op jit(solution)/shard_map/ppermute | solution.py:289
  35.3 0.0 collective-permute-done.5.refs_1_
  35.3 5.2 %collective-permute-done.12.refs_5_ = f32[1,64,768]{2,1,0:T(8,128)S(1)} collective-permute-done((f32[1,64,768]{2,1,0:T(8,128)S(1)}, f32[1,64,768]{2,1,0:T(8,128)S(1)}, u32[]{:S(2)}, u32[]{:S(2)}) %collective-permute-start.12) | collective-permute-done | bytes 196640 | tf_op jit(solution)/shard_map/ppermute | solution.py:289
  40.5 1.0 %collective-permute-done.11.refs_4_ = f32[1,64,768]{2,1,0:T(8,128)S(1)} collective-permute-done((f32[1,64,768]{2,1,0:T(8,128)S(1)}, f32[1,64,768]{2,1,0:T(8,128)S(1)}, u32[]{:S(2)}, u32[]{:S(2)}) %collective-permute-start.11) | collective-permute-done | bytes 196640 | tf_op jit(solution)/shard_map/ppermute | solution.py:289
  41.5 0.9 %finish.1 = bf16[1,768,128]{2,1,0:T(8,128)(2,1)} custom-call(f32[1,128,768]{2,1,0:T(8,128)S(1)} %get-tuple-element.43.refs_0_, f32[1,64,768]{2,1,0:T(8,128)S(1)} %collective-permute-done.5.refs_1_, f32[1,64,768]{2,1,0:T(8,128)S(1)} %collective-permute-done.7.refs_2_, f32[1,128,768]{2,1,0:T(8,128)S(1)} %collective-permute-done.8.refs_3_, ...), custom_call_target="tpu_custom_call" | custom-call | flops 24999999488 | bytes 1000 | tf_op jit(solution)/shard_map/finish/pallas_call | solution.py:207
  (11 shorter events, 0.2 us)
Async XLA Ops:
  0.0 2.2 %copy-start = (bf16[2,1,128,6144]{3,2,1,0:T(8,128)(2,1)S(1)}, bf16[2,1,128,6144]{3,2,1,0:T(8,128)(2,1)}, u32[]{:S(2)}) copy-start(bf16[2,1,128,6144]{3,2,1,0:T(8,128)(2,1)} %refs_0_.25) | copy-start | bytes 9437188
  1.7 1.9 %collective-permute-start.1 = (f32[1,128,768]{2,1,0:T(8,128)S(1)}, f32[1,128,768]{2,1,0:T(8,128)S(1)}, u32[]{:S(2)}, u32[]{:S(2)}) collective-permute-start(f32[1,128,768]{2,1,0:T(8,128)S(1)} %get-tuple-element.38), channel_id=1, source_target_pairs={{0,1},{1,0},{2,3},{3,2},{4,5},{5,4},{6,7},{7,6},{8,9},{9,8},{10,11... | collective-permute-start | bytes 1179656 | tf_op jit(solution)/shard_map/ppermute | solution.py:289
  2.8 6.6 %collective-permute-start = (f32[7,128,768]{2,1,0:T(8,128)S(1)}, f32[7,128,768]{2,1,0:T(8,128)S(1)}, u32[]{:S(2)}, u32[]{:S(2)}) collective-permute-start(f32[7,128,768]{2,1,0:T(8,128)S(1)} %get-tuple-element.37), channel_id=1, source_target_pairs={{0,1},{1,0},{2,3},{3,2},{4,5},{5,4},{6,7},{7,6},{8,9},{9,8},{10,11... | collective-permute-start | bytes 8257544 | tf_op jit(solution)/shard_map/ppermute | solution.py:289
  3.9 13.8 %collective-permute-start.3 = (f32[1,64,768]{2,1,0:T(8,128)S(1)}, f32[1,64,768]{2,1,0:T(8,128)S(1)}, u32[]{:S(2)}, u32[]{:S(2)}) collective-permute-start(f32[1,64,768]{2,1,0:T(8,128)S(1)} %get-tuple-element.46), channel_id=1, source_target_pairs={{0,2},{1,3},{2,0},{3,1},{4,6},{5,7},{6,4},{7,5},{8,10},{9,11},{10,... | collective-permute-start | bytes 589832 | tf_op jit(solution)/shard_map/ppermute | solution.py:289
  6.9 8.7 %collective-permute-start.4 = (f32[1,64,768]{2,1,0:T(8,128)S(1)}, f32[1,64,768]{2,1,0:T(8,128)S(1)}, u32[]{:S(2)}, u32[]{:S(2)}) collective-permute-start(f32[1,64,768]{2,1,0:T(8,128)S(1)} %get-tuple-element.48), channel_id=1, source_target_pairs={{0,24},{8,16},{16,8},{24,0},{1,25},{9,17},{17,9},{25,1},{2,26},{10... | collective-permute-start | bytes 589832 | tf_op jit(solution)/shard_map/ppermute | solution.py:292
  9.6 14.5 %collective-permute-start.2 = (f32[2,64,768]{2,1,0:T(8,128)S(1)}, f32[2,64,768]{2,1,0:T(8,128)S(1)}, u32[]{:S(2)}, u32[]{:S(2)}) collective-permute-start(f32[2,64,768]{2,1,0:T(8,128)S(1)} %get-tuple-element.45), channel_id=1, source_target_pairs={{0,24},{8,16},{16,8},{24,0},{1,25},{9,17},{17,9},{25,1},{2,26},{10... | collective-permute-start | bytes 1179656 | tf_op jit(solution)/shard_map/ppermute | solution.py:292
  15.7 14.4 %collective-permute-start.9 = (f32[1,64,768]{2,1,0:T(8,128)S(1)}, f32[1,64,768]{2,1,0:T(8,128)S(1)}, u32[]{:S(2)}, u32[]{:S(2)}) collective-permute-start(f32[1,64,768]{2,1,0:T(8,128)S(1)} %get-tuple-element.60), channel_id=1, source_target_pairs={{0,2},{1,3},{2,0},{3,1},{4,6},{5,7},{6,4},{7,5},{8,10},{9,11},{10,... | collective-permute-start | bytes 589832 | tf_op jit(solution)/shard_map/ppermute | solution.py:289
  15.8 8.9 %collective-permute-start.6 = (f32[1,64,768]{2,1,0:T(8,128)S(1)}, f32[1,64,768]{2,1,0:T(8,128)S(1)}, u32[]{:S(2)}, u32[]{:S(2)}) collective-permute-start(f32[1,64,768]{2,1,0:T(8,128)S(1)} %get-tuple-element.55), channel_id=1, source_target_pairs={{0,2},{1,3},{2,0},{3,1},{4,6},{5,7},{6,4},{7,5},{8,10},{9,11},{10,... | collective-permute-start | bytes 589832 | tf_op jit(solution)/shard_map/ppermute | solution.py:289
  18.0 14.5 %collective-permute-start.10 = (f32[2,64,768]{2,1,0:T(8,128)S(1)}, f32[2,64,768]{2,1,0:T(8,128)S(1)}, u32[]{:S(2)}, u32[]{:S(2)}) collective-permute-start(f32[2,64,768]{2,1,0:T(8,128)S(1)} %get-tuple-element.61), channel_id=1, source_target_pairs={{0,24},{8,16},{16,8},{24,0},{1,25},{9,17},{17,9},{25,1},{2,26},{10... | collective-permute-start | bytes 1179656 | tf_op jit(solution)/shard_map/ppermute | solution.py:292
  24.1 11.2 %collective-permute-start.5 = (f32[1,64,768]{2,1,0:T(8,128)S(1)}, f32[1,64,768]{2,1,0:T(8,128)S(1)}, u32[]{:S(2)}, u32[]{:S(2)}) collective-permute-start(f32[1,64,768]{2,1,0:T(8,128)S(1)} %get-tuple-element.53), channel_id=1, source_target_pairs={{0,2},{1,3},{2,0},{3,1},{4,6},{5,7},{6,4},{7,5},{8,10},{9,11},{10,... | collective-permute-start | bytes 589832 | tf_op jit(solution)/shard_map/ppermute | solution.py:289
  24.7 10.6 %collective-permute-start.7 = (f32[1,64,768]{2,1,0:T(8,128)S(1)}, f32[1,64,768]{2,1,0:T(8,128)S(1)}, u32[]{:S(2)}, u32[]{:S(2)}) collective-permute-start(f32[1,64,768]{2,1,0:T(8,128)S(1)} %get-tuple-element.57), channel_id=1, source_target_pairs={{0,4},{1,5},{2,6},{3,7},{4,0},{5,1},{6,2},{7,3},{8,12},{9,13},{10,... | collective-permute-start | bytes 589832 | tf_op jit(solution)/shard_map/ppermute | solution.py:289
  27.5 14.0 %collective-permute-start.8 = (f32[1,128,768]{2,1,0:T(8,128)S(1)}, f32[1,128,768]{2,1,0:T(8,128)S(1)}, u32[]{:S(2)}, u32[]{:S(2)}) collective-permute-start(f32[1,128,768]{2,1,0:T(8,128)S(1)} %get-tuple-element.59), channel_id=1, source_target_pairs={{0,24},{8,16},{16,8},{24,0},{1,25},{9,17},{17,9},{25,1},{2,26},{10... | collective-permute-start | bytes 1179656 | tf_op jit(solution)/shard_map/ppermute | solution.py:292
  32.5 7.9 %collective-permute-start.12 = (f32[1,64,768]{2,1,0:T(8,128)S(1)}, f32[1,64,768]{2,1,0:T(8,128)S(1)}, u32[]{:S(2)}, u32[]{:S(2)}) collective-permute-start(f32[1,64,768]{2,1,0:T(8,128)S(1)} %get-tuple-element.65), channel_id=1, source_target_pairs={{0,2},{1,3},{2,0},{3,1},{4,6},{5,7},{6,4},{7,5},{8,10},{9,11},{10,... | collective-permute-start | bytes 589832 | tf_op jit(solution)/shard_map/ppermute | solution.py:289
  32.6 8.9 %collective-permute-start.11 = (f32[1,64,768]{2,1,0:T(8,128)S(1)}, f32[1,64,768]{2,1,0:T(8,128)S(1)}, u32[]{:S(2)}, u32[]{:S(2)}) collective-permute-start(f32[1,64,768]{2,1,0:T(8,128)S(1)} %get-tuple-element.63), channel_id=1, source_target_pairs={{0,4},{1,5},{2,6},{3,7},{4,0},{5,1},{6,2},{7,3},{8,12},{9,13},{10,... | collective-permute-start | bytes 589832 | tf_op jit(solution)/shard_map/ppermute | solution.py:289
